TPU v7x, 128 devices: a whole 4x4x4 slice. The times are simulated.
128 devices in a mesh: grid: 16 (over z, x_hi, core), pair: 8 (over y, x_lo).
Axes of the slice: x: 4 (x_hi: 2, x_lo: 2; x = x_hi * 2 + x_lo), y: 4, z: 4, core: 2. Of those that a mesh axis runs over, the one named last changes fastest.
Arguments:
- amplitudes: bfloat16 [8, 1500, 1500], P('pair'), may hold values from -6 to 6
- factors: bfloat16 [1500, 6000], P(None, 'grid'), may hold values from -0.15625 to 0.15625
- z_values: bfloat16 [6000, 6000], P('grid', 'pair'), may hold values from -6 to 6
- z_scales: float32 [48, 48], P('grid', 'pair'), may hold values from 0.3 to 3
- pair_index: int32 [8], P('pair'), may hold values from 0 to 11174
- vir_energy: float32 [1500], replicated, may hold values from 0.5 to 2.5
- occ_energy: float32 [150], replicated, may hold values from -4 to -0.5
Outputs:
- update: float32 [8, 2250000], P('pair', 'grid')
All inputs are finite; a program needn't handle non-finite values.
Results may differ from a plain program's by a relative error of at most 0.004.
Values may be sent and summed in bfloat16 or wider, within the bound.
No kernel may reach another device: no remote copies, remote signals or barrier semaphores. Data moves between devices by JAX's collectives and lax.ppermute only.
A program may use at most 128 MiB of HBM per device.

v0:
```python
import jax
import jax.numpy as jnp
from jax import lax
from jax.sharding import PartitionSpec as P

ZBLK = 125


def broadcast(block, axis, source):
    block = jnp.where(lax.axis_index(axis) == source, block, jnp.zeros_like(block))
    return lax.psum(block, axis)


def pair_orbitals(packed, occ_count):
    row_ids = jnp.arange(1, occ_count, dtype=jnp.int32)
    starts = row_ids * (2 * occ_count - row_ids - 1) // 2
    first_occ = jnp.sum((starts[None, :] <= packed[:, None]).astype(jnp.int32), axis=1)
    second = packed - first_occ * (2 * occ_count - first_occ - 1) // 2 + first_occ + 1
    return (first_occ, second)


def local(amplitudes, factors, z_values, z_scales, pair_index, vir_energy, occ_energy):
    n_grid = lax.axis_size("grid")
    n_pair = lax.axis_size("pair")
    spread_ratio = n_grid // n_pair
    grid_pos = lax.axis_index("grid")
    pair_pos = lax.axis_index("pair")
    virtuals = factors.shape[0]
    column_blocks = []
    for member in range(spread_ratio):
        column_blocks.append(broadcast(factors, "grid", pair_pos * spread_ratio + member))
    q_factors = jnp.concatenate(column_blocks, axis=1)
    halves = jnp.einsum(
        "vp,kvd->kpd", factors, amplitudes, preferred_element_type=jnp.float32
    ).astype(jnp.bfloat16)
    z_full = z_values.astype(jnp.float32) * jnp.repeat(
        jnp.repeat(z_scales, ZBLK, axis=0), ZBLK, axis=1
    )
    projected = jnp.einsum(
        "kpd,dq->kpq",
        lax.all_gather(halves, "pair", axis=0, tiled=True),
        q_factors,
        preferred_element_type=jnp.float32,
    )
    weighted = (projected * z_full).astype(jnp.bfloat16)
    partials = jnp.einsum("kpq,vq->kpv", weighted, q_factors, preferred_element_type=jnp.float32)
    back_rows = lax.psum_scatter(partials, "pair", scatter_dimension=0, tiled=True)
    factors_wide = factors.astype(jnp.float32)
    local_terms = jnp.einsum(
        "vp,kpb->kvb",
        factors_wide,
        back_rows,
        precision=lax.Precision.HIGHEST,
        preferred_element_type=jnp.float32,
    )
    local_terms = local_terms.reshape(local_terms.shape[0], virtuals * virtuals)
    share = virtuals * virtuals // n_grid
    first_cell = grid_pos * share
    summed_all = lax.psum(local_terms, "grid")
    own_share = lax.dynamic_slice_in_dim(summed_all, first_cell, share, 1)
    occ_count = occ_energy.shape[0]
    first_occ, second_occ = pair_orbitals(pair_index, occ_count)
    orbital_ids = jnp.arange(occ_count, dtype=jnp.int32)
    one_first = (orbital_ids[None, :] == first_occ[:, None]).astype(jnp.float32)
    one_second = (orbital_ids[None, :] == second_occ[:, None]).astype(jnp.float32)
    occ_sum = jnp.sum((one_first + one_second) * occ_energy[None, :], axis=1)
    vir_flat = (vir_energy[:, None] + vir_energy[None, :]).reshape(virtuals * virtuals)
    vir_part = lax.dynamic_slice_in_dim(vir_flat, first_cell, share, 0)
    return own_share / (vir_part[None, :] - occ_sum[:, None])


def solution(mesh):
    placed = (
        P("pair", None, None),
        P(None, "grid"),
        P("grid", "pair"),
        P("grid", "pair"),
        P("pair"),
        P(),
        P(),
    )
    return jax.shard_map(
        local, mesh=mesh, in_specs=placed, out_specs=P("pair", "grid"), check_vma=False
    )
```

profile of v0, /device:TPU:0, one launch (start us, length us, event | category | flops | bytes accessed | tf_op | source)
XLA Modules:
  0.0 995.9 jit_solution(3208883124442230774)
XLA Ops:
  7.4 0.0 all-reduce.6.cloned.1.call-start
  7.4 0.0 copy-start
  7.4 3.0 broadcast_select_fusion.1
  10.3 0.0 all-reduce.6.cloned.1.call-update
  10.4 0.0 all-gather.2.cloned.1.call-start
  10.4 0.0 copy-done
  10.4 4.9 fusion.7
  15.3 0.0 copy-start.3
  15.4 0.0 copy-start.1
  15.4 2.1 copy.12
  17.5 0.0 all-gather.2.cloned.1.call-update
  17.5 0.2 reduce-scatter.2.cloned.1.call-start
  17.7 0.0 copy-done.3
  17.8 0.1 copy.14
  17.8 0.1 broadcast_in_dim.4
  17.9 0.1 reshape.58
  18.0 0.0 copy-done.1
  18.0 1.1 copy.13
  19.1 0.1 broadcast_in_dim.5
  19.1 0.1 reshape.59
  19.3 1.2 convert_multiply_fusion
  20.5 0.4 copy.15
  20.8 295.7 %all-reduce.6.cloned.1.call-done = (bf16[1500,375]{1,0:T(8,128)(2,1)}, bf16[1500,375]{1,0:T(8,128)(2,1)}) async-done(((bf16[1500,375]{1,0:T(8,128)(2,1)}, bf16[1500,375]{1,0:T(8,128)(2,1)}), (bf16[1500,375]{1,0:T(8,128)(2,1)}, bf16[1500,375]{1,0:T(8,128)(2,1)})) %all-reduce.6.cloned.1.call-update) | async-done | bytes 2250016 | tf_op jit(solution)/shard_map/psum | solution.py:11
  316.5 0.0 all-gather.2.cloned.1.call-done
  316.5 26.3 %fusion = f32[8,375,1500]{2,1,0:T(8,128)} fusion(f32[375,750]{1,0:T(8,128)S(1)} %copy.15, bf16[8,375,1500]{2,1,0:T(8,128)(2,1)} %all-gather.2.cloned.1.call-done, bf16[1500,375]{1,0:T(8,128)(2,1)} %get-tuple-element.5, bf16[1500,375]{1,0:T(8,128)(2,1)} %get-tuple-element.6), kind=kOutput, calls=%fused_computation.2 | convolution fusion | flops 13513500672 | bytes 30375000 | tf_op jit(solution)/shard_map/kpq,vq->kpv/dot_general | solution.py:46
  342.7 0.0 reduce-scatter.2.cloned.1.call-update
  342.8 0.3 all-reduce.4.cloned.1.call-start
  343.0 358.6 %reduce-scatter.2.cloned.1.call-done = f32[1,375,1500]{2,1,0:T(8,128)} async-done(((f32[8,375,1500]{2,1,0:T(8,128)}), f32[1,375,1500]{2,1,0:T(8,128)}) %reduce-scatter.2.cloned.1.call-update) | async-done | bytes 2250016 | tf_op jit(solution)/shard_map/reduce_scatter | solution.py:47
  701.6 15.0 %convolution_bitcast_fusion = f32[1,1500,1500]{1,2,0:T(8,128)} fusion(bf16[1500,375]{1,0:T(8,128)(2,1)S(1)} %copy-done, f32[1,375,1500]{2,1,0:T(8,128)} %reduce-scatter.2.cloned.1.call-done), kind=kOutput, calls=%fused_computation.1 | convolution fusion | flops 10125000704 | bytes 12375000 | tf_op jit(solution)/shard_map/vp,kpb->kvb/dot_general | solution.py:49
  716.7 9.5 copy.16
  726.1 12.2 %reshape.63 = f32[2250000]{0:T(1024)} reshape(f32[1,1500,1500]{2,1,0:T(8,128)} %copy.16) | data formatting | bytes 18000000
  738.4 35.0 %reshape.61 = f32[1,2250000]{1,0:T(1,128)} reshape(f32[2250000]{0:T(1024)} %reshape.63) | data formatting | bytes 18000000 | tf_op jit(solution)/shard_map/reshape | solution.py:56
  773.4 0.0 copy-start.2
  773.4 0.0 all-reduce.4.cloned.1.call-update
  774.1 0.7 fusion.13
  776.6 0.0 copy-done.2
  776.6 4.2 broadcast_add_fusion
  780.9 0.0 copy-start.4
  780.9 12.2 %add.62 = f32[2250000]{0:T(1024)} reshape(f32[1500,1500]{1,0:T(8,128)} %broadcast_add_fusion) | data formatting | bytes 18000000 | tf_op jit(solution)/shard_map/add | solution.py:67
  793.0 0.0 copy-done.4
  793.0 1.2 fusion.16
  794.2 1.8 dynamic-slice_subtract_fusion
  796.1 188.1 %all-reduce.4.cloned.1.call-done = f32[1,2250000]{1,0:T(1,128)} async-done(((f32[1,2250000]{1,0:T(1,128)}), f32[1,2250000]{1,0:T(1,128)}) %all-reduce.4.cloned.1.call-update) | async-done | bytes 9000016 | tf_op jit(solution)/shard_map/psum | solution.py:59
  984.1 4.3 reshape_divide_fusion
Async XLA Ops:
  7.4 309.1 %all-reduce.6.cloned.1.call-start = ((), (), s32[]{:S(2)}) async-start(), calls=%async_computation.4 | async-start | bytes 4620288 | tf_op jit(solution)/shard_map/psum | solution.py:11
  7.4 3.0 copy-start
  10.4 306.1 %all-gather.2.cloned.1.call-start = ((), (), s32[]{:S(2)}) async-start(), calls=%async_computation.1 | async-start | bytes 10395648 | tf_op jit(solution)/shard_map/all_gather | solution.py:41
  15.3 2.4 copy-start.3
  15.4 2.7 copy-start.1
  17.5 684.1 %reduce-scatter.2.cloned.1.call-start = ((), (), s32[]{:S(2)}) async-start(), calls=%async_computation.2 | async-start | bytes 20791296 | tf_op jit(solution)/shard_map/reduce_scatter | solution.py:47
  342.8 641.4 %all-reduce.4.cloned.1.call-start = ((), (), s32[]{:S(2)}) async-start(), calls=%async_computation.3 | async-start | bytes 18000896 | tf_op jit(solution)/shard_map/psum | solution.py:59
  773.4 3.3 copy-start.2
  780.9 12.2 %copy-start.4 = (f32[150]{0:T(256)S(1)}, f32[150]{0:T(256)}, u32[]{:S(2)}) copy-start(f32[150]{0:T(256)} %param.13) | copy-start | bytes 1804
Sparse Core Ops, SparseCore 0:
  10.8 305.6 all-reduce.5
  773.5 210.5 all-reduce.3
Sparse Core Ops, SparseCore 1:
  17.6 196.7 all-gather.1
  342.8 358.8 reduce-scatter.1
where the time goes:
time: 997 us; the launch traced here: 996 us
  waiting for transfers between devices  842 us (84%)
  local copies, waits for them, and re-layouts  72.9 us (7%)
  matrix products  46.2 us (5%)
  between operations  17.5 us (2%)
  other arithmetic  16.4 us (2%)
    reduce_scatter x1, waiting for transfers between devices, local(): lax.psum_scatter(partials, 'pair', scatter_dimension=0, tiled=True)  359 us
    psum x1, waiting for transfers between devices, broadcast(): return lax.psum(block, axis)  296 us
    psum x1, waiting for transfers between devices, local(): summed_all = lax.psum(local_terms, 'grid')  188 us
    reshape x1, local copies, waits for them, and re-layouts, local(): local_terms = local_terms.reshape(local_terms.shape[0], virtuals * virtuals)  35 us
    dot_general x1, matrix products, local(): jnp.einsum('kpq,vq->kpv', weighted, q_factors, preferred_element_type=jnp...  26.3 us
  transfers between devices with their start and end apart: 4, of which 3 were waited for; matrix products, arithmetic and copies ran while one was open for 3% of the time, Pallas kernels for 0%

commit v1 on v0

v1 whole, which is shorter than its diff:
```python
import itertools

import jax
import jax.numpy as jnp
from jax import lax
from jax.sharding import PartitionSpec as P

ZBLK = 125
BLK = 375
BPAD = 384
VPAD = 1536
WIN = 96
RING = 4
BOTH = ("grid", "pair")
ALL = list(itertools.product(range(4), range(4), range(2), range(4)))


def flat_index(z, x, c, y):
    return ((z % 4) * 4 + (x % 4) // 2 * 2 + c % 2) * 8 + (y % 4) * 2 + (x % 4) % 2


def move(block, target):
    pairs = []
    for z, x, c, y in ALL:
        dest = target(z, x, c, y)
        if dest is not None:
            pairs.append((flat_index(z, x, c, y), flat_index(*dest)))
    return lax.ppermute(block, BOTH, pairs)


def pair_orbitals(packed, occ_count):
    row_ids = jnp.arange(1, occ_count, dtype=jnp.int32)
    starts = row_ids * (2 * occ_count - row_ids - 1) // 2
    first_occ = jnp.sum((starts[None, :] <= packed[:, None]).astype(jnp.int32), axis=1)
    second = packed - first_occ * (2 * occ_count - first_occ - 1) // 2 + first_occ + 1
    return (first_occ, second)


def dot(a, b, dims):
    return lax.dot_general(a, b, (dims, ((), ())), preferred_element_type=jnp.float32)


def ring_gather(own, axis):
    def shifted(step):
        if axis == "z":
            return lambda z, x, c, y: (z + step, x, c, y)
        return lambda z, x, c, y: (z, x, c, y + step)

    before = move(own, shifted(1))
    after = move(own, shifted(-1))
    half = own.shape[0] // 2
    far_low = move(before[:half], shifted(1))
    far_high = move(after[half:], shifted(-1))
    far = jnp.concatenate([far_low, far_high], axis=0)
    return [own, after, far, before]


def local(amplitudes, factors, z_values, z_scales, pair_index, vir_energy, occ_energy):
    virtuals = factors.shape[0]
    grid_pos = lax.axis_index("grid")
    pair_pos = lax.axis_index("pair")
    z_pos = grid_pos // 4
    x_hi = (grid_pos // 2) % 2
    core = grid_pos % 2
    y_pos = pair_pos // 2
    x_pos = 2 * x_hi + pair_pos % 2
    outer = (x_pos == 0) | (x_pos == 3)

    scales = lax.all_gather(z_scales, BOTH).reshape(16, 8, 3, 6)

    z_own = jnp.pad(z_values, ((0, BPAD - BLK), (0, 2 * (BPAD - BLK))))
    hop_a = {0: 1, 3: 2, 2: 0, 1: 3}
    hop_b = {2: 1, 1: 2}
    recv_a = move(z_own, lambda z, x, c, y: (z, hop_a[x], c, y))
    recv_b = move(z_own, lambda z, x, c, y: (z, hop_b[x], c, y) if x in hop_b else None)
    z_rows = jnp.concatenate(
        [jnp.where(outer, z_own, recv_a), jnp.where(outer, recv_a, recv_b)], axis=0
    )
    z_ring = ring_gather(z_rows, "y")

    x_own = jnp.pad(factors.T, ((0, BPAD - BLK), (0, VPAD - virtuals)))
    x_ring = ring_gather(x_own, "z")
    x_other = move(x_own, lambda z, x, c, y: (z, 3 - x, c, y))
    across = lambda b: move(b, lambda z, x, c, y: (z, x, 1 - c, y))

    p_block = jnp.concatenate([x_own, x_other], axis=0)
    amp = jnp.pad(amplitudes[0], ((0, VPAD - virtuals), (0, VPAD - virtuals)))
    halves = dot(p_block, amp, ((1,), (0,))).astype(jnp.bfloat16)

    z_all = jnp.stack(z_ring)
    back = None
    row_blocks = jnp.stack([z_pos * 4 + x_hi * 2 + core, z_pos * 4 + (1 - x_hi) * 2 + core])
    for step in range(RING):
        mine = x_ring[step]
        theirs = across(mine)
        q_block = jnp.concatenate(
            [jnp.where(core == 0, mine, theirs), jnp.where(core == 0, theirs, mine)], axis=0
        )
        spot = (z_pos + step) % RING
        z_here = lax.dynamic_index_in_dim(z_all, (spot - y_pos) % RING, 0, keepdims=False)
        scale = scales[row_blocks, spot * 2 + x_hi]
        scale = jnp.repeat(jnp.repeat(scale, ZBLK, axis=1), ZBLK, axis=2)
        scale = jnp.pad(scale, ((0, 0), (0, BPAD - BLK), (0, 2 * (BPAD - BLK))))
        scale = scale.reshape(2 * BPAD, 2 * BPAD)
        q_block = jnp.concatenate(
            [q_block[:BLK], q_block[BPAD : BPAD + BLK], jnp.zeros((18, VPAD), q_block.dtype)], axis=0
        )
        projected = dot(halves, q_block, ((1,), (1,)))
        weighted = (projected * (z_here.astype(jnp.float32) * scale)).astype(jnp.bfloat16)
        part = dot(weighted, q_block, ((1,), (0,)))
        back = part if back is None else back + part

    windows = []
    for c in range(2):
        for chip in range(8):
            start = (chip * 2 + c) * BLK // 4
            windows.append(lax.slice_in_dim(p_block, start, start + WIN, axis=1))
    p_windows = jnp.concatenate(windows, axis=1)
    residual = dot(p_windows, back.astype(jnp.bfloat16), ((0,), (0,)))
    residual = residual.reshape(2, 8 * WIN, VPAD)
    keep = lax.dynamic_index_in_dim(residual, core, 0, keepdims=False)
    give = lax.dynamic_index_in_dim(residual, 1 - core, 0, keepdims=False)
    chip_sum = keep + across(give.astype(jnp.bfloat16)).astype(jnp.float32)
    chip_sum = chip_sum.reshape(4, 2, WIN, VPAD)

    def for_dest(dz, dx):
        return lax.dynamic_slice(
            chip_sum, ((z_pos + dz) % 4, (x_hi + dx) % 2, 0, 0), (1, 1, WIN, VPAD)
        )[0, 0]

    total = for_dest(0, 0)
    for dx in range(2):
        for dz in range(4):
            if dx or dz:
                piece = for_dest(dz, dx).astype(jnp.bfloat16)
                total = total + move(
                    piece, lambda z, x, c, y: (z + dz, x + 2 * dx, c, y)
                ).astype(jnp.float32)

    occ_count = occ_energy.shape[0]
    first_occ, second_occ = pair_orbitals(pair_index, occ_count)
    orbital_ids = jnp.arange(occ_count, dtype=jnp.int32)
    one_first = (orbital_ids[None, :] == first_occ[:, None]).astype(jnp.float32)
    one_second = (orbital_ids[None, :] == second_occ[:, None]).astype(jnp.float32)
    occ_sum = jnp.sum((one_first + one_second) * occ_energy[None, :], axis=1)
    share = virtuals * virtuals // 16
    first_row = grid_pos * BLK // 4
    vir_rows = lax.dynamic_slice_in_dim(jnp.pad(vir_energy, (0, VPAD - virtuals)), first_row, WIN, 0)
    out = total[:, :virtuals] / (vir_rows[:, None] + vir_energy[None, :] - occ_sum)
    first_cell = grid_pos * share - first_row * virtuals
    return lax.dynamic_slice_in_dim(out.reshape(1, WIN * virtuals), first_cell, share, 1)


def solution(mesh):
    placed = (
        P("pair", None, None),
        P(None, "grid"),
        P("grid", "pair"),
        P("grid", "pair"),
        P("pair"),
        P(),
        P(),
    )
    return jax.shard_map(
        local, mesh=mesh, in_specs=placed, out_specs=P("pair", "grid"), check_vma=False
    )
```

time: 997 us -> 575 us (0.58)
  waiting for transfers between devices: 842 us -> 51.3 us
  blocking collectives: 0 us -> 345 us
  starting transfers between devices: 0.53 us -> 29.2 us
  local copies, waits for them, and re-layouts: 72.9 us -> 91.7 us
  matrix products: 46.2 us -> 29.5 us
  between operations: 17.5 us -> 3.15 us
    psum x2 -> x0, waiting for transfers between devices: 484 us -> none  [the longest x1 296 us: broadcast(): return lax.psum(block, axis)]
    reduce_scatter x1 -> x0, waiting for transfers between devices: 359 us -> none  [local(): lax.psum_scatter(partials, 'pair', scatter_dimension=0, tiled=True)]
    all_gather x0 -> x1, blocking collectives: none -> 345 us  [local(): scales = lax.all_gather(z_scales, BOTH).reshape(16, 8, 3, 6)]
    ppermute x0 -> x23, waiting for transfers between devices: none -> 51.3 us  [move(): return lax.ppermute(block, BOTH, pairs)]
    ppermute x0 -> x23, starting transfers between devices: none -> 29.2 us  [move(): return lax.ppermute(block, BOTH, pairs)]
    dot_general x3 -> x10, matrix products: 46.2 us -> 29.5 us  [dot(): lax.dot_general(a, b, (dims, ((), ())), preferred_element_type=jnp.float32)]
    reshape x3 -> x13, local copies, waits for them, and re-layouts: 35.2 us -> 21.4 us  [the longest x12 20.5 us: local(): scale = jnp.repeat(jnp.repeat(scale, ZBLK, axis=1), ZBLK, axis=2)]
    add x1 -> x0, local copies, waits for them, and re-layouts: 12.2 us -> none  [local(): vir_energy[:, None] + vir_energy[None, :]]
  transfers between devices with their start and end apart: 4 -> 23, of which waited for: 3 -> 9; matrix products, arithmetic and copies ran while one was open for 3% -> 20% of each run, Pallas kernels for 0% -> 0%
where the time goes in v1:
time: 575 us; the launch traced here: 573 us
  blocking collectives  345 us (60%)
  local copies, waits for them, and re-layouts  91.7 us (16%)
  waiting for transfers between devices  51.3 us (9%)
  matrix products  29.5 us (5%)
  starting transfers between devices  29.2 us (5%)
  other arithmetic  23.6 us (4%)
    all_gather x1, blocking collectives, local(): scales = lax.all_gather(z_scales, BOTH).reshape(16, 8, 3, 6)  345 us
    ppermute x23, waiting for transfers between devices, move(): return lax.ppermute(block, BOTH, pairs)  51.3 us
    dot_general x10, matrix products, dot(): lax.dot_general(a, b, (dims, ((), ())), preferred_element_type=jnp.float32)  29.5 us
    ppermute x23, starting transfers between devices, move(): return lax.ppermute(block, BOTH, pairs)  29.2 us
    unnamed x34, local copies, waits for them, and re-layouts  23.6 us
    reshape x12, local copies, waits for them, and re-layouts, local(): scale = jnp.repeat(jnp.repeat(scale, ZBLK, axis=1), ZBLK, axis=2)  20.5 us
  transfers between devices with their start and end apart: 23, of which 9 were waited for; matrix products, arithmetic and copies ran while one was open for 20% of the time, Pallas kernels for 0%

profile of v1, /device:TPU:0, one launch (start us, length us, event | category | flops | bytes accessed | tf_op | source)
XLA Modules:
  0.0 573.3 jit_solution(4468802644162020628)
XLA Ops:
  0.0 1.6 copy.28
  1.7 4.2 collective-permute-start.8
  6.0 1.5 collective-permute-start.3
  7.5 3.5 collective-permute-start.2
  12.1 12.4 %collective-permute-done.2 = bf16[384,768]{1,0:T(8,128)(2,1)} collective-permute-done((bf16[384,768]{1,0:T(8,128)(2,1)S(1)}, bf16[384,768]{1,0:T(8,128)(2,1)}, u32[]{:S(2)}, u32[]{:S(2)}) %collective-permute-start.2) | collective-permute-done | bytes 589856 | tf_op jit(solution)/shard_map/ppermute | solution.py:28
  27.0 3.0 collective-permute-start.4
  31.2 1.6 collective-permute-start.5
  32.9 344.9 %all-gather.1 = f32[128,3,6]{2,1,0:T(4,128)} all-gather(f32[1,3,6]{2,1,0:T(4,128)S(1)} %bitcast.102), channel_id=2, replica_groups=mesh['grid'=16,'pair'=8] {'grid','pair'}, dimensions={0}, use_global_device_ids=true | all-gather | bytes 9288 | tf_op jit(solution)/shard_map/all_gather | solution.py:69
  377.8 1.5 gather_fusion.3
  379.4 1.5 gather_fusion.2
  381.1 1.5 gather_fusion.1
  382.6 1.5 gather_fusion
  395.9 1.4 reshape.190
  398.1 1.6 broadcast_in_dim.23
  399.7 2.8 reshape.191
  402.5 3.0 copy.44
  405.6 2.3 broadcast_in_dim.21
  407.9 2.9 reshape.188
  410.7 3.1 copy.43
  413.8 3.4 pad.39.clone
  417.2 1.6 pad.38.clone
  418.8 1.6 broadcast_in_dim.17
  420.3 2.9 reshape.182
  423.2 3.0 copy.41
  426.2 3.2 pad.36.clone
  429.4 1.6 broadcast_in_dim.19
  431.0 2.8 reshape.185
  433.8 3.1 copy.42
  436.9 3.3 pad.37.clone
  440.2 1.9 slice.165
  442.2 1.9 slice.164
  444.1 2.0 collective-permute-start.11
  446.1 3.2 fusion.53
  449.3 7.8 %fusion.2 = bf16[768,1536]{1,0:T(8,128)(2,1)} fusion(bf16[1500,1500]{1,0:T(8,128)(2,1)} %bitcast.103, bf16[384,1536]{1,0:T(8,128)(2,1)} %collective-permute-done, bf16[384,1536]{1,0:T(8,128)(2,1)S(1)} %pad.33), kind=kOutput, calls=%fused_computation.43 | convolution fusion | flops 3629776896 | bytes 9218592 | tf_op jit(solution)/shard_map/dot_general | solution.py:40
  457.1 2.9 fusion.52
  460.0 5.5 concatenate.59
  468.2 2.1 collective-permute-start.6
  470.2 1.7 broadcast_select_fusion.7
  474.8 7.9 %collective-permute-done.7 = bf16[384,768]{1,0:T(8,128)(2,1)S(1)} collective-permute-done((bf16[384,768]{1,0:T(8,128)(2,1)S(1)}, bf16[384,768]{1,0:T(8,128)(2,1)S(1)}, u32[]{:S(2)}, u32[]{:S(2)}) %collective-permute-start.7) | collective-permute-done | bytes 589856 | tf_op jit(solution)/shard_map/ppermute | solution.py:28
  482.8 2.4 collective-permute-done.6
  485.3 2.1 pad_maximum_fusion.1
  488.3 2.1 fusion.13
  491.9 2.1 fusion.16
  494.1 2.1 fusion.11
  496.2 2.1 fusion.15
  498.4 1.6 broadcast_select_fusion.1
  500.4 2.1 fusion.7
  502.7 1.5 copy-done.3
  504.2 2.1 fusion.9
  506.3 2.1 fusion.14
  508.4 2.8 add_convert_fusion
  511.3 3.9 fusion.72
  515.2 3.6 copy-done.2
  518.8 1.7 fusion.5
  520.5 4.9 collective-permute-done.15
  525.4 3.7 bitcast_add_fusion
  529.2 2.1 copy-done
  531.6 2.1 collective-permute-start.16
  539.7 5.2 collective-permute-start.21
  545.0 3.3 collective-permute-done.16
  550.0 9.7 %collective-permute-done.18 = bf16[96,1536]{1,0:T(8,128)(2,1)S(1)} collective-permute-done((bf16[96,1536]{1,0:T(8,128)(2,1)S(1)}, bf16[96,1536]{1,0:T(8,128)(2,1)S(1)}, u32[]{:S(2)}, u32[]{:S(2)}) %collective-permute-start.18) | collective-permute-done | bytes 294944 | tf_op jit(solution)/shard_map/ppermute | solution.py:28
  559.7 5.8 %collective-permute-done.20 = bf16[96,1536]{1,0:T(8,128)(2,1)S(1)} collective-permute-done((bf16[96,1536]{1,0:T(8,128)(2,1)S(1)}, bf16[96,1536]{1,0:T(8,128)(2,1)S(1)}, u32[]{:S(2)}, u32[]{:S(2)}) %collective-permute-start.20) | collective-permute-done | bytes 294944 | tf_op jit(solution)/shard_map/ppermute | solution.py:28
  565.5 3.7 collective-permute-done.19
  571.2 2.0 constant_dynamic-slice_fusion
  (92 shorter events, 33.8 us)
Async XLA Ops:
  0.0 5.9 %copy-start.8 = (bf16[375,750]{1,0:T(8,128)(2,1)S(1)}, bf16[375,750]{1,0:T(8,128)(2,1)}, u32[]{:S(2)}) copy-start(bf16[375,750]{1,0:T(8,128)(2,1)} %param.9) | copy-start | bytes 1687504
  1.7 29.4 %collective-permute-start.8 = (bf16[384,1536]{1,0:T(8,128)(2,1)S(1)}, bf16[384,1536]{1,0:T(8,128)(2,1)}, u32[]{:S(2)}, u32[]{:S(2)}) collective-permute-start(bf16[384,1536]{1,0:T(8,128)(2,1)S(1)} %pad.33), channel_id=1, source_target_pairs={{0,96},{2,98},{4,100},{6,102},{8,104},{10,106},{12,108},{14,110},{... | collective-permute-start | bytes 3538952 | tf_op jit(solution)/shard_map/ppermute | solution.py:28
  6.0 6.1 %collective-permute-start.3 = (bf16[384,768]{1,0:T(8,128)(2,1)S(1)}, bf16[384,768]{1,0:T(8,128)(2,1)}, u32[]{:S(2)}, u32[]{:S(2)}) collective-permute-start(bf16[384,768]{1,0:T(8,128)(2,1)S(1)} %pad.35), channel_id=1, source_target_pairs={{1,16},{3,18},{5,20},{7,22},{9,24},{11,26},{13,28},{15,30},{16,1},... | collective-permute-start | bytes 1769480 | tf_op jit(solution)/shard_map/ppermute | solution.py:28
  7.5 17.0 %collective-permute-start.2 = (bf16[384,768]{1,0:T(8,128)(2,1)S(1)}, bf16[384,768]{1,0:T(8,128)(2,1)}, u32[]{:S(2)}, u32[]{:S(2)}) collective-permute-start(bf16[384,768]{1,0:T(8,128)(2,1)S(1)} %pad.35), channel_id=1, source_target_pairs={{0,1},{2,3},{4,5},{6,7},{8,9},{10,11},{12,13},{14,15},{1,17},{3,19... | collective-permute-start | bytes 1769480 | tf_op jit(solution)/shard_map/ppermute | solution.py:28
  11.0 431.2 %collective-permute-start.10 = (bf16[384,1536]{1,0:T(8,128)(2,1)S(1)}, bf16[384,1536]{1,0:T(8,128)(2,1)}, u32[]{:S(2)}, u32[]{:S(2)}) collective-permute-start(bf16[384,1536]{1,0:T(8,128)(2,1)S(1)} %pad.33), channel_id=1, source_target_pairs={{0,32},{2,34},{4,36},{6,38},{8,40},{10,42},{12,44},{14,46},{1,33},... | collective-permute-start | bytes 3538952 | tf_op jit(solution)/shard_map/ppermute | solution.py:28
  11.0 433.1 %collective-permute-start = (bf16[384,1536]{1,0:T(8,128)(2,1)S(1)}, bf16[384,1536]{1,0:T(8,128)(2,1)}, u32[]{:S(2)}, u32[]{:S(2)}) collective-permute-start(bf16[384,1536]{1,0:T(8,128)(2,1)S(1)} %pad.33), channel_id=1, source_target_pairs={{0,17},{2,19},{4,21},{6,23},{8,25},{10,27},{12,29},{14,31},{1,16},... | collective-permute-start | bytes 3538952 | tf_op jit(solution)/shard_map/ppermute | solution.py:28
  12.1 456.0 %collective-permute-start.1 = (bf16[384,1536]{1,0:T(8,128)(2,1)S(1)}, bf16[384,1536]{1,0:T(8,128)(2,1)}, u32[]{:S(2)}, u32[]{:S(2)}) collective-permute-start(bf16[384,1536]{1,0:T(8,128)(2,1)S(1)} %pad.33), channel_id=1, source_target_pairs={{0,8},{2,10},{4,12},{6,14},{8,0},{10,2},{12,4},{14,6},{1,9},{3,11}... | collective-permute-start | bytes 3538952 | tf_op jit(solution)/shard_map/ppermute | solution.py:28
  25.8 7.1 %copy-start.11 = (f32[3,6]{1,0:T(4,128)S(1)}, f32[3,6]{1,0:T(4,128)}, u32[]{:S(2)}) copy-start(f32[3,6]{1,0:T(4,128)} %param.10) | copy-start | bytes 220
  27.0 438.5 %collective-permute-start.4 = (bf16[768,768]{1,0:T(8,128)(2,1)}, bf16[768,768]{1,0:T(8,128)(2,1)}, u32[]{:S(2)}, u32[]{:S(2)}) collective-permute-start(bf16[768,768]{1,0:T(8,128)(2,1)} %get-tuple-element.39), channel_id=1, source_target_pairs={{0,6},{2,0},{4,2},{6,4},{8,14},{10,8},{12,10},{14,12},{1,7},{3,1},... | collective-permute-start | bytes 3538952 | tf_op jit(solution)/shard_map/ppermute | solution.py:28
  31.2 435.8 %collective-permute-start.5 = (bf16[768,768]{1,0:T(8,128)(2,1)}, bf16[768,768]{1,0:T(8,128)(2,1)}, u32[]{:S(2)}, u32[]{:S(2)}) collective-permute-start(bf16[768,768]{1,0:T(8,128)(2,1)} %get-tuple-element.39), channel_id=1, source_target_pairs={{0,2},{2,4},{4,6},{6,0},{8,10},{10,12},{12,14},{14,8},{1,3},{3,5},... | collective-permute-start | bytes 3538952 | tf_op jit(solution)/shard_map/ppermute | solution.py:28
  413.8 3.4 copy-start.1
  417.2 1.6 copy-start.9
  442.2 31.0 %collective-permute-start.12 = (bf16[192,1536]{1,0:T(8,128)(2,1)}, bf16[192,1536]{1,0:T(8,128)(2,1)}, u32[]{:S(2)}, u32[]{:S(2)}) collective-permute-start(bf16[192,1536]{1,0:T(8,128)(2,1)} %slice.165), channel_id=1, source_target_pairs={{0,96},{2,98},{4,100},{6,102},{8,104},{10,106},{12,108},{14,110},{... | collective-permute-start | bytes 1769480 | tf_op jit(solution)/shard_map/ppermute | solution.py:28
  444.1 27.8 %collective-permute-start.11 = (bf16[192,1536]{1,0:T(8,128)(2,1)}, bf16[192,1536]{1,0:T(8,128)(2,1)}, u32[]{:S(2)}, u32[]{:S(2)}) collective-permute-start(bf16[192,1536]{1,0:T(8,128)(2,1)} %slice.164), channel_id=1, source_target_pairs={{0,32},{2,34},{4,36},{6,38},{8,40},{10,42},{12,44},{14,46},{1,33},... | collective-permute-start | bytes 1769480 | tf_op jit(solution)/shard_map/ppermute | solution.py:28
  465.6 24.9 %collective-permute-start.9 = (bf16[384,1536]{1,0:T(8,128)(2,1)}, bf16[384,1536]{1,0:T(8,128)(2,1)S(1)}, u32[]{:S(2)}, u32[]{:S(2)}) collective-permute-start(bf16[384,1536]{1,0:T(8,128)(2,1)} %collective-permute-done.8), channel_id=1, source_target_pairs={{0,8},{2,10},{4,12},{6,14},{8,0},{10,2},{12,4},{14,6},{1,9},{3,11}... | collective-permute-start | bytes 3538952 | tf_op jit(solution)/shard_map/ppermute | solution.py:28
  467.0 15.8 %collective-permute-start.7 = (bf16[384,768]{1,0:T(8,128)(2,1)S(1)}, bf16[384,768]{1,0:T(8,128)(2,1)S(1)}, u32[]{:S(2)}, u32[]{:S(2)}) collective-permute-start(bf16[384,768]{1,0:T(8,128)(2,1)S(1)} %slice.159), channel_id=1, source_target_pairs={{0,6},{2,0},{4,2},{6,4},{8,14},{10,8},{12,10},{14,12},{1,7},{3,1},... | collective-permute-start | bytes 1769480 | tf_op jit(solution)/shard_map/ppermute | solution.py:28
  468.2 17.0 %collective-permute-start.6 = (bf16[384,768]{1,0:T(8,128)(2,1)S(1)}, bf16[384,768]{1,0:T(8,128)(2,1)S(1)}, u32[]{:S(2)}, u32[]{:S(2)}) collective-permute-start(bf16[384,768]{1,0:T(8,128)(2,1)S(1)} %slice.158), channel_id=1, source_target_pairs={{0,2},{2,4},{4,6},{6,0},{8,10},{10,12},{12,14},{14,8},{1,3},{3,5},... | collective-permute-start | bytes 1769480 | tf_op jit(solution)/shard_map/ppermute | solution.py:28
  471.9 26.4 %collective-permute-start.14 = (bf16[384,1536]{1,0:T(8,128)(2,1)}, bf16[384,1536]{1,0:T(8,128)(2,1)S(1)}, u32[]{:S(2)}, u32[]{:S(2)}) collective-permute-start(bf16[384,1536]{1,0:T(8,128)(2,1)} %collective-permute-done.10), channel_id=1, source_target_pairs={{0,8},{2,10},{4,12},{6,14},{8,0},{10,2},{12,4},{14,6},{1,9},{3,11}... | collective-permute-start | bytes 3538952 | tf_op jit(solution)/shard_map/ppermute | solution.py:28
  474.2 28.3 %collective-permute-start.13 = (bf16[384,1536]{1,0:T(8,128)(2,1)S(1)}, bf16[384,1536]{1,0:T(8,128)(2,1)S(1)}, u32[]{:S(2)}, u32[]{:S(2)}) collective-permute-start(bf16[384,1536]{1,0:T(8,128)(2,1)S(1)} %constant_dynamic-update-slice_fusion), channel_id=1, source_target_pairs={{0,8},{2,10},{4,12},{6,14},{8,0},{10,2},{12,4},{14,6},{1,9},{3,11}... | collective-permute-start | bytes 3538952 | tf_op jit(solution)/shard_map/ppermute | solution.py:28
  485.2 2.4 copy-start.6
  485.3 3.1 copy-start.13
  491.9 2.2 copy-start.5
  498.3 2.0 copy-start.4
  502.5 1.7 copy-start.3
  508.4 2.9 copy-start.7
  515.2 3.6 copy-start.2
  520.5 4.9 collective-permute-start.15
  529.1 2.1 copy-start
  529.2 7.9 %copy-start.10 = (f32[1500]{0:T(1024)S(1)}, f32[1500]{0:T(1024)}, u32[]{:S(2)}) copy-start(f32[1500]{0:T(1024)} %param.12) | copy-start | bytes 18004
  529.2 7.9 %copy-start.12 = (f32[150]{0:T(256)S(1)}, f32[150]{0:T(256)}, u32[]{:S(2)}) copy-start(f32[150]{0:T(256)} %param.13) | copy-start | bytes 1804
  531.5 13.4 %collective-permute-start.17 = (bf16[96,1536]{1,0:T(8,128)(2,1)S(1)}, bf16[96,1536]{1,0:T(8,128)(2,1)S(1)}, u32[]{:S(2)}, u32[]{:S(2)}) collective-permute-start(bf16[96,1536]{1,0:T(8,128)(2,1)S(1)} %get-tuple-element.12), channel_id=1, source_target_pairs={{0,64},{2,66},{4,68},{6,70},{8,72},{10,74},{12,76},{14,78},{1,65},... | collective-permute-start | bytes 884744 | tf_op jit(solution)/shard_map/ppermute | solution.py:28
  531.6 16.6 %collective-permute-start.16 = (bf16[96,1536]{1,0:T(8,128)(2,1)S(1)}, bf16[96,1536]{1,0:T(8,128)(2,1)S(1)}, u32[]{:S(2)}, u32[]{:S(2)}) collective-permute-start(bf16[96,1536]{1,0:T(8,128)(2,1)S(1)} %get-tuple-element.13), channel_id=1, source_target_pairs={{0,32},{2,34},{4,36},{6,38},{8,40},{10,42},{12,44},{14,46},{1,33},... | collective-permute-start | bytes 884744 | tf_op jit(solution)/shard_map/ppermute | solution.py:28
  538.4 21.3 %collective-permute-start.18 = (bf16[96,1536]{1,0:T(8,128)(2,1)S(1)}, bf16[96,1536]{1,0:T(8,128)(2,1)S(1)}, u32[]{:S(2)}, u32[]{:S(2)}) collective-permute-start(bf16[96,1536]{1,0:T(8,128)(2,1)S(1)} %get-tuple-element.7), channel_id=1, source_target_pairs={{0,96},{2,98},{4,100},{6,102},{8,104},{10,106},{12,108},{14,110},{... | collective-permute-start | bytes 884744 | tf_op jit(solution)/shard_map/ppermute | solution.py:28
  539.7 20.0 %collective-permute-start.22 = (bf16[96,1536]{1,0:T(8,128)(2,1)S(1)}, bf16[96,1536]{1,0:T(8,128)(2,1)S(1)}, u32[]{:S(2)}, u32[]{:S(2)}) collective-permute-start(bf16[96,1536]{1,0:T(8,128)(2,1)S(1)} %get-tuple-element.8), channel_id=1, source_target_pairs={{0,112},{2,114},{4,116},{6,118},{8,120},{10,122},{12,124},{14,126}... | collective-permute-start | bytes 884744 | tf_op jit(solution)/shard_map/ppermute | solution.py:28
  539.7 20.0 %collective-permute-start.21 = (bf16[96,1536]{1,0:T(8,128)(2,1)S(1)}, bf16[96,1536]{1,0:T(8,128)(2,1)S(1)}, u32[]{:S(2)}, u32[]{:S(2)}) collective-permute-start(bf16[96,1536]{1,0:T(8,128)(2,1)S(1)} %get-tuple-element.9), channel_id=1, source_target_pairs={{0,80},{2,82},{4,84},{6,86},{8,88},{10,90},{12,92},{14,94},{1,81},... | collective-permute-start | bytes 884744 | tf_op jit(solution)/shard_map/ppermute | solution.py:28
  544.9 20.6 %collective-permute-start.20 = (bf16[96,1536]{1,0:T(8,128)(2,1)S(1)}, bf16[96,1536]{1,0:T(8,128)(2,1)S(1)}, u32[]{:S(2)}, u32[]{:S(2)}) collective-permute-start(bf16[96,1536]{1,0:T(8,128)(2,1)S(1)} %get-tuple-element.10), channel_id=1, source_target_pairs={{0,48},{2,50},{4,52},{6,54},{8,56},{10,58},{12,60},{14,62},{1,49},... | collective-permute-start | bytes 884744 | tf_op jit(solution)/shard_map/ppermute | solution.py:28
  548.3 20.9 %collective-permute-start.19 = (bf16[96,1536]{1,0:T(8,128)(2,1)S(1)}, bf16[96,1536]{1,0:T(8,128)(2,1)S(1)}, u32[]{:S(2)}, u32[]{:S(2)}) collective-permute-start(bf16[96,1536]{1,0:T(8,128)(2,1)S(1)} %get-tuple-element.11), channel_id=1, source_target_pairs={{0,16},{2,18},{4,20},{6,22},{8,24},{10,26},{12,28},{14,30},{1,17},... | collective-permute-start | bytes 884744 | tf_op jit(solution)/shard_map/ppermute | solution.py:28

commit v2 on v0

v2 whole, which is shorter than its diff:
```python
import itertools

import jax
import jax.numpy as jnp
from jax import lax
from jax.experimental import pallas as pl
from jax.experimental.pallas import tpu as pltpu
from jax.sharding import PartitionSpec as P

VIRT = 1500
ZBLK = 125
BLK = 375
BPAD = 384
TWO = 2 * BPAD
VPAD = 1536
WIN = 96
BOTH = ("grid", "pair")
ALL = list(itertools.product(range(4), range(4), range(2), range(4)))
F32 = jnp.float32
BF16 = jnp.bfloat16


def flat_index(z, x, c, y):
    return ((z % 4) * 4 + (x % 4) // 2 * 2 + c % 2) * 8 + (y % 4) * 2 + (x % 4) % 2


def move(block, target):
    pairs = []
    for z, x, c, y in ALL:
        dest = target(z, x, c, y)
        if dest is not None:
            pairs.append((flat_index(z, x, c, y), flat_index(*dest)))
    return lax.ppermute(block, BOTH, pairs)


def across(block):
    return move(block, lambda z, x, c, y: (z, x, 1 - c, y))


def pair_orbitals(packed, occ_count):
    row_ids = jnp.arange(1, occ_count, dtype=jnp.int32)
    starts = row_ids * (2 * occ_count - row_ids - 1) // 2
    first_occ = jnp.sum((starts[None, :] <= packed[:, None]).astype(jnp.int32), axis=1)
    second = packed - first_occ * (2 * occ_count - first_occ - 1) // 2 + first_occ + 1
    return (first_occ, second)


def dot(a, b, contract_a, contract_b):
    return lax.dot_general(
        a, b, (((contract_a,), (contract_b,)), ((), ())), preferred_element_type=F32
    )


def call(kernel, out_shape, scratch, *args, prefetch=None, aliases=None, grid=(), in_specs=None, out_specs=None):
    vmem = pl.BlockSpec(memory_space=pltpu.VMEM)
    many = isinstance(out_shape, (tuple, list))
    spec = pltpu.PrefetchScalarGridSpec(
        num_scalar_prefetch=0 if prefetch is None else 1,
        grid=grid,
        in_specs=in_specs or [vmem] * len(args),
        out_specs=out_specs or (tuple([vmem] * len(out_shape)) if many else vmem),
        scratch_shapes=scratch,
    )
    lead = () if prefetch is None else (prefetch,)
    return pl.pallas_call(
        kernel,
        out_shape=out_shape,
        grid_spec=spec,
        input_output_aliases=aliases or {},
        compiler_params=pltpu.CompilerParams(vmem_limit_bytes=56 * 2**20),
    )(*lead, *args)


def pad_metric(z_ref, s_ref, o_ref, tmp):
    tmp[...] = jnp.zeros_like(tmp)
    z = z_ref[...].astype(F32)
    tmp[:BLK, :BLK] = z[:, :BLK]
    tmp[:BLK, BPAD : BPAD + BLK] = z[:, BLK:]
    lane = lax.broadcasted_iota(jnp.int32, (1, TWO), 1)
    for r in range(3):
        row = jnp.zeros((1, TWO), F32)
        for q in range(6):
            start = (q // 3) * BPAD + (q % 3) * ZBLK
            row = jnp.where((lane >= start) & (lane < start + ZBLK), s_ref[r, q], row)
        for part in range(3):
            piece = row.astype(BF16).astype(F32)
            tmp[BLK + 3 * part + r : BLK + 3 * part + r + 1, :] = piece
            row = row - piece
    o_ref[...] = tmp[...].astype(BF16)


def scaled(block):
    z = block.astype(F32)
    tail = z[BPAD - 16 :, :]
    parts = [tail[7 + r : 8 + r] + tail[10 + r : 11 + r] + tail[13 + r : 14 + r] for r in range(3)]
    row = lax.broadcasted_iota(jnp.int32, (BPAD, 1), 0)
    scale = jnp.where(row < ZBLK, parts[0], jnp.where(row < 2 * ZBLK, parts[1], parts[2]))
    return jnp.where(row < BLK, z * scale, 0.0)


def pack_factors(info, mine_ref, theirs_ref, *refs):
    o_ref = refs[-1]
    o_ref[...] = jnp.zeros_like(o_ref)

    @pl.when(info[0] == 0)
    def _():
        o_ref[0, :VIRT, :BLK] = mine_ref[...]
        o_ref[0, :VIRT, BPAD : BPAD + BLK] = theirs_ref[...]

    @pl.when(info[0] == 1)
    def _():
        o_ref[0, :VIRT, :BLK] = theirs_ref[...]
        o_ref[0, :VIRT, BPAD : BPAD + BLK] = mine_ref[...]


def first_half(own_ref, other_ref, amp_ref, h_ref, w_ref, xf, tp):
    xf[...] = jnp.zeros_like(xf)
    xf[:VIRT, :BLK] = own_ref[...].astype(F32)
    xf[:VIRT, BPAD : BPAD + BLK] = other_ref[...].astype(F32)
    tp[...] = jnp.zeros_like(tp)
    tp[:VIRT, :VIRT] = amp_ref[0]
    for c in range(2):
        for chip in range(8):
            start = (chip * 2 + c) * BLK // 4
            w_ref[c, chip] = xf[start : start + WIN, :].astype(BF16)
    for r in range(3):
        rows = slice(256 * r, 256 * r + 256)
        left = xf[:, rows].T.astype(BF16)
        h_ref[rows, :] = dot(left, tp[...], 1, 0).astype(BF16)


def ladder(halves, x, zs, rows):
    projected = dot(halves, x, 1, 0)
    weighted = (projected * zs[rows, :]).astype(BF16)
    return dot(weighted, x, 1, 1)


def early_blocks(info, h_ref, x_ref, z0_ref, z1_ref, z2_ref, back_ref, zs):
    step = pl.program_id(0)
    for i, z_ref in enumerate((z0_ref, z1_ref, z2_ref)):

        @pl.when(step == i)
        def _():
            for b in range(2):
                zs[b * BPAD : (b + 1) * BPAD, :] = scaled(z_ref[b])

    for r in range(3):
        rows = slice(256 * r, 256 * r + 256)
        part = ladder(h_ref[rows, :], x_ref[0], zs, rows)

        @pl.when(step == 0)
        def _():
            back_ref[rows, :] = part

        @pl.when(step > 0)
        def _():
            back_ref[rows, :] += part


def last_block(info, h_ref, x_ref, z_ref, back_ref, w_ref, keep_ref, give_ref, zs, bb, left):
    for b in range(2):
        zs[b * BPAD : (b + 1) * BPAD, :] = scaled(z_ref[b])
    for r in range(3):
        rows = slice(256 * r, 256 * r + 256)
        part = ladder(h_ref[rows, :], x_ref[0], zs, rows)
        bb[rows, :] = (back_ref[rows, :] + part).astype(BF16)
    core = info[0]
    for side, o_ref in ((1 - core, give_ref), (core, keep_ref)):
        for j in range(8):
            left[WIN * j : WIN * j + WIN, :] = w_ref[side, info[8 + j]]
        for n in range(6):
            cols = slice(256 * n, 256 * n + 256)
            o_ref[:, cols] = dot(left[...], bb[:, cols], 1, 0).astype(o_ref.dtype)


def chip_total(keep_ref, got_ref, own_ref, *out_refs):
    own_ref[...] = keep_ref[:WIN, :] + got_ref[:WIN, :].astype(F32)
    for j, o_ref in enumerate(out_refs):
        rows = slice(WIN * (j + 1), WIN * (j + 2))
        o_ref[...] = (keep_ref[rows, :] + got_ref[rows, :].astype(F32)).astype(BF16)


def shape(*dims, dtype=BF16):
    return jax.ShapeDtypeStruct(dims, dtype)


def local(amplitudes, factors, z_values, z_scales, pair_index, vir_energy, occ_energy):
    grid_pos = lax.axis_index("grid")
    pair_pos = lax.axis_index("pair")
    z_pos = grid_pos // 4
    x_hi = (grid_pos // 2) % 2
    core = grid_pos % 2
    y_pos = pair_pos // 2
    x_pos = 2 * x_hi + pair_pos % 2
    outer = (x_pos == 0) | (x_pos == 3)
    order = [(y_pos + i) % 4 for i in (0, 1, 3, 2)]
    chips = [(z_pos + j % 4) % 4 * 2 + (x_hi + j // 4) % 2 for j in range(8)]
    info = jnp.stack([core, z_pos, z_pos, z_pos] + order + chips).astype(jnp.int32)

    vmem = pl.BlockSpec(memory_space=pltpu.VMEM)
    z_own = call(
        pad_metric,
        shape(BPAD, TWO),
        [pltpu.VMEM((BPAD, TWO), F32)],
        z_values,
        z_scales,
        in_specs=[vmem, pl.BlockSpec(memory_space=pltpu.SMEM)],
    )
    hop_a = {0: 1, 3: 2, 2: 0, 1: 3}
    hop_b = {2: 1, 1: 2}
    recv_a = move(z_own, lambda z, x, c, y: (z, hop_a[x], c, y))
    recv_b = move(z_own, lambda z, x, c, y: (z, hop_b[x], c, y) if x in hop_b else None)
    z_here = jnp.stack([jnp.where(outer, z_own, recv_a), jnp.where(outer, recv_a, recv_b)])
    z_before = move(z_here, lambda z, x, c, y: (z, x, c, y + 1))
    z_after = move(z_here, lambda z, x, c, y: (z, x, c, y - 1))
    onward = lambda z, x, c, y: (z, x, c, y + 1 - 2 * c)
    z_far = move(jnp.where(core == 0, z_before, z_after), onward)

    x_before = move(factors, lambda z, x, c, y: (z + 1, x, c, y))
    x_after = move(factors, lambda z, x, c, y: (z - 1, x, c, y))
    onward_z = lambda z, x, c, y: (z + 1 - 2 * c, x, c, y)
    x_far = move(jnp.where(core == 0, x_before, x_after), onward_z)
    x_other = move(factors, lambda z, x, c, y: (z, 3 - x, c, y))

    x_all = None
    for step, mine in ((0, factors), (1, x_after), (3, x_before), (2, x_far)):
        args = [mine, across(mine)] + ([] if x_all is None else [x_all])
        x_all = call(
            pack_factors,
            shape(4, VPAD, TWO),
            [],
            *args,
            prefetch=info,
            aliases={} if x_all is None else {3: 0},
            grid=(1,),
            in_specs=[vmem, vmem] + ([] if x_all is None else [pl.BlockSpec(memory_space=pl.ANY)]),
            out_specs=pl.BlockSpec(
                (1, VPAD, TWO), lambda i, info, step=step: (lax.rem(info[1] + step, 4), 0, 0)
            ),
        )

    halves, windows = call(
        first_half,
        (shape(TWO, VPAD), shape(2, 8, WIN, TWO)),
        [pltpu.VMEM((VPAD, TWO), F32), pltpu.VMEM((VPAD, VPAD), BF16)],
        factors,
        x_other,
        amplitudes,
    )
    back = call(
        early_blocks,
        shape(TWO, VPAD, dtype=F32),
        [pltpu.VMEM((TWO, TWO), F32)],
        halves,
        x_all,
        z_here,
        z_after,
        z_before,
        prefetch=info,
        grid=(3,),
        in_specs=[vmem, pl.BlockSpec((1, VPAD, TWO), lambda i, info: (info[4 + i], 0, 0)), vmem, vmem, vmem],
        out_specs=vmem,
    )
    keep, give = call(
        last_block,
        (shape(8 * WIN, VPAD, dtype=F32), shape(8 * WIN, VPAD)),
        [pltpu.VMEM((TWO, TWO), F32), pltpu.VMEM((TWO, VPAD), BF16), pltpu.VMEM((8 * WIN, TWO), BF16)],
        halves,
        x_all,
        z_far,
        back,
        windows,
        prefetch=info,
        grid=(1,),
        in_specs=[vmem, pl.BlockSpec((1, VPAD, TWO), lambda i, info: (info[7], 0, 0)), vmem, vmem, vmem],
        out_specs=(vmem, vmem),
    )
    got = across(give)
    total, *pieces = call(
        chip_total,
        tuple([shape(WIN, VPAD, dtype=F32)] + [shape(WIN, VPAD)] * 7),
        [],
        keep,
        got,
    )
    for j, piece in enumerate(pieces, start=1):
        dz, dx = j % 4, j // 4
        total = total + move(piece, lambda z, x, c, y: (z + dz, x + 2 * dx, c, y)).astype(F32)

    occ_count = occ_energy.shape[0]
    first_occ, second_occ = pair_orbitals(pair_index, occ_count)
    orbital_ids = jnp.arange(occ_count, dtype=jnp.int32)
    one_first = (orbital_ids[None, :] == first_occ[:, None]).astype(F32)
    one_second = (orbital_ids[None, :] == second_occ[:, None]).astype(F32)
    occ_sum = jnp.sum((one_first + one_second) * occ_energy[None, :], axis=1)
    share = VIRT * VIRT // 16
    first_row = grid_pos * BLK // 4
    vir_rows = lax.dynamic_slice_in_dim(jnp.pad(vir_energy, (0, VPAD - VIRT)), first_row, WIN, 0)
    out = total[:, :VIRT] / (vir_rows[:, None] + vir_energy[None, :] - occ_sum)
    first_cell = grid_pos * share - first_row * VIRT
    return lax.dynamic_slice_in_dim(out.reshape(1, WIN * VIRT), first_cell, share, 1)


def solution(mesh):
    placed = (
        P("pair", None, None),
        P(None, "grid"),
        P("grid", "pair"),
        P("grid", "pair"),
        P("pair"),
        P(),
        P(),
    )
    return jax.shard_map(
        local, mesh=mesh, in_specs=placed, out_specs=P("pair", "grid"), check_vma=False
    )
```

time: 997 us -> 197 us (0.20)
  waiting for transfers between devices: 842 us -> 82.5 us
  Pallas kernels: 0 us -> 70.8 us
  local copies, waits for them, and re-layouts: 72.9 us -> 7.6 us
  matrix products: 46.2 us -> 0 us
  starting transfers between devices: 0.53 us -> 26.5 us
  between operations: 17.5 us -> 2.89 us
  other arithmetic: 16.4 us -> 5.87 us
    psum x2 -> x0, waiting for transfers between devices: 484 us -> none  [the longest x1 296 us: broadcast(): return lax.psum(block, axis)]
    reduce_scatter x1 -> x0, waiting for transfers between devices: 359 us -> none  [local(): lax.psum_scatter(partials, 'pair', scatter_dimension=0, tiled=True)]
    ppermute x0 -> x21, waiting for transfers between devices: none -> 82.5 us  [move(): return lax.ppermute(block, BOTH, pairs)]
    pallas_call x0 -> x9, Pallas kernels: none -> 70.8 us  [call(): pl.pallas_call(kernel, out_shape=out_shape, grid_spec=spec, input_output_...]
    dot_general x3 -> x0, matrix products: 46.2 us -> none  [the longest x1 26.3 us: local(): jnp.einsum('kpq,vq->kpv', weighted, q_factors, preferred_element_type=jnp...]
    reshape x3 -> x1, local copies, waits for them, and re-layouts: 35.2 us -> 0.97 us  [local(): out.reshape(1, WIN * VIRT)]
    ppermute x0 -> x21, starting transfers between devices: none -> 26.5 us  [move(): return lax.ppermute(block, BOTH, pairs)]
    add x1 -> x0, local copies, waits for them, and re-layouts: 12.2 us -> none  [local(): vir_energy[:, None] + vir_energy[None, :]]
  transfers between devices with their start and end apart: 4 -> 21, of which waited for: 3 -> 11; matrix products, arithmetic and copies ran while one was open for 3% -> 3% of each run, Pallas kernels for 0% -> 26%
where the time goes in v2:
time: 197 us; the launch traced here: 196 us
  waiting for transfers between devices  82.5 us (42%)
  Pallas kernels  70.8 us (36%)
  starting transfers between devices  26.5 us (13%)
  local copies, waits for them, and re-layouts  7.6 us (4%)
  other arithmetic  5.87 us (3%)
  between operations  2.89 us (1%)
    ppermute x21, waiting for transfers between devices, move(): return lax.ppermute(block, BOTH, pairs)  82.5 us
    pallas_call x9, Pallas kernels, call(): pl.pallas_call(kernel, out_shape=out_shape, grid_spec=spec, input_output_...  70.8 us
    ppermute x21, starting transfers between devices, move(): return lax.ppermute(block, BOTH, pairs)  26.5 us
  transfers between devices with their start and end apart: 21, of which 11 were waited for; matrix products, arithmetic and copies ran while one was open for 3% of the time, Pallas kernels for 26%

profile of v2, /device:TPU:0, one launch (start us, length us, event | category | flops | bytes accessed | tf_op | source)
XLA Modules:
  0.0 196.2 jit_solution(15445502505361923433)
XLA Ops:
  0.0 4.1 %collective-permute-start.2 = (bf16[1500,375]{1,0:T(8,128)(2,1)}, bf16[1500,375]{1,0:T(8,128)(2,1)}, u32[]{:S(2)}, u32[]{:S(2)}) collective-permute-start(bf16[1500,375]{1,0:T(8,128)(2,1)} %mine_ref.1), channel_id=1, source_target_pairs={{0,96},{2,98},{4,100},{6,102},{8,104},{10,106},{12,108},{14,110},{... | collective-permute-start | bytes 3375008 | tf_op jit(solution)/shard_map/ppermute | solution.py:33
  4.1 0.0 collective-permute-start.1
  4.1 2.1 %shard_map.78 = bf16[384,768]{1,0:T(8,128)(2,1)} custom-call(bf16[375,750]{1,0:T(8,128)(2,1)} %z_ref.1, f32[3,6]{1,0:T(4,128)} %s_ref.1), custom_call_target="tpu_custom_call" | custom-call | tf_op jit(solution)/shard_map/pallas_call | solution.py:65
  6.2 1.5 collective-permute-start.8
  7.7 0.7 collective-permute-start.9
  8.4 0.1 collective-permute-start.7
  8.6 14.2 %collective-permute-done.8 = bf16[384,768]{1,0:T(8,128)(2,1)S(1)} collective-permute-done((bf16[384,768]{1,0:T(8,128)(2,1)}, bf16[384,768]{1,0:T(8,128)(2,1)S(1)}, u32[]{:S(2)}, u32[]{:S(2)}) %collective-permute-start.8) | collective-permute-done | bytes 589856 | tf_op jit(solution)/shard_map/ppermute | solution.py:33
  22.8 0.0 collective-permute-done.9
  22.8 1.2 select_bitcast_fusion.1
  23.9 0.1 pad_maximum_fusion.z0_ref
  24.1 1.6 collective-permute-start.10
  25.7 1.7 collective-permute-start.11
  27.4 1.8 collective-permute-done.2.mine_ref
  29.1 3.4 %collective-permute-done.1.mine_ref = bf16[1500,375]{1,0:T(8,128)(2,1)} collective-permute-done((bf16[1500,375]{1,0:T(8,128)(2,1)}, bf16[1500,375]{1,0:T(8,128)(2,1)}, u32[]{:S(2)}, u32[]{:S(2)}) %collective-permute-start.1) | collective-permute-done | bytes 1125032 | tf_op jit(solution)/shard_map/ppermute | solution.py:33
  32.5 1.4 broadcast_select_fusion.1
  34.0 0.1 collective-permute-start.3
  34.0 17.9 %collective-permute-done.10.z2_ref = bf16[2,384,768]{2,1,0:T(8,128)(2,1)S(1)} collective-permute-done((bf16[2,384,768]{2,1,0:T(8,128)(2,1)S(1)}, bf16[2,384,768]{2,1,0:T(8,128)(2,1)S(1)}, u32[]{:S(2)}, u32[]{:S(2)}) %collective-permute-start.10) | collective-permute-done | bytes 1179680 | tf_op jit(solution)/shard_map/ppermute | solution.py:33
  51.9 0.0 collective-permute-done.11.z1_ref
  51.9 0.1 broadcast_select_fusion
  52.1 0.9 copy-done.1
  53.0 0.4 copy-done.2
  53.4 1.1 collective-permute-start.12
  54.5 2.8 %collective-permute-start = (bf16[1500,375]{1,0:T(8,128)(2,1)}, bf16[1500,375]{1,0:T(8,128)(2,1)}, u32[]{:S(2)}, u32[]{:S(2)}) collective-permute-start(bf16[1500,375]{1,0:T(8,128)(2,1)} %mine_ref.1), channel_id=1, source_target_pairs={{0,17},{2,19},{4,21},{6,23},{8,25},{10,27},{12,29},{14,31},{1,16},... | collective-permute-start | bytes 3375008 | tf_op jit(solution)/shard_map/ppermute | solution.py:33
  57.3 0.0 collective-permute-start.6
  57.3 0.0 collective-permute-done.7.theirs_ref
  57.3 0.5 collective-permute-start.5
  57.8 0.0 collective-permute-done.3.mine_ref
  57.8 0.1 collective-permute-start.4
  58.0 0.7 stack.70.info
  58.7 4.1 %shard_map.74.refs_0_ = bf16[4,1536,768]{2,1,0:T(8,128)(2,1)} custom-call(s32[16]{0:T(128)} %stack.70.info, bf16[1500,375]{1,0:T(8,128)(2,1)} %mine_ref.1, bf16[1500,375]{1,0:T(8,128)(2,1)} %collective-permute-done.7.theirs_ref), custom_call_target="tpu_custom_call" | custom-call | tf_op jit(solution)/shard_map/pallas_call | solution.py:65
  62.8 19.4 %collective-permute-done.other_ref = bf16[1500,375]{1,0:T(8,128)(2,1)} collective-permute-done((bf16[1500,375]{1,0:T(8,128)(2,1)}, bf16[1500,375]{1,0:T(8,128)(2,1)}, u32[]{:S(2)}, u32[]{:S(2)}) %collective-permute-start) | collective-permute-done | bytes 1125032 | tf_op jit(solution)/shard_map/ppermute | solution.py:33
  82.1 8.6 %shard_map.73 = (bf16[768,1536]{1,0:T(8,128)(2,1)}, bf16[2,8,96,768]{3,2,1,0:T(8,128)(2,1)}) custom-call(bf16[1500,375]{1,0:T(8,128)(2,1)} %mine_ref.1, bf16[1500,375]{1,0:T(8,128)(2,1)} %collective-permute-done.other_ref, bf16[1,1500,1500]{2,1,0:T(8,128)(2,1)} %amp_ref.1), custom_call_target="tpu_custom_call" | custom-call | tf_op jit(solution)/shard_map/pallas_call | solution.py:65
  90.7 0.0 collective-permute-done.6.theirs_ref
  90.7 4.1 %shard_map.75.refs_0_ = bf16[4,1536,768]{2,1,0:T(8,128)(2,1)} custom-call(s32[16]{0:T(128)} %stack.70.info, bf16[1500,375]{1,0:T(8,128)(2,1)} %collective-permute-done.2.mine_ref, bf16[1500,375]{1,0:T(8,128)(2,1)} %collective-permute-done.6.theirs_ref, bf16[4,1536,768]{2,1,0:T(8,128)(2,1)} %shard_map.74.refs_0_), custom_call_target="tpu_custom_call", output_to_operand_aliasing={{}: (3, {})} | custom-call | tf_op jit(solution)/shard_map/pallas_call | solution.py:65
  94.8 0.0 collective-permute-done.5.theirs_ref
  94.8 4.1 %shard_map.76.refs_0_ = bf16[4,1536,768]{2,1,0:T(8,128)(2,1)} custom-call(s32[16]{0:T(128)} %stack.70.info, bf16[1500,375]{1,0:T(8,128)(2,1)} %collective-permute-done.1.mine_ref, bf16[1500,375]{1,0:T(8,128)(2,1)} %collective-permute-done.5.theirs_ref, bf16[4,1536,768]{2,1,0:T(8,128)(2,1)} %shard_map.75.refs_0_), custom_call_target="tpu_custom_call", output_to_operand_aliasing={{}: (3, {})} | custom-call | tf_op jit(solution)/shard_map/pallas_call | solution.py:65
  98.9 4.3 %shard_map.77.x_ref = bf16[4,1536,768]{2,1,0:T(8,128)(2,1)} custom-call(s32[16]{0:T(128)} %stack.70.info, bf16[1500,375]{1,0:T(8,128)(2,1)} %copy-done.5, bf16[1500,375]{1,0:T(8,128)(2,1)} %collective-permute-done.4.theirs_ref, bf16[4,1536,768]{2,1,0:T(8,128)(2,1)} %shard_map.76.refs_0_), custom_call_target="tpu_custom_call", output_to_operand_aliasing={{}: (3, {})} | custom-call | tf_op jit(solution)/shard_map/pallas_call | solution.py:65
  103.2 23.3 %shard_map.79.back_ref = f32[768,1536]{1,0:T(8,128)} custom-call(s32[16]{0:T(128)} %stack.70.info, bf16[768,1536]{1,0:T(8,128)(2,1)} %get-tuple-element.17.h_ref, bf16[4,1536,768]{2,1,0:T(8,128)(2,1)} %shard_map.77.x_ref, bf16[2,384,768]{2,1,0:T(8,128)(2,1)} %copy-done, bf16[2,384,768]{2,1,0:T(8,128)(2,1)} %copy-done.2, bf16[2,384,768]{2,1,0:T(8,128)(2,1)} %copy-done.1), custom_call_target="tpu_custom_call" | custom-call | tf_op jit(solution)/shard_map/pallas_call | solution.py:65
  126.5 1.0 copy-done.4
  127.6 15.5 %shard_map.80 = (f32[768,1536]{1,0:T(8,128)}, bf16[768,1536]{1,0:T(8,128)(2,1)}) custom-call(s32[16]{0:T(128)} %stack.70.info, bf16[768,1536]{1,0:T(8,128)(2,1)} %get-tuple-element.17.h_ref, bf16[4,1536,768]{2,1,0:T(8,128)(2,1)} %shard_map.77.x_ref, bf16[2,384,768]{2,1,0:T(8,128)(2,1)} %copy-done.4, f32[768,1536]{1,0:T(8,128)} %shard_map.79.back_ref, ...), custom_call_target="tpu_custom_call" | custom-call | tf_op jit(solution)/shard_map/pallas_call | solution.py:65
  143.1 0.0 collective-permute-start.13
  143.1 4.7 %collective-permute-done.13.got_ref = bf16[768,1536]{1,0:T(8,128)(2,1)S(1)} collective-permute-done((bf16[768,1536]{1,0:T(8,128)(2,1)}, bf16[768,1536]{1,0:T(8,128)(2,1)S(1)}, u32[]{:S(2)}, u32[]{:S(2)}) %collective-permute-start.13) | collective-permute-done | bytes 2359328 | tf_op jit(solution)/shard_map/ppermute | solution.py:33
  147.8 1.4 copy-done.3
  149.3 4.7 %shard_map.81 = (f32[96,1536]{1,0:T(8,128)}, bf16[96,1536]{1,0:T(8,128)(2,1)}, bf16[96,1536]{1,0:T(8,128)(2,1)}, bf16[96,1536]{1,0:T(8,128)(2,1)}, bf16[96,1536]...) custom-call(f32[768,1536]{1,0:T(8,128)} %get-tuple-element.19.keep_ref, ...), custom_call_target="tpu_custom_call" | custom-call | tf_op jit(solution)/shard_map/pallas_call | solution.py:65
  154.0 1.0 collective-permute-start.15
  154.9 2.2 %collective-permute-start.14 = (bf16[96,1536]{1,0:T(8,128)(2,1)}, bf16[96,1536]{1,0:T(8,128)(2,1)S(1)}, u32[]{:S(2)}, u32[]{:S(2)}) collective-permute-start(bf16[96,1536]{1,0:T(8,128)(2,1)} %get-tuple-element.22), channel_id=1, source_target_pairs={{0,32},{2,34},{4,36},{6,38},{8,40},{10,42},{12,44},{14,46},{1,33},... | collective-permute-start | bytes 884744 | tf_op jit(solution)/shard_map/ppermute | solution.py:33
  157.8 0.7 fusion.6
  160.4 0.1 pad_dynamic-slice_fusion
  160.5 1.3 fusion.9
  161.8 1.0 collective-permute-start.16
  162.9 2.0 %collective-permute-start.17 = (bf16[96,1536]{1,0:T(8,128)(2,1)}, bf16[96,1536]{1,0:T(8,128)(2,1)S(1)}, u32[]{:S(2)}, u32[]{:S(2)}) collective-permute-start(bf16[96,1536]{1,0:T(8,128)(2,1)} %get-tuple-element.25), channel_id=1, source_target_pairs={{0,16},{2,18},{4,20},{6,22},{8,24},{10,26},{12,28},{14,30},{1,17},... | collective-permute-start | bytes 884744 | tf_op jit(solution)/shard_map/ppermute | solution.py:33
  164.8 2.0 %collective-permute-start.18 = (bf16[96,1536]{1,0:T(8,128)(2,1)}, bf16[96,1536]{1,0:T(8,128)(2,1)S(1)}, u32[]{:S(2)}, u32[]{:S(2)}) collective-permute-start(bf16[96,1536]{1,0:T(8,128)(2,1)} %get-tuple-element.26), channel_id=1, source_target_pairs={{0,48},{2,50},{4,52},{6,54},{8,56},{10,58},{12,60},{14,62},{1,49},... | collective-permute-start | bytes 884744 | tf_op jit(solution)/shard_map/ppermute | solution.py:33
  166.8 0.0 collective-permute-done.15
  166.8 2.1 %collective-permute-start.19 = (bf16[96,1536]{1,0:T(8,128)(2,1)}, bf16[96,1536]{1,0:T(8,128)(2,1)S(1)}, u32[]{:S(2)}, u32[]{:S(2)}) collective-permute-start(bf16[96,1536]{1,0:T(8,128)(2,1)} %get-tuple-element.27), channel_id=1, source_target_pairs={{0,80},{2,82},{4,84},{6,86},{8,88},{10,90},{12,92},{14,94},{1,81},... | collective-permute-start | bytes 884744 | tf_op jit(solution)/shard_map/ppermute | solution.py:33
  168.9 2.1 %collective-permute-done.14 = bf16[96,1536]{1,0:T(8,128)(2,1)S(1)} collective-permute-done((bf16[96,1536]{1,0:T(8,128)(2,1)}, bf16[96,1536]{1,0:T(8,128)(2,1)S(1)}, u32[]{:S(2)}, u32[]{:S(2)}) %collective-permute-start.14) | collective-permute-done | bytes 294944 | tf_op jit(solution)/shard_map/ppermute | solution.py:33
  171.1 2.0 %collective-permute-start.20 = (bf16[96,1536]{1,0:T(8,128)(2,1)}, bf16[96,1536]{1,0:T(8,128)(2,1)S(1)}, u32[]{:S(2)}, u32[]{:S(2)}) collective-permute-start(bf16[96,1536]{1,0:T(8,128)(2,1)} %get-tuple-element.28), channel_id=1, source_target_pairs={{0,112},{2,114},{4,116},{6,118},{8,120},{10,122},{12,124},{14,126}... | collective-permute-start | bytes 884744 | tf_op jit(solution)/shard_map/ppermute | solution.py:33
  173.1 0.1 convert_add_fusion
  173.1 1.4 collective-permute-done.17
  174.5 5.9 %collective-permute-done.18 = bf16[96,1536]{1,0:T(8,128)(2,1)S(1)} collective-permute-done((bf16[96,1536]{1,0:T(8,128)(2,1)}, bf16[96,1536]{1,0:T(8,128)(2,1)S(1)}, u32[]{:S(2)}, u32[]{:S(2)}) %collective-permute-start.18) | collective-permute-done | bytes 294944 | tf_op jit(solution)/shard_map/ppermute | solution.py:33
  180.5 7.5 %collective-permute-done.19 = bf16[96,1536]{1,0:T(8,128)(2,1)S(1)} collective-permute-done((bf16[96,1536]{1,0:T(8,128)(2,1)}, bf16[96,1536]{1,0:T(8,128)(2,1)S(1)}, u32[]{:S(2)}, u32[]{:S(2)}) %collective-permute-start.19) | collective-permute-done | bytes 294944 | tf_op jit(solution)/shard_map/ppermute | solution.py:33
  187.9 4.2 %collective-permute-done.20 = bf16[96,1536]{1,0:T(8,128)(2,1)S(1)} collective-permute-done((bf16[96,1536]{1,0:T(8,128)(2,1)}, bf16[96,1536]{1,0:T(8,128)(2,1)S(1)}, u32[]{:S(2)}, u32[]{:S(2)}) %collective-permute-start.20) | collective-permute-done | bytes 294944 | tf_op jit(solution)/shard_map/ppermute | solution.py:33
  192.2 1.0 fusion.5
  193.2 1.0 reshape.34
  194.1 2.0 %constant_dynamic-slice_fusion = f32[1,140625]{1,0:T(1,128)} fusion(f32[1,144000]{1,0:T(1,128)S(1)} %reshape.34, s32[]{:T(128)S(6)} %select_n.161), kind=kLoop, calls=%fused_computation.26 | loop fusion | bytes 1125004 | tf_op jit(solution)/shard_map/dynamic_slice | solution.py:301
  (18 shorter events, 0.1 us)
Async XLA Ops:
  0.0 29.1 %collective-permute-start.2 = (bf16[1500,375]{1,0:T(8,128)(2,1)}, bf16[1500,375]{1,0:T(8,128)(2,1)}, u32[]{:S(2)}, u32[]{:S(2)}) collective-permute-start(bf16[1500,375]{1,0:T(8,128)(2,1)} %mine_ref.1), channel_id=1, source_target_pairs={{0,96},{2,98},{4,100},{6,102},{8,104},{10,106},{12,108},{14,110},{... | collective-permute-start | bytes 3375008 | tf_op jit(solution)/shard_map/ppermute | solution.py:33
  4.1 28.4 %collective-permute-start.1 = (bf16[1500,375]{1,0:T(8,128)(2,1)}, bf16[1500,375]{1,0:T(8,128)(2,1)}, u32[]{:S(2)}, u32[]{:S(2)}) collective-permute-start(bf16[1500,375]{1,0:T(8,128)(2,1)} %mine_ref.1), channel_id=1, source_target_pairs={{0,32},{2,34},{4,36},{6,38},{8,40},{10,42},{12,44},{14,46},{1,33},... | collective-permute-start | bytes 3375008 | tf_op jit(solution)/shard_map/ppermute | solution.py:33
  6.2 16.5 %collective-permute-start.8 = (bf16[384,768]{1,0:T(8,128)(2,1)}, bf16[384,768]{1,0:T(8,128)(2,1)S(1)}, u32[]{:S(2)}, u32[]{:S(2)}) collective-permute-start(bf16[384,768]{1,0:T(8,128)(2,1)} %shard_map.78), channel_id=1, source_target_pairs={{0,1},{2,3},{4,5},{6,7},{8,9},{10,11},{12,13},{14,15},{1,17},{3,19... | collective-permute-start | bytes 1769480 | tf_op jit(solution)/shard_map/ppermute | solution.py:33
  7.7 15.0 %collective-permute-start.9 = (bf16[384,768]{1,0:T(8,128)(2,1)}, bf16[384,768]{1,0:T(8,128)(2,1)S(1)}, u32[]{:S(2)}, u32[]{:S(2)}) collective-permute-start(bf16[384,768]{1,0:T(8,128)(2,1)} %shard_map.78), channel_id=1, source_target_pairs={{1,16},{3,18},{5,20},{7,22},{9,24},{11,26},{13,28},{15,30},{16,1},... | collective-permute-start | bytes 1769480 | tf_op jit(solution)/shard_map/ppermute | solution.py:33
  8.4 48.9 %collective-permute-start.7 = (bf16[1500,375]{1,0:T(8,128)(2,1)}, bf16[1500,375]{1,0:T(8,128)(2,1)}, u32[]{:S(2)}, u32[]{:S(2)}) collective-permute-start(bf16[1500,375]{1,0:T(8,128)(2,1)} %mine_ref.1), channel_id=1, source_target_pairs={{0,8},{2,10},{4,12},{6,14},{8,0},{10,2},{12,4},{14,6},{1,9},{3,11}... | collective-permute-start | bytes 3375008 | tf_op jit(solution)/shard_map/ppermute | solution.py:33
  24.0 9.9 %copy-start = (bf16[2,384,768]{2,1,0:T(8,128)(2,1)}, bf16[2,384,768]{2,1,0:T(8,128)(2,1)S(1)}, u32[]{:S(2)}) copy-start(bf16[2,384,768]{2,1,0:T(8,128)(2,1)S(1)} %pad_maximum_fusion.z0_ref) | copy-start | bytes 3538948
  24.1 27.9 %collective-permute-start.10 = (bf16[2,384,768]{2,1,0:T(8,128)(2,1)S(1)}, bf16[2,384,768]{2,1,0:T(8,128)(2,1)S(1)}, u32[]{:S(2)}, u32[]{:S(2)}) collective-permute-start(bf16[2,384,768]{2,1,0:T(8,128)(2,1)S(1)} %pad_maximum_fusion.z0_ref), channel_id=1, source_target_pairs={{0,2},{2,4},{4,6},{6,0},{8,10},{10,12},{12,14},{14,8},{1,3},{3,5},... | collective-permute-start | bytes 3538952 | tf_op jit(solution)/shard_map/ppermute | solution.py:33
  25.7 26.2 %collective-permute-start.11 = (bf16[2,384,768]{2,1,0:T(8,128)(2,1)S(1)}, bf16[2,384,768]{2,1,0:T(8,128)(2,1)S(1)}, u32[]{:S(2)}, u32[]{:S(2)}) collective-permute-start(bf16[2,384,768]{2,1,0:T(8,128)(2,1)S(1)} %pad_maximum_fusion.z0_ref), channel_id=1, source_target_pairs={{0,6},{2,0},{4,2},{6,4},{8,14},{10,8},{12,10},{14,12},{1,7},{3,1},... | collective-permute-start | bytes 3538952 | tf_op jit(solution)/shard_map/ppermute | solution.py:33
  34.0 23.8 %collective-permute-start.3 = (bf16[1500,375]{1,0:T(8,128)(2,1)S(1)}, bf16[1500,375]{1,0:T(8,128)(2,1)S(1)}, u32[]{:S(2)}, u32[]{:S(2)}) collective-permute-start(bf16[1500,375]{1,0:T(8,128)(2,1)S(1)} %broadcast_select_fusion.1), channel_id=1, source_target_pairs={{0,32},{2,34},{4,36},{6,38},{8,104},{10,106},{12,108},{14,110},{1,... | collective-permute-start | bytes 3375008 | tf_op jit(solution)/shard_map/ppermute | solution.py:33
  51.9 1.1 copy-start.1
  51.9 1.5 copy-start.2
  53.4 73.2 %collective-permute-start.12 = (bf16[2,384,768]{2,1,0:T(8,128)(2,1)S(1)}, bf16[2,384,768]{2,1,0:T(8,128)(2,1)S(1)}, u32[]{:S(2)}, u32[]{:S(2)}) collective-permute-start(bf16[2,384,768]{2,1,0:T(8,128)(2,1)S(1)} %broadcast_select_fusion), channel_id=1, source_target_pairs={{0,2},{2,4},{4,6},{6,0},{8,14},{10,8},{12,10},{14,12},{1,3},{3,5},... | collective-permute-start | bytes 3538952 | tf_op jit(solution)/shard_map/ppermute | solution.py:33
  54.5 27.6 %collective-permute-start = (bf16[1500,375]{1,0:T(8,128)(2,1)}, bf16[1500,375]{1,0:T(8,128)(2,1)}, u32[]{:S(2)}, u32[]{:S(2)}) collective-permute-start(bf16[1500,375]{1,0:T(8,128)(2,1)} %mine_ref.1), channel_id=1, source_target_pairs={{0,17},{2,19},{4,21},{6,23},{8,25},{10,27},{12,29},{14,31},{1,16},... | collective-permute-start | bytes 3375008 | tf_op jit(solution)/shard_map/ppermute | solution.py:33
  57.3 33.4 %collective-permute-start.6 = (bf16[1500,375]{1,0:T(8,128)(2,1)}, bf16[1500,375]{1,0:T(8,128)(2,1)}, u32[]{:S(2)}, u32[]{:S(2)}) collective-permute-start(bf16[1500,375]{1,0:T(8,128)(2,1)} %collective-permute-done.2.mine_ref), channel_id=1, source_target_pairs={{0,8},{2,10},{4,12},{6,14},{8,0},{10,2},{12,4},{14,6},{1,9},{3,11}... | collective-permute-start | bytes 3375008 | tf_op jit(solution)/shard_map/ppermute | solution.py:33
  57.3 37.5 %collective-permute-start.5 = (bf16[1500,375]{1,0:T(8,128)(2,1)}, bf16[1500,375]{1,0:T(8,128)(2,1)}, u32[]{:S(2)}, u32[]{:S(2)}) collective-permute-start(bf16[1500,375]{1,0:T(8,128)(2,1)} %collective-permute-done.1.mine_ref), channel_id=1, source_target_pairs={{0,8},{2,10},{4,12},{6,14},{8,0},{10,2},{12,4},{14,6},{1,9},{3,11}... | collective-permute-start | bytes 3375008 | tf_op jit(solution)/shard_map/ppermute | solution.py:33
  57.8 4.9 %copy-start.5 = (bf16[1500,375]{1,0:T(8,128)(2,1)}, bf16[1500,375]{1,0:T(8,128)(2,1)S(1)}, u32[]{:S(2)}) copy-start(bf16[1500,375]{1,0:T(8,128)(2,1)S(1)} %collective-permute-done.3.mine_ref) | copy-start | bytes 3375004
  57.8 41.1 %collective-permute-start.4 = (bf16[1500,375]{1,0:T(8,128)(2,1)S(1)}, bf16[1500,375]{1,0:T(8,128)(2,1)}, u32[]{:S(2)}, u32[]{:S(2)}) collective-permute-start(bf16[1500,375]{1,0:T(8,128)(2,1)S(1)} %collective-permute-done.3.mine_ref), channel_id=1, source_target_pairs={{0,8},{2,10},{4,12},{6,14},{8,0},{10,2},{12,4},{14,6},{1,9},{3,11}... | collective-permute-start | bytes 3375008 | tf_op jit(solution)/shard_map/ppermute | solution.py:33
  126.5 1.0 copy-start.4
  143.1 4.7 %collective-permute-start.13 = (bf16[768,1536]{1,0:T(8,128)(2,1)}, bf16[768,1536]{1,0:T(8,128)(2,1)S(1)}, u32[]{:S(2)}, u32[]{:S(2)}) collective-permute-start(bf16[768,1536]{1,0:T(8,128)(2,1)} %get-tuple-element.20), channel_id=1, source_target_pairs={{0,8},{2,10},{4,12},{6,14},{8,0},{10,2},{12,4},{14,6},{1,9},{3,11}... | collective-permute-start | bytes 7077896 | tf_op jit(solution)/shard_map/ppermute | solution.py:33
  147.8 1.4 copy-start.3
  149.3 11.1 %copy-start.7 = (f32[1500]{0:T(1024)S(1)}, f32[1500]{0:T(1024)}, u32[]{:S(2)}) copy-start(f32[1500]{0:T(1024)} %param.12) | copy-start | bytes 18004
  149.3 11.2 %copy-start.8 = (f32[150]{0:T(256)S(1)}, f32[150]{0:T(256)}, u32[]{:S(2)}) copy-start(f32[150]{0:T(256)} %param.13) | copy-start | bytes 1804
  154.0 19.1 %copy-start.6 = (f32[96,1536]{1,0:T(8,128)S(1)}, f32[96,1536]{1,0:T(8,128)}, u32[]{:S(2)}) copy-start(f32[96,1536]{1,0:T(8,128)} %get-tuple-element.21) | copy-start | bytes 1769476
  154.0 12.8 %collective-permute-start.15 = (bf16[96,1536]{1,0:T(8,128)(2,1)}, bf16[96,1536]{1,0:T(8,128)(2,1)S(1)}, u32[]{:S(2)}, u32[]{:S(2)}) collective-permute-start(bf16[96,1536]{1,0:T(8,128)(2,1)} %get-tuple-element.23), channel_id=1, source_target_pairs={{0,64},{2,66},{4,68},{6,70},{8,72},{10,74},{12,76},{14,78},{1,65},... | collective-permute-start | bytes 884744 | tf_op jit(solution)/shard_map/ppermute | solution.py:33
  154.9 16.1 %collective-permute-start.14 = (bf16[96,1536]{1,0:T(8,128)(2,1)}, bf16[96,1536]{1,0:T(8,128)(2,1)S(1)}, u32[]{:S(2)}, u32[]{:S(2)}) collective-permute-start(bf16[96,1536]{1,0:T(8,128)(2,1)} %get-tuple-element.22), channel_id=1, source_target_pairs={{0,32},{2,34},{4,36},{6,38},{8,40},{10,42},{12,44},{14,46},{1,33},... | collective-permute-start | bytes 884744 | tf_op jit(solution)/shard_map/ppermute | solution.py:33
  161.8 11.3 %collective-permute-start.16 = (bf16[96,1536]{1,0:T(8,128)(2,1)}, bf16[96,1536]{1,0:T(8,128)(2,1)S(1)}, u32[]{:S(2)}, u32[]{:S(2)}) collective-permute-start(bf16[96,1536]{1,0:T(8,128)(2,1)} %get-tuple-element.24), channel_id=1, source_target_pairs={{0,96},{2,98},{4,100},{6,102},{8,104},{10,106},{12,108},{14,110},{... | collective-permute-start | bytes 884744 | tf_op jit(solution)/shard_map/ppermute | solution.py:33
  162.9 11.7 %collective-permute-start.17 = (bf16[96,1536]{1,0:T(8,128)(2,1)}, bf16[96,1536]{1,0:T(8,128)(2,1)S(1)}, u32[]{:S(2)}, u32[]{:S(2)}) collective-permute-start(bf16[96,1536]{1,0:T(8,128)(2,1)} %get-tuple-element.25), channel_id=1, source_target_pairs={{0,16},{2,18},{4,20},{6,22},{8,24},{10,26},{12,28},{14,30},{1,17},... | collective-permute-start | bytes 884744 | tf_op jit(solution)/shard_map/ppermute | solution.py:33
  164.8 15.6 %collective-permute-start.18 = (bf16[96,1536]{1,0:T(8,128)(2,1)}, bf16[96,1536]{1,0:T(8,128)(2,1)S(1)}, u32[]{:S(2)}, u32[]{:S(2)}) collective-permute-start(bf16[96,1536]{1,0:T(8,128)(2,1)} %get-tuple-element.26), channel_id=1, source_target_pairs={{0,48},{2,50},{4,52},{6,54},{8,56},{10,58},{12,60},{14,62},{1,49},... | collective-permute-start | bytes 884744 | tf_op jit(solution)/shard_map/ppermute | solution.py:33
  166.8 21.1 %collective-permute-start.19 = (bf16[96,1536]{1,0:T(8,128)(2,1)}, bf16[96,1536]{1,0:T(8,128)(2,1)S(1)}, u32[]{:S(2)}, u32[]{:S(2)}) collective-permute-start(bf16[96,1536]{1,0:T(8,128)(2,1)} %get-tuple-element.27), channel_id=1, source_target_pairs={{0,80},{2,82},{4,84},{6,86},{8,88},{10,90},{12,92},{14,94},{1,81},... | collective-permute-start | bytes 884744 | tf_op jit(solution)/shard_map/ppermute | solution.py:33
  171.1 21.1 %collective-permute-start.20 = (bf16[96,1536]{1,0:T(8,128)(2,1)}, bf16[96,1536]{1,0:T(8,128)(2,1)S(1)}, u32[]{:S(2)}, u32[]{:S(2)}) collective-permute-start(bf16[96,1536]{1,0:T(8,128)(2,1)} %get-tuple-element.28), channel_id=1, source_target_pairs={{0,112},{2,114},{4,116},{6,118},{8,120},{10,122},{12,124},{14,126}... | collective-permute-start | bytes 884744 | tf_op jit(solution)/shard_map/ppermute | solution.py:33

commit v3 on v2

v3 whole, which is shorter than its diff:
```python
import itertools

import jax
import jax.numpy as jnp
from jax import lax
from jax.experimental import pallas as pl
from jax.experimental.pallas import tpu as pltpu
from jax.sharding import PartitionSpec as P

VIRT = 1500
ZBLK = 125
BLK = 375
BPAD = 384
TWO = 2 * BPAD
VPAD = 1536
WIN = 96
BOTH = ("grid", "pair")
ALL = list(itertools.product(range(4), range(4), range(2), range(4)))
F32 = jnp.float32
BF16 = jnp.bfloat16


def flat_index(z, x, c, y):
    return ((z % 4) * 4 + (x % 4) // 2 * 2 + c % 2) * 8 + (y % 4) * 2 + (x % 4) % 2


def move(block, target):
    pairs = []
    for z, x, c, y in ALL:
        dest = target(z, x, c, y)
        if dest is not None:
            pairs.append((flat_index(z, x, c, y), flat_index(*dest)))
    return lax.ppermute(block, BOTH, pairs)


def across(block):
    return move(block, lambda z, x, c, y: (z, x, 1 - c, y))


def pair_orbitals(packed, occ_count):
    row_ids = jnp.arange(1, occ_count, dtype=jnp.int32)
    starts = row_ids * (2 * occ_count - row_ids - 1) // 2
    first_occ = jnp.sum((starts[None, :] <= packed[:, None]).astype(jnp.int32), axis=1)
    second = packed - first_occ * (2 * occ_count - first_occ - 1) // 2 + first_occ + 1
    return (first_occ, second)


def dot(a, b, contract_a, contract_b):
    return lax.dot_general(
        a, b, (((contract_a,), (contract_b,)), ((), ())), preferred_element_type=F32
    )


VMEM = pl.BlockSpec(memory_space=pltpu.VMEM)
SMEM = pl.BlockSpec(memory_space=pltpu.SMEM)
HBM = pl.BlockSpec(memory_space=pl.ANY)


def call(kernel, out_shape, scratch, *args, in_specs=None, out_specs=None):
    many = isinstance(out_shape, (tuple, list))
    return pl.pallas_call(
        kernel,
        out_shape=out_shape,
        in_specs=in_specs or [VMEM] * len(args),
        out_specs=out_specs or (tuple([VMEM] * len(out_shape)) if many else VMEM),
        scratch_shapes=scratch,
        compiler_params=pltpu.CompilerParams(vmem_limit_bytes=56 * 2**20),
    )(*args)


def prepare(z_ref, s_ref, x_ref, z_out, x_out, tmp):
    tmp[...] = jnp.zeros_like(tmp)
    z = z_ref[...].astype(F32)
    tmp[:BLK, :BLK] = z[:, :BLK]
    tmp[:BLK, BPAD : BPAD + BLK] = z[:, BLK:]
    lane = lax.broadcasted_iota(jnp.int32, (1, TWO), 1)
    for r in range(3):
        row = jnp.zeros((1, TWO), F32)
        for q in range(6):
            start = (q // 3) * BPAD + (q % 3) * ZBLK
            row = jnp.where((lane >= start) & (lane < start + ZBLK), s_ref[r, q], row)
        for part in range(3):
            piece = row.astype(BF16).astype(F32)
            tmp[BLK + 3 * part + r : BLK + 3 * part + r + 1, :] = piece
            row = row - piece
    z_out[...] = tmp[...].astype(BF16)
    x_out[...] = jnp.zeros_like(x_out)
    x_out[:VIRT, :BLK] = x_ref[...]


def scaled(block):
    z = block.astype(F32)
    tail = z[BPAD - 16 :, :]
    parts = [tail[7 + r : 8 + r] + tail[10 + r : 11 + r] + tail[13 + r : 14 + r] for r in range(3)]
    row = lax.broadcasted_iota(jnp.int32, (BPAD, 1), 0)
    scale = jnp.where(row < ZBLK, parts[0], jnp.where(row < 2 * ZBLK, parts[1], parts[2]))
    return jnp.where(row < BLK, z * scale, 0.0)


def half_rows(x_ref, xf, w_ref):
    xf[...] = x_ref[...].astype(F32)
    for c in range(2):
        for chip in range(8):
            start = (chip * 2 + c) * BLK // 4
            w_ref[c, chip] = xf[start : start + WIN, :].astype(BF16)
    return xf[...].T.astype(BF16)


def half_own(x_ref, amp_ref, h_ref, w_ref, t_ref, xf):
    t_ref[...] = jnp.zeros_like(t_ref)
    t_ref[:VIRT, :VIRT] = amp_ref[0]
    h_ref[...] = dot(half_rows(x_ref, xf, w_ref), t_ref[...], 1, 0).astype(BF16)


def half_other(x_ref, t_ref, h_ref, w_ref, xf):
    h_ref[...] = dot(half_rows(x_ref, xf, w_ref), t_ref[...], 1, 0).astype(BF16)


def factor_copies(info, place, x_ref, slot_ref, sems):
    return [
        pltpu.make_async_copy(
            x_ref.at[2 * info[4 + place] + c], slot_ref.at[:, pl.ds(c * BPAD, BPAD)], sems.at[c]
        )
        for c in range(2)
    ]


def ladder(h_ref, x, z):
    projected = dot(h_ref[...], x, 1, 0)
    weighted = (projected * scaled(z)).astype(BF16)
    return dot(weighted, x, 1, 1)


def early_blocks(info, h0_ref, h1_ref, x_ref, *refs):
    z_refs, back_out = refs[:3], refs[3]
    xs, zs, acc, xsem, zsem, osem = refs[4:]
    loads = []
    for i in range(3):
        loads.append(factor_copies(info, i, x_ref, xs.at[i], xsem.at[i]))
        loads[i].append(pltpu.make_async_copy(z_refs[i], zs.at[i], zsem.at[i]))
        for load in loads[i]:
            load.start()
    stores = []
    for i in range(3):
        for load in loads[i]:
            load.wait()
        for b, h_ref in enumerate((h0_ref, h1_ref)):
            rows = pl.ds(b * BPAD, BPAD)
            part = ladder(h_ref, xs[i], zs[i, b])
            acc[rows, :] = part if i == 0 else acc[rows, :] + part
            if i == 2:
                stores.append(pltpu.make_async_copy(acc.at[rows, :], back_out.at[rows, :], osem.at[b]))
                stores[b].start()
    for store in stores:
        store.wait()


def gather_windows(info, side, w0_ref, w1_ref, left):
    for j in range(8):
        for b, w_ref in enumerate((w0_ref, w1_ref)):
            left[WIN * j : WIN * j + WIN, b * BPAD : b * BPAD + BPAD] = w_ref[side, info[8 + j]]


def last_block(info, h0_ref, h1_ref, x_ref, z_ref, back_in, w0_ref, w1_ref, back_out, give_ref, xs, acc, left, xsem, bsem):
    loads = factor_copies(info, 3, x_ref, xs, xsem)
    for load in loads:
        load.start()
    back_load = pltpu.make_async_copy(back_in, acc, bsem)
    back_load.start()
    gather_windows(info, 1 - info[0], w0_ref, w1_ref, left)
    for load in loads:
        load.wait()
    for b, h_ref in enumerate((h0_ref, h1_ref)):
        rows = pl.ds(b * BPAD, BPAD)
        part = ladder(h_ref, xs[...], z_ref[b])
        if b == 0:
            back_load.wait()
        back_out[rows, :] = (acc[rows, :] + part).astype(BF16)
    give_ref[...] = dot(left[...], back_out[...], 1, 0).astype(BF16)


def chip_total(info, back_ref, w0_ref, w1_ref, got_ref, own_ref, *refs):
    out_refs, left = refs[:7], refs[7]
    gather_windows(info, info[0], w0_ref, w1_ref, left)
    for n in range(6):
        cols = slice(256 * n, 256 * n + 256)
        part = dot(left[...], back_ref[:, cols], 1, 0) + got_ref[:, cols].astype(F32)
        own_ref[:, cols] = part[:WIN]
        for j, o_ref in enumerate(out_refs):
            o_ref[:, cols] = part[WIN * (j + 1) : WIN * (j + 2)].astype(BF16)


def shape(*dims, dtype=BF16):
    return jax.ShapeDtypeStruct(dims, dtype)


def local(amplitudes, factors, z_values, z_scales, pair_index, vir_energy, occ_energy):
    grid_pos = lax.axis_index("grid")
    pair_pos = lax.axis_index("pair")
    z_pos = grid_pos // 4
    x_hi = (grid_pos // 2) % 2
    core = grid_pos % 2
    y_pos = pair_pos // 2
    x_pos = 2 * x_hi + pair_pos % 2
    outer = (x_pos == 0) | (x_pos == 3)
    order = [(y_pos + i) % 4 for i in (0, 1, 3, 2)]
    chips = [(z_pos + j % 4) % 4 * 2 + (x_hi + j // 4) % 2 for j in range(8)]
    info = jnp.stack([core, core, core, core] + order + chips).astype(jnp.int32)

    z_own, x_own = call(
        prepare,
        (shape(BPAD, TWO), shape(VPAD, BPAD)),
        [pltpu.VMEM((BPAD, TWO), F32)],
        z_values,
        z_scales,
        factors,
        in_specs=[VMEM, SMEM, VMEM],
    )
    hop_a = {0: 1, 3: 2, 2: 0, 1: 3}
    hop_b = {2: 1, 1: 2}
    recv_a = move(z_own, lambda z, x, c, y: (z, hop_a[x], c, y))
    recv_b = move(z_own, lambda z, x, c, y: (z, hop_b[x], c, y) if x in hop_b else None)
    groups = [[4 * z + 2 * h + c for z in range(4) for c in range(2)] for h in range(2)]
    x_all = lax.all_gather(x_own, "grid", axis_index_groups=groups)
    half_0, wins_0, amp = call(
        half_own,
        (shape(BPAD, VPAD), shape(2, 8, WIN, BPAD), shape(VPAD, VPAD)),
        [pltpu.VMEM((VPAD, BPAD), F32)],
        x_own,
        amplitudes,
    )
    z_here = jnp.stack([jnp.where(outer, z_own, recv_a), jnp.where(outer, recv_a, recv_b)])
    z_here, x_again, half_0 = lax.optimization_barrier((z_here, x_own, half_0))
    z_before = move(z_here, lambda z, x, c, y: (z, x, c, y + 1))
    z_after = move(z_here, lambda z, x, c, y: (z, x, c, y - 1))
    x_other = move(x_again, lambda z, x, c, y: (z, 3 - x, c, y))

    z_onward = jnp.where(core == 0, z_before, z_after)
    z_far = move(z_onward, lambda z, x, c, y: (z, x, c, y + 1 - 2 * c))
    half_1, wins_1 = call(
        half_other,
        (shape(BPAD, VPAD), shape(2, 8, WIN, BPAD)),
        [pltpu.VMEM((VPAD, BPAD), F32)],
        x_other,
        amp,
    )
    back = call(
        early_blocks,
        shape(TWO, VPAD, dtype=F32),
        [
            pltpu.VMEM((3, VPAD, TWO), BF16),
            pltpu.VMEM((3, 2, BPAD, TWO), BF16),
            pltpu.VMEM((TWO, VPAD), F32),
            pltpu.SemaphoreType.DMA((3, 2)),
            pltpu.SemaphoreType.DMA((3,)),
            pltpu.SemaphoreType.DMA((2,)),
        ],
        info,
        half_0,
        half_1,
        x_all,
        z_here,
        z_after,
        z_before,
        in_specs=[SMEM] + [VMEM] * 2 + [HBM] * 4,
        out_specs=HBM,
    )
    back_rows, give = call(
        last_block,
        (shape(TWO, VPAD), shape(8 * WIN, VPAD)),
        [
            pltpu.VMEM((VPAD, TWO), BF16),
            pltpu.VMEM((TWO, VPAD), F32),
            pltpu.VMEM((8 * WIN, TWO), BF16),
            pltpu.SemaphoreType.DMA((2,)),
            pltpu.SemaphoreType.DMA,
        ],
        info,
        half_0,
        half_1,
        x_all,
        z_far,
        back,
        wins_0,
        wins_1,
        in_specs=[SMEM] + [VMEM] * 2 + [HBM] + [VMEM, HBM, VMEM, VMEM],
        out_specs=(VMEM, VMEM),
    )
    got = across(give)
    total, *pieces = call(
        chip_total,
        tuple([shape(WIN, VPAD, dtype=F32)] + [shape(WIN, VPAD)] * 7),
        [pltpu.VMEM((8 * WIN, TWO), BF16)],
        info,
        back_rows,
        wins_0,
        wins_1,
        got,
        in_specs=[SMEM] + [VMEM] * 4,
        out_specs=tuple([VMEM] * 8),
    )
    for j, piece in enumerate(pieces, start=1):
        dz, dx = j % 4, j // 4
        total = total + move(piece, lambda z, x, c, y: (z + dz, x + 2 * dx, c, y)).astype(F32)

    occ_count = occ_energy.shape[0]
    first_occ, second_occ = pair_orbitals(pair_index, occ_count)
    orbital_ids = jnp.arange(occ_count, dtype=jnp.int32)
    one_first = (orbital_ids[None, :] == first_occ[:, None]).astype(F32)
    one_second = (orbital_ids[None, :] == second_occ[:, None]).astype(F32)
    occ_sum = jnp.sum((one_first + one_second) * occ_energy[None, :], axis=1)
    share = VIRT * VIRT // 16
    first_row = grid_pos * BLK // 4
    vir_rows = lax.dynamic_slice_in_dim(jnp.pad(vir_energy, (0, VPAD - VIRT)), first_row, WIN, 0)
    out = total[:, :VIRT] / (vir_rows[:, None] + vir_energy[None, :] - occ_sum)
    first_cell = grid_pos * share - first_row * VIRT
    return lax.dynamic_slice_in_dim(out.reshape(1, WIN * VIRT), first_cell, share, 1)


def solution(mesh):
    placed = (
        P("pair", None, None),
        P(None, "grid"),
        P("grid", "pair"),
        P("grid", "pair"),
        P("pair"),
        P(),
        P(),
    )
    return jax.shard_map(
        local, mesh=mesh, in_specs=placed, out_specs=P("pair", "grid"), check_vma=False
    )
```

time: 197 us -> 163 us (0.83)
  waiting for transfers between devices: 82.5 us -> 54.8 us
  Pallas kernels: 70.8 us -> 54.3 us
  between operations: 2.89 us -> 16 us
    ppermute x21 -> x14, waiting for transfers between devices: 82.5 us -> 53.6 us  [move(): return lax.ppermute(block, BOTH, pairs)]
    pallas_call x9 -> x6, Pallas kernels: 70.8 us -> 54.3 us  [call(): pl.pallas_call(kernel, out_shape=out_shape, in_specs=in_specs or [VMEM] *...]
    ppermute x21 -> x14, starting transfers between devices: 26.5 us -> 24.8 us  [move(): return lax.ppermute(block, BOTH, pairs)]
  transfers between devices with their start and end apart: 21 -> 15, of which waited for: 11 -> 9; matrix products, arithmetic and copies ran while one was open for 3% -> 3% of each run, Pallas kernels for 26% -> 19%
where the time goes in v3:
time: 163 us; the launch traced here: 161 us
  waiting for transfers between devices  54.8 us (34%)
  Pallas kernels  54.3 us (33%)
  starting transfers between devices  24.8 us (15%)
  between operations  16 us (10%)
  local copies, waits for them, and re-layouts  6.75 us (4%)
  other arithmetic  4.5 us (3%)
    pallas_call x6, Pallas kernels, call(): pl.pallas_call(kernel, out_shape=out_shape, in_specs=in_specs or [VMEM] *...  54.3 us
    ppermute x14, waiting for transfers between devices, move(): return lax.ppermute(block, BOTH, pairs)  53.6 us
    ppermute x14, starting transfers between devices, move(): return lax.ppermute(block, BOTH, pairs)  24.8 us
  transfers between devices with their start and end apart: 15, of which 9 were waited for; matrix products, arithmetic and copies ran while one was open for 3% of the time, Pallas kernels for 19%

profile of v3, /device:TPU:0, one launch (start us, length us, event | category | flops | bytes accessed | tf_op | source)
XLA Modules:
  0.0 161.1 jit_solution(12828522578088122016)
XLA Ops:
  6.5 0.0 all-gather.3.cloned.1.call-start
  6.5 2.9 %shard_map.73 = (bf16[384,768]{1,0:T(8,128)(2,1)}, bf16[1536,384]{1,0:T(8,128)(2,1)}) custom-call(bf16[375,750]{1,0:T(8,128)(2,1)} %z_ref.1, f32[3,6]{1,0:T(4,128)} %s_ref.1, bf16[1500,375]{1,0:T(8,128)(2,1)} %x_ref.1), custom_call_target="tpu_custom_call" | custom-call | tf_op jit(solution)/shard_map/pallas_call | solution.py:61
  9.4 0.0 copy-start.5
  9.4 0.0 all-gather.3.cloned.1.call-update
  9.5 1.0 copy-done.5
  10.5 1.6 collective-permute-start
  12.1 0.7 collective-permute-start.1
  12.8 7.1 %shard_map.74 = (bf16[384,1536]{1,0:T(8,128)(2,1)}, bf16[2,8,96,384]{3,2,1,0:T(8,128)(2,1)}, bf16[1536,1536]{1,0:T(8,128)(2,1)}) custom-call(bf16[1536,384]{1,0:T(8,128)(2,1)} %get-tuple-element.29.x_ref, bf16[1,1500,1500]{2,1,0:T(8,128)(2,1)} %amp_ref.1), custom_call_target="tpu_custom_call" | custom-call | tf_op jit(solution)/shard_map/pallas_call | solution.py:61
  19.9 7.1 %collective-permute-done = bf16[384,768]{1,0:T(8,128)(2,1)S(1)} collective-permute-done((bf16[384,768]{1,0:T(8,128)(2,1)S(1)}, bf16[384,768]{1,0:T(8,128)(2,1)S(1)}, u32[]{:S(2)}, u32[]{:S(2)}) %collective-permute-start) | collective-permute-done | bytes 589856 | tf_op jit(solution)/shard_map/ppermute | solution.py:33
  26.9 0.0 collective-permute-done.1
  26.9 0.1 select_bitcast_fusion.1
  27.0 0.1 pad_maximum_fusion.refs_0_
  27.2 0.0 copy-start
  27.2 1.9 %collective-permute-start.3 = (bf16[2,384,768]{2,1,0:T(8,128)(2,1)S(1)}, bf16[2,384,768]{2,1,0:T(8,128)(2,1)S(1)}, u32[]{:S(2)}, u32[]{:S(2)}) collective-permute-start(bf16[2,384,768]{2,1,0:T(8,128)(2,1)S(1)} %pad_maximum_fusion.refs_0_), channel_id=1, source_target_pairs={{0,2},{2,4},{4,6},{6,0},{8,10},{10,12},{12,14},{14,8},{1,3},{3,5},... | collective-permute-start | bytes 3538952 | tf_op jit(solution)/shard_map/ppermute | solution.py:33
  29.0 1.5 collective-permute-start.4
  30.6 2.9 %collective-permute-start.2 = (bf16[1536,384]{1,0:T(8,128)(2,1)}, bf16[1536,384]{1,0:T(8,128)(2,1)}, u32[]{:S(2)}, u32[]{:S(2)}) collective-permute-start(bf16[1536,384]{1,0:T(8,128)(2,1)} %get-tuple-element.29.x_ref), channel_id=1, source_target_pairs={{0,17},{2,19},{4,21},{6,23},{8,25},{10,27},{12,29},{14,31},{1,16},... | collective-permute-start | bytes 3538952 | tf_op jit(solution)/shard_map/ppermute | solution.py:33
  33.5 22.1 %collective-permute-done.3.refs_2_ = bf16[2,384,768]{2,1,0:T(8,128)(2,1)S(1)} collective-permute-done((bf16[2,384,768]{2,1,0:T(8,128)(2,1)S(1)}, bf16[2,384,768]{2,1,0:T(8,128)(2,1)S(1)}, u32[]{:S(2)}, u32[]{:S(2)}) %collective-permute-start.3) | collective-permute-done | bytes 1179680 | tf_op jit(solution)/shard_map/ppermute | solution.py:33
  55.6 0.0 copy-start.1
  55.6 0.0 collective-permute-done.4.refs_1_
  55.6 0.0 copy-start.2
  55.6 1.3 broadcast_select_fusion
  56.9 0.0 copy-done
  56.9 0.2 copy-done.1
  57.1 0.3 copy-done.2
  57.4 1.3 collective-permute-start.5
  58.7 0.7 stack.67.info
  59.4 0.0 collective-permute-done.2.x_ref
  59.4 5.8 %shard_map.75 = (bf16[384,1536]{1,0:T(8,128)(2,1)}, bf16[2,8,96,384]{3,2,1,0:T(8,128)(2,1)}) custom-call(bf16[1536,384]{1,0:T(8,128)(2,1)} %collective-permute-done.2.x_ref, bf16[1536,1536]{1,0:T(8,128)(2,1)} %get-tuple-element.30.t_ref), custom_call_target="tpu_custom_call" | custom-call | tf_op jit(solution)/shard_map/pallas_call | solution.py:61
  65.2 1.2 all-gather.3.cloned.1.call-done
  66.4 17.9 %shard_map.76.back_in = f32[768,1536]{1,0:T(8,128)} custom-call(s32[16]{0:T(128)} %stack.67.info, bf16[384,1536]{1,0:T(8,128)(2,1)} %get-tuple-element.28.h0_ref, bf16[384,1536]{1,0:T(8,128)(2,1)} %get-tuple-element.31.h1_ref, bf16[8,1536,384]{2,1,0:T(8,128)(2,1)} %bitcast.22, bf16[2,384,768]{2,1,0:T(8,128)(2,1)} %copy-done, bf16[2,384,768]{2,1,0:T(8,128)(2,1)} %copy-done.2, ...), custom_call_target="tpu_custom_call" | custom-call | tf_op jit(solution)/shard_map/pallas_call | solution.py:61
  84.4 0.0 collective-permute-done.5.z_ref
  84.4 14.1 %shard_map.77 = (bf16[768,1536]{1,0:T(8,128)(2,1)}, bf16[768,1536]{1,0:T(8,128)(2,1)}) custom-call(s32[16]{0:T(128)} %stack.67.info, bf16[384,1536]{1,0:T(8,128)(2,1)} %get-tuple-element.28.h0_ref, bf16[384,1536]{1,0:T(8,128)(2,1)} %get-tuple-element.31.h1_ref, bf16[8,1536,384]{2,1,0:T(8,128)(2,1)} %bitcast.23, ...), custom_call_target="tpu_custom_call" | custom-call | tf_op jit(solution)/shard_map/pallas_call | solution.py:61
  98.5 0.3 collective-permute-start.6
  98.8 4.5 %collective-permute-done.6.got_ref = bf16[768,1536]{1,0:T(8,128)(2,1)S(1)} collective-permute-done((bf16[768,1536]{1,0:T(8,128)(2,1)}, bf16[768,1536]{1,0:T(8,128)(2,1)S(1)}, u32[]{:S(2)}, u32[]{:S(2)}) %collective-permute-start.6) | collective-permute-done | bytes 2359328 | tf_op jit(solution)/shard_map/ppermute | solution.py:33
  103.3 0.0 copy-start.3
  103.3 1.4 copy-done.3
  104.8 0.0 copy-start.6
  104.8 0.0 copy-start.7
  104.8 6.5 %shard_map.78 = (f32[96,1536]{1,0:T(8,128)}, bf16[96,1536]{1,0:T(8,128)(2,1)}, bf16[96,1536]{1,0:T(8,128)(2,1)}, bf16[96,1536]{1,0:T(8,128)(2,1)}, bf16[96,1536]...) custom-call(s32[16]{0:T(128)} %stack.67.info, ...), custom_call_target="tpu_custom_call" | custom-call | tf_op jit(solution)/shard_map/pallas_call | solution.py:61
  111.3 0.0 copy-start.4
  111.3 2.7 %collective-permute-start.8 = (bf16[96,1536]{1,0:T(8,128)(2,1)}, bf16[96,1536]{1,0:T(8,128)(2,1)S(1)}, u32[]{:S(2)}, u32[]{:S(2)}) collective-permute-start(bf16[96,1536]{1,0:T(8,128)(2,1)} %get-tuple-element.39), channel_id=1, source_target_pairs={{0,64},{2,66},{4,68},{6,70},{8,72},{10,74},{12,76},{14,78},{1,65},... | collective-permute-start | bytes 884744 | tf_op jit(solution)/shard_map/ppermute | solution.py:33
  113.9 1.0 collective-permute-start.7
  115.6 0.6 fusion.6
  118.0 0.0 copy-done.6
  118.0 0.1 pad_dynamic-slice_fusion
  118.1 0.0 copy-done.7
  118.1 1.3 fusion.9
  119.3 4.2 %collective-permute-start.10 = (bf16[96,1536]{1,0:T(8,128)(2,1)}, bf16[96,1536]{1,0:T(8,128)(2,1)S(1)}, u32[]{:S(2)}, u32[]{:S(2)}) collective-permute-start(bf16[96,1536]{1,0:T(8,128)(2,1)} %get-tuple-element.41), channel_id=1, source_target_pairs={{0,16},{2,18},{4,20},{6,22},{8,24},{10,26},{12,28},{14,30},{1,17},... | collective-permute-start | bytes 884744 | tf_op jit(solution)/shard_map/ppermute | solution.py:33
  123.6 0.0 collective-permute-start.11
  123.6 6.0 %collective-permute-start.12 = (bf16[96,1536]{1,0:T(8,128)(2,1)}, bf16[96,1536]{1,0:T(8,128)(2,1)S(1)}, u32[]{:S(2)}, u32[]{:S(2)}) collective-permute-start(bf16[96,1536]{1,0:T(8,128)(2,1)} %get-tuple-element.43), channel_id=1, source_target_pairs={{0,80},{2,82},{4,84},{6,86},{8,88},{10,90},{12,92},{14,94},{1,81},... | collective-permute-start | bytes 884744 | tf_op jit(solution)/shard_map/ppermute | solution.py:33
  129.6 0.0 collective-permute-done.8
  129.6 0.0 collective-permute-start.13
  129.7 0.0 collective-permute-done.7
  129.7 0.6 collective-permute-start.9
  130.3 0.0 copy-done.4
  130.3 0.1 convert_add_fusion
  130.4 1.3 collective-permute-done.10
  131.6 8.8 %collective-permute-done.11 = bf16[96,1536]{1,0:T(8,128)(2,1)S(1)} collective-permute-done((bf16[96,1536]{1,0:T(8,128)(2,1)}, bf16[96,1536]{1,0:T(8,128)(2,1)S(1)}, u32[]{:S(2)}, u32[]{:S(2)}) %collective-permute-start.11) | collective-permute-done | bytes 294944 | tf_op jit(solution)/shard_map/ppermute | solution.py:33
  140.4 5.4 %collective-permute-done.12 = bf16[96,1536]{1,0:T(8,128)(2,1)S(1)} collective-permute-done((bf16[96,1536]{1,0:T(8,128)(2,1)}, bf16[96,1536]{1,0:T(8,128)(2,1)S(1)}, u32[]{:S(2)}, u32[]{:S(2)}) %collective-permute-start.12) | collective-permute-done | bytes 294944 | tf_op jit(solution)/shard_map/ppermute | solution.py:33
  145.8 3.5 %collective-permute-done.13 = bf16[96,1536]{1,0:T(8,128)(2,1)S(1)} collective-permute-done((bf16[96,1536]{1,0:T(8,128)(2,1)}, bf16[96,1536]{1,0:T(8,128)(2,1)S(1)}, u32[]{:S(2)}, u32[]{:S(2)}) %collective-permute-start.13) | collective-permute-done | bytes 294944 | tf_op jit(solution)/shard_map/ppermute | solution.py:33
  149.3 0.9 collective-permute-done.9
  150.2 1.0 fusion.5
  151.2 1.0 reshape.34
  152.2 2.0 %constant_dynamic-slice_fusion = f32[1,140625]{1,0:T(1,128)} fusion(f32[1,144000]{1,0:T(1,128)S(1)} %reshape.34, s32[]{:T(128)S(6)} %select_n.151), kind=kLoop, calls=%fused_computation.25 | loop fusion | bytes 1125004 | tf_op jit(solution)/shard_map/dynamic_slice | solution.py:317
  (1 shorter events, 0.0 us)
Async XLA Ops:
  6.5 59.9 %all-gather.3.cloned.1.call-start = ((), (), s32[]{:S(2)}) async-start(), calls=%async_computation | async-start | bytes 10616832 | tf_op jit(solution)/shard_map/all_gather | solution.py:224
  9.4 1.1 copy-start.5
  10.5 16.4 %collective-permute-start = (bf16[384,768]{1,0:T(8,128)(2,1)S(1)}, bf16[384,768]{1,0:T(8,128)(2,1)S(1)}, u32[]{:S(2)}, u32[]{:S(2)}) collective-permute-start(bf16[384,768]{1,0:T(8,128)(2,1)S(1)} %copy-done.5), channel_id=1, source_target_pairs={{0,1},{2,3},{4,5},{6,7},{8,9},{10,11},{12,13},{14,15},{1,17},{3,19... | collective-permute-start | bytes 1769480 | tf_op jit(solution)/shard_map/ppermute | solution.py:33
  12.1 14.9 %collective-permute-start.1 = (bf16[384,768]{1,0:T(8,128)(2,1)S(1)}, bf16[384,768]{1,0:T(8,128)(2,1)S(1)}, u32[]{:S(2)}, u32[]{:S(2)}) collective-permute-start(bf16[384,768]{1,0:T(8,128)(2,1)S(1)} %copy-done.5), channel_id=1, source_target_pairs={{1,16},{3,18},{5,20},{7,22},{9,24},{11,26},{13,28},{15,30},{16,1},... | collective-permute-start | bytes 1769480 | tf_op jit(solution)/shard_map/ppermute | solution.py:33
  27.2 29.7 %copy-start = (bf16[2,384,768]{2,1,0:T(8,128)(2,1)}, bf16[2,384,768]{2,1,0:T(8,128)(2,1)S(1)}, u32[]{:S(2)}) copy-start(bf16[2,384,768]{2,1,0:T(8,128)(2,1)S(1)} %pad_maximum_fusion.refs_0_) | copy-start | bytes 3538948
  27.2 28.4 %collective-permute-start.3 = (bf16[2,384,768]{2,1,0:T(8,128)(2,1)S(1)}, bf16[2,384,768]{2,1,0:T(8,128)(2,1)S(1)}, u32[]{:S(2)}, u32[]{:S(2)}) collective-permute-start(bf16[2,384,768]{2,1,0:T(8,128)(2,1)S(1)} %pad_maximum_fusion.refs_0_), channel_id=1, source_target_pairs={{0,2},{2,4},{4,6},{6,0},{8,10},{10,12},{12,14},{14,8},{1,3},{3,5},... | collective-permute-start | bytes 3538952 | tf_op jit(solution)/shard_map/ppermute | solution.py:33
  29.0 26.6 %collective-permute-start.4 = (bf16[2,384,768]{2,1,0:T(8,128)(2,1)S(1)}, bf16[2,384,768]{2,1,0:T(8,128)(2,1)S(1)}, u32[]{:S(2)}, u32[]{:S(2)}) collective-permute-start(bf16[2,384,768]{2,1,0:T(8,128)(2,1)S(1)} %pad_maximum_fusion.refs_0_), channel_id=1, source_target_pairs={{0,6},{2,0},{4,2},{6,4},{8,14},{10,8},{12,10},{14,12},{1,7},{3,1},... | collective-permute-start | bytes 3538952 | tf_op jit(solution)/shard_map/ppermute | solution.py:33
  30.6 28.8 %collective-permute-start.2 = (bf16[1536,384]{1,0:T(8,128)(2,1)}, bf16[1536,384]{1,0:T(8,128)(2,1)}, u32[]{:S(2)}, u32[]{:S(2)}) collective-permute-start(bf16[1536,384]{1,0:T(8,128)(2,1)} %get-tuple-element.29.x_ref), channel_id=1, source_target_pairs={{0,17},{2,19},{4,21},{6,23},{8,25},{10,27},{12,29},{14,31},{1,16},... | collective-permute-start | bytes 3538952 | tf_op jit(solution)/shard_map/ppermute | solution.py:33
  55.6 1.5 copy-start.1
  55.6 1.8 %copy-start.2 = (bf16[2,384,768]{2,1,0:T(8,128)(2,1)}, bf16[2,384,768]{2,1,0:T(8,128)(2,1)S(1)}, u32[]{:S(2)}) copy-start(bf16[2,384,768]{2,1,0:T(8,128)(2,1)S(1)} %collective-permute-done.4.refs_1_) | copy-start | bytes 3538948
  57.4 27.0 %collective-permute-start.5 = (bf16[2,384,768]{2,1,0:T(8,128)(2,1)}, bf16[2,384,768]{2,1,0:T(8,128)(2,1)}, u32[]{:S(2)}, u32[]{:S(2)}) collective-permute-start(bf16[2,384,768]{2,1,0:T(8,128)(2,1)} %broadcast_select_fusion), channel_id=1, source_target_pairs={{0,2},{2,4},{4,6},{6,0},{8,14},{10,8},{12,10},{14,12},{1,3},{3,5},... | collective-permute-start | bytes 3538952 | tf_op jit(solution)/shard_map/ppermute | solution.py:33
  98.5 4.8 %collective-permute-start.6 = (bf16[768,1536]{1,0:T(8,128)(2,1)}, bf16[768,1536]{1,0:T(8,128)(2,1)S(1)}, u32[]{:S(2)}, u32[]{:S(2)}) collective-permute-start(bf16[768,1536]{1,0:T(8,128)(2,1)} %get-tuple-element.36), channel_id=1, source_target_pairs={{0,8},{2,10},{4,12},{6,14},{8,0},{10,2},{12,4},{14,6},{1,9},{3,11}... | collective-permute-start | bytes 7077896 | tf_op jit(solution)/shard_map/ppermute | solution.py:33
  103.3 1.4 copy-start.3
  104.8 13.2 %copy-start.6 = (f32[1500]{0:T(1024)S(1)}, f32[1500]{0:T(1024)}, u32[]{:S(2)}) copy-start(f32[1500]{0:T(1024)} %param.12) | copy-start | bytes 18004
  104.8 13.3 %copy-start.7 = (f32[150]{0:T(256)S(1)}, f32[150]{0:T(256)}, u32[]{:S(2)}) copy-start(f32[150]{0:T(256)} %param.13) | copy-start | bytes 1804
  111.3 19.1 %copy-start.4 = (f32[96,1536]{1,0:T(8,128)S(1)}, f32[96,1536]{1,0:T(8,128)}, u32[]{:S(2)}) copy-start(f32[96,1536]{1,0:T(8,128)} %get-tuple-element.37) | copy-start | bytes 1769476
  111.3 18.4 %collective-permute-start.8 = (bf16[96,1536]{1,0:T(8,128)(2,1)}, bf16[96,1536]{1,0:T(8,128)(2,1)S(1)}, u32[]{:S(2)}, u32[]{:S(2)}) collective-permute-start(bf16[96,1536]{1,0:T(8,128)(2,1)} %get-tuple-element.39), channel_id=1, source_target_pairs={{0,64},{2,66},{4,68},{6,70},{8,72},{10,74},{12,76},{14,78},{1,65},... | collective-permute-start | bytes 884744 | tf_op jit(solution)/shard_map/ppermute | solution.py:33
  113.9 15.7 %collective-permute-start.7 = (bf16[96,1536]{1,0:T(8,128)(2,1)}, bf16[96,1536]{1,0:T(8,128)(2,1)S(1)}, u32[]{:S(2)}, u32[]{:S(2)}) collective-permute-start(bf16[96,1536]{1,0:T(8,128)(2,1)} %get-tuple-element.38), channel_id=1, source_target_pairs={{0,32},{2,34},{4,36},{6,38},{8,40},{10,42},{12,44},{14,46},{1,33},... | collective-permute-start | bytes 884744 | tf_op jit(solution)/shard_map/ppermute | solution.py:33
  119.3 12.3 %collective-permute-start.10 = (bf16[96,1536]{1,0:T(8,128)(2,1)}, bf16[96,1536]{1,0:T(8,128)(2,1)S(1)}, u32[]{:S(2)}, u32[]{:S(2)}) collective-permute-start(bf16[96,1536]{1,0:T(8,128)(2,1)} %get-tuple-element.41), channel_id=1, source_target_pairs={{0,16},{2,18},{4,20},{6,22},{8,24},{10,26},{12,28},{14,30},{1,17},... | collective-permute-start | bytes 884744 | tf_op jit(solution)/shard_map/ppermute | solution.py:33
  123.6 16.9 %collective-permute-start.11 = (bf16[96,1536]{1,0:T(8,128)(2,1)}, bf16[96,1536]{1,0:T(8,128)(2,1)S(1)}, u32[]{:S(2)}, u32[]{:S(2)}) collective-permute-start(bf16[96,1536]{1,0:T(8,128)(2,1)} %get-tuple-element.42), channel_id=1, source_target_pairs={{0,48},{2,50},{4,52},{6,54},{8,56},{10,58},{12,60},{14,62},{1,49},... | collective-permute-start | bytes 884744 | tf_op jit(solution)/shard_map/ppermute | solution.py:33
  123.6 22.2 %collective-permute-start.12 = (bf16[96,1536]{1,0:T(8,128)(2,1)}, bf16[96,1536]{1,0:T(8,128)(2,1)S(1)}, u32[]{:S(2)}, u32[]{:S(2)}) collective-permute-start(bf16[96,1536]{1,0:T(8,128)(2,1)} %get-tuple-element.43), channel_id=1, source_target_pairs={{0,80},{2,82},{4,84},{6,86},{8,88},{10,90},{12,92},{14,94},{1,81},... | collective-permute-start | bytes 884744 | tf_op jit(solution)/shard_map/ppermute | solution.py:33
  129.6 19.7 %collective-permute-start.13 = (bf16[96,1536]{1,0:T(8,128)(2,1)}, bf16[96,1536]{1,0:T(8,128)(2,1)S(1)}, u32[]{:S(2)}, u32[]{:S(2)}) collective-permute-start(bf16[96,1536]{1,0:T(8,128)(2,1)} %get-tuple-element.44), channel_id=1, source_target_pairs={{0,112},{2,114},{4,116},{6,118},{8,120},{10,122},{12,124},{14,126}... | collective-permute-start | bytes 884744 | tf_op jit(solution)/shard_map/ppermute | solution.py:33
  129.7 20.6 %collective-permute-start.9 = (bf16[96,1536]{1,0:T(8,128)(2,1)}, bf16[96,1536]{1,0:T(8,128)(2,1)S(1)}, u32[]{:S(2)}, u32[]{:S(2)}) collective-permute-start(bf16[96,1536]{1,0:T(8,128)(2,1)} %get-tuple-element.40), channel_id=1, source_target_pairs={{0,96},{2,98},{4,100},{6,102},{8,104},{10,106},{12,108},{14,110},{... | collective-permute-start | bytes 884744 | tf_op jit(solution)/shard_map/ppermute | solution.py:33
Sparse Core Ops, SparseCore 0:
  9.6 56.7 all-gather.2

commit v4 on v0

v4 whole, which is shorter than its diff:
```python
import itertools

import jax
import jax.numpy as jnp
from jax import lax
from jax.experimental import pallas as pl
from jax.experimental.pallas import tpu as pltpu
from jax.sharding import PartitionSpec as P

VIRT = 1500
ZBLK = 125
BLK = 375
BPAD = 384
TWO = 2 * BPAD
VPAD = 1536
WIN = 96
BOTH = ("grid", "pair")
ALL = list(itertools.product(range(4), range(4), range(2), range(4)))
F32 = jnp.float32
BF16 = jnp.bfloat16


def flat_index(z, x, c, y):
    return ((z % 4) * 4 + (x % 4) // 2 * 2 + c % 2) * 8 + (y % 4) * 2 + (x % 4) % 2


def move(block, target):
    pairs = []
    for z, x, c, y in ALL:
        dest = target(z, x, c, y)
        if dest is not None:
            pairs.append((flat_index(z, x, c, y), flat_index(*dest)))
    return lax.ppermute(block, BOTH, pairs)


def across(block):
    return move(block, lambda z, x, c, y: (z, x, 1 - c, y))


def pair_orbitals(packed, occ_count):
    row_ids = jnp.arange(1, occ_count, dtype=jnp.int32)
    starts = row_ids * (2 * occ_count - row_ids - 1) // 2
    first_occ = jnp.sum((starts[None, :] <= packed[:, None]).astype(jnp.int32), axis=1)
    second = packed - first_occ * (2 * occ_count - first_occ - 1) // 2 + first_occ + 1
    return (first_occ, second)


def dot(a, b, contract_a, contract_b):
    return lax.dot_general(
        a, b, (((contract_a,), (contract_b,)), ((), ())), preferred_element_type=F32
    )


VMEM = pl.BlockSpec(memory_space=pltpu.VMEM)
SMEM = pl.BlockSpec(memory_space=pltpu.SMEM)
HBM = pl.BlockSpec(memory_space=pl.ANY)


def call(kernel, out_shape, scratch, *args, in_specs=None, out_specs=None, mib=20):
    many = isinstance(out_shape, (tuple, list))
    return pl.pallas_call(
        kernel,
        out_shape=out_shape,
        in_specs=in_specs or [VMEM] * len(args),
        out_specs=out_specs or (tuple([VMEM] * len(out_shape)) if many else VMEM),
        scratch_shapes=scratch,
        compiler_params=pltpu.CompilerParams(vmem_limit_bytes=mib * 2**20),
    )(*args)


def pad_metric(z_hbm, s_ref, z_out, tmp, z_ref, sem):
    load = pltpu.make_async_copy(z_hbm, z_ref, sem)
    load.start()
    tmp[...] = jnp.zeros_like(tmp)
    load.wait()
    z = z_ref[...].astype(F32)
    tmp[:BLK, :BLK] = z[:, :BLK]
    tmp[:BLK, BPAD : BPAD + BLK] = z[:, BLK:]
    lane = lax.broadcasted_iota(jnp.int32, (1, TWO), 1)
    for r in range(3):
        row = jnp.zeros((1, TWO), F32)
        for q in range(6):
            start = (q // 3) * BPAD + (q % 3) * ZBLK
            row = jnp.where((lane >= start) & (lane < start + ZBLK), s_ref[r, q], row)
        for part in range(3):
            piece = row.astype(BF16).astype(F32)
            tmp[BLK + 3 * part + r : BLK + 3 * part + r + 1, :] = piece
            row = row - piece
    z_out[...] = tmp[...].astype(BF16)


def pad_factors(own_ref, pair_ref, both_out, own_out):
    both_out[...] = jnp.zeros_like(both_out)
    both_out[0, :VIRT, :BLK] = own_ref[...]
    both_out[1, :VIRT, :BLK] = pair_ref[...]
    own_out[...] = jnp.zeros_like(own_out)
    own_out[:VIRT, :BLK] = own_ref[...]


def scaled(block):
    z = block.astype(F32)
    tail = z[BPAD - 16 :, :]
    parts = [tail[7 + r : 8 + r] + tail[10 + r : 11 + r] + tail[13 + r : 14 + r] for r in range(3)]
    row = lax.broadcasted_iota(jnp.int32, (BPAD, 1), 0)
    scale = jnp.where(row < ZBLK, parts[0], jnp.where(row < 2 * ZBLK, parts[1], parts[2]))
    return jnp.where(row < BLK, z * scale, 0.0)


def half(info, x_ref, amp_ref, h_ref, w_ref, xf):
    if x_ref.shape != xf.shape:
        xf[...] = jnp.zeros_like(xf)
    xf[: x_ref.shape[0], : x_ref.shape[1]] = x_ref[...].astype(F32)
    for c in range(2):
        for chip in range(8):
            start = (chip * 2 + c) * BLK // 4
            w_ref[info[2 + c], info[8 + chip]] = xf[start : start + WIN, :].astype(BF16)
    h_ref[...] = jnp.zeros_like(h_ref)
    h_ref[:, :VIRT] = dot(xf[...].T.astype(BF16)[:, :VIRT], amp_ref[0], 1, 0).astype(BF16)


def copy_whole(in_ref, o_ref):
    o_ref[...] = in_ref[...]


def choose_rows(info, own_ref, a_ref, b_ref, o_ref):
    @pl.when(info[1] == 1)
    def _():
        o_ref[0] = own_ref[...]
        o_ref[1] = a_ref[...]

    @pl.when(info[1] == 0)
    def _():
        o_ref[0] = a_ref[...]
        o_ref[1] = b_ref[...]


def choose_onward(info, first_ref, second_ref, o_ref):
    @pl.when(info[0] == 0)
    def _():
        o_ref[...] = first_ref[...]

    @pl.when(info[0] == 1)
    def _():
        o_ref[...] = second_ref[...]


class Factors:
    def __init__(self, info, step, x_refs, slot, first_col, sems):
        own, near, swapped, far, far_pair = x_refs
        self.info, self.step, self.sems = info, step, sems
        self.slot, self.first_col = slot, first_col
        self.sources = {
            (0, 0): (own.at[0], own.at[1]),
            (0, 1): (own.at[1], own.at[0]),
            (1, 0): (swapped.at[1], swapped.at[0]),
            (1, 1): (near.at[1], near.at[0]),
            (2, 0): (far, far_pair),
            (2, 1): (far_pair, far),
            (3, 0): (near.at[0], near.at[1]),
            (3, 1): (swapped.at[0], swapped.at[1]),
        }

    def copy(self, ref, side):
        to = self.slot.at[:, pl.ds(self.first_col + side * BPAD, BPAD)]
        return pltpu.make_async_copy(ref, to, self.sems.at[side])

    def start(self):
        for (place, core), refs in self.sources.items():

            @pl.when((self.info[4 + self.step] == place) & (self.info[0] == core))
            def _():
                for side in range(2):
                    self.copy(refs[side], side).start()

    def wait(self):
        for side in range(2):
            self.copy(self.sources[2, 0][side], side).wait()


def weigh(h_ref, x, z):
    return (dot(h_ref[...], x, 1, 0) * scaled(z)).astype(BF16)


def weigh_early(info, h0_ref, h1_ref, *refs):
    x_refs, z_refs, w_out, x_out = refs[:5], refs[5:8], refs[8], refs[9]
    zs, xsem, zsem = refs[10:]
    loads = []
    for i in range(3):
        loads.append(Factors(info, i, x_refs, x_out, i * TWO, xsem.at[i]))
        loads.append(pltpu.make_async_copy(z_refs[i], zs.at[i], zsem.at[i]))
        loads[-2].start()
        loads[-1].start()
    for i in range(3):
        loads[2 * i].wait()
        loads[2 * i + 1].wait()
        cols = slice(i * TWO, i * TWO + TWO)
        for b, h_ref in enumerate((h0_ref, h1_ref)):
            w_out[b * BPAD : b * BPAD + BPAD, cols] = weigh(h_ref, x_out[:, cols], zs[i, b])


def window_loads(side, w0_ref, w1_ref, left, sems):
    loads = [
        pltpu.make_async_copy(w_ref.at[side], left.at[:, :, pl.ds(b * BPAD, BPAD)], sems.at[b])
        for b, w_ref in enumerate((w0_ref, w1_ref))
    ]
    for load in loads:
        load.start()
    return loads


def give_half(left_loads, left, back, give_ref):
    for load in left_loads:
        load.wait()
    give_ref[...] = dot(left[...].reshape(8 * WIN, TWO), back, 1, 0).astype(BF16)


def back_half(rows, w_ref, newest_ref, x_ref, xn_ref):
    part = dot(w_ref[...], x_ref[rows, :], 1, 1) + dot(newest_ref[...], xn_ref[rows, :], 1, 1)
    return part.astype(BF16)


def last_block(info, h0_ref, h1_ref, *refs):
    x_refs, z_ref, w_ref, x_ref, w0_ref, w1_ref = refs[:5], *refs[5:10]
    w_out, xn_out, back_out, give_ref, left, xsem, vsem = refs[10:]
    newest = Factors(info, 3, x_refs, xn_out, 0, xsem)
    newest.start()
    left_loads = window_loads(0, w0_ref, w1_ref, left, vsem)
    newest.wait()
    for b, h_ref in enumerate((h0_ref, h1_ref)):
        w_out[b * BPAD : b * BPAD + BPAD, :] = weigh(h_ref, xn_out[...], z_ref[b])
    back_out[...] = back_half(slice(0, TWO), w_ref, w_out, x_ref, xn_out)
    give_half(left_loads, left, back_out[...], give_ref)


def second_half(w_ref, newest_ref, x_ref, xn_ref, w0_ref, w1_ref, back_out, give_ref, left, vsem):
    left_loads = window_loads(0, w0_ref, w1_ref, left, vsem)
    back_out[...] = back_half(slice(TWO, VPAD), w_ref, newest_ref, x_ref, xn_ref)
    give_half(left_loads, left, back_out[...], give_ref)


def keep_sum(back_ref, w0_ref, w1_ref, got_ref, left, vsem):
    for load in window_loads(1, w0_ref, w1_ref, left, vsem):
        load.wait()
    return dot(left[...].reshape(8 * WIN, TWO), back_ref[...], 1, 0) + got_ref[...].astype(F32)


def keep_x(back_ref, w0_ref, w1_ref, got_ref, own_ref, send_ref, left, vsem):
    total = keep_sum(back_ref, w0_ref, w1_ref, got_ref, left, vsem)
    own_ref[...] = total[: 4 * WIN]
    send_ref[...] = total[4 * WIN :].astype(BF16)


def keep_z(back_ref, w0_ref, w1_ref, got_ref, own_ref, *refs):
    send_refs, left, vsem = refs[:3], refs[3], refs[4]
    total = keep_sum(back_ref, w0_ref, w1_ref, got_ref, left, vsem)
    for dx in range(2):
        for dz in range(4):
            part = total[(4 * dx + dz) * WIN : (4 * dx + dz + 1) * WIN]
            if dz == 0:
                own_ref[dx] = part
            else:
                send_refs[dz - 1][dx] = part.astype(BF16)


def then_z(own_ref, got_ref, out_ref, *send_refs):
    total = own_ref[...] + got_ref[...].astype(F32)
    out_ref[...] = total[:WIN]
    for dz in range(1, 4):
        send_refs[dz - 1][...] = total[dz * WIN : (dz + 1) * WIN].astype(BF16)


def then_x(own_ref, got_1, got_2, got_3, out_ref, send_ref):
    total = own_ref[...] + got_1[...].astype(F32) + got_2[...].astype(F32) + got_3[...].astype(F32)
    out_ref[...] = total[0]
    send_ref[...] = total[1].astype(BF16)


def shape(*dims, dtype=BF16):
    return jax.ShapeDtypeStruct(dims, dtype)


def local(amplitudes, factors, z_values, z_scales, pair_index, vir_energy, occ_energy):
    grid_pos = lax.axis_index("grid")
    pair_pos = lax.axis_index("pair")
    z_pos = grid_pos // 4
    x_hi = (grid_pos // 2) % 2
    core = grid_pos % 2
    y_pos = pair_pos // 2
    x_pos = 2 * x_hi + pair_pos % 2
    outer = (x_pos == 0) | (x_pos == 3)
    order = [(y_pos + i - z_pos) % 4 for i in (0, 1, 3, 2)]
    places = [(chip // 2 - z_pos) % 4 + 4 * ((chip % 2 - x_hi) % 2) for chip in range(8)]
    info = jnp.stack([core, outer.astype(jnp.int32), 1 - core, core] + order + places).astype(jnp.int32)

    theirs = across(factors)
    z_own = call(
        pad_metric,
        shape(BPAD, TWO),
        [
            pltpu.VMEM((BPAD, TWO), F32),
            pltpu.VMEM((BLK, 2 * BLK), BF16),
            pltpu.SemaphoreType.DMA,
        ],
        z_values,
        z_scales,
        in_specs=[HBM, SMEM],
        mib=60,
    )
    hop_a = {0: 1, 3: 2, 2: 0, 1: 3}
    hop_b = {2: 1, 1: 2}
    recv_a = move(z_own, lambda z, x, c, y: (z, hop_a[x], c, y))
    recv_b = move(z_own, lambda z, x, c, y: (z, hop_b[x], c, y) if x in hop_b else None)
    theirs, z_own = lax.optimization_barrier((theirs, z_own))
    x_pair, x_own = call(
        pad_factors, (shape(2, VPAD, BPAD), shape(VPAD, BPAD)), [], factors, theirs
    )

    def halves_of(block, amp):
        return call(
            half,
            (shape(BPAD, VPAD), shape(2, 8, WIN, BPAD)),
            [pltpu.VMEM((VPAD, BPAD), F32)],
            info,
            block,
            amp,
            in_specs=[SMEM, VMEM, VMEM],
        )

    half_0, wins_0 = halves_of(x_own, amplitudes)
    onward = lambda z, x, c, y: (z + 1 - 2 * c, x, c, y)
    near = move(x_pair, onward)
    recv_a, recv_b, half_0, x_again, pair_index = lax.optimization_barrier(
        (recv_a, recv_b, half_0, x_own, pair_index)
    )
    x_other = move(x_again, lambda z, x, c, y: (z, 3 - x, c, y))
    z_here = call(
        choose_rows,
        shape(2, BPAD, TWO),
        [],
        info,
        z_own,
        recv_a,
        recv_b,
        in_specs=[SMEM] + [VMEM] * 3,
    )
    z_before = move(z_here, lambda z, x, c, y: (z, x, c, y + 1))
    z_after = move(z_here, lambda z, x, c, y: (z, x, c, y - 1))
    occ_count = occ_energy.shape[0]
    first_occ, second_occ = pair_orbitals(pair_index, occ_count)
    orbital_ids = jnp.arange(occ_count, dtype=jnp.int32)
    one_first = (orbital_ids[None, :] == first_occ[:, None]).astype(F32)
    one_second = (orbital_ids[None, :] == second_occ[:, None]).astype(F32)
    occ_sum = jnp.sum((one_first + one_second) * occ_energy[None, :], axis=1)
    share = VIRT * VIRT // 16
    first_row = grid_pos * BLK // 4
    vir_rows = lax.dynamic_slice_in_dim(jnp.pad(vir_energy, (0, VPAD - VIRT)), first_row, WIN, 0)
    gaps = vir_rows[:, None] + vir_energy[None, :] - occ_sum
    far = move(near[0], onward)
    amp_later, near = lax.optimization_barrier((amplitudes, near))
    amp_again = call(copy_whole, shape(1, VIRT, VIRT), [], amp_later)
    z_before, z_after, near, far, x_other, gaps, amp_again = lax.optimization_barrier(
        (z_before, z_after, near, far, x_other, gaps, amp_again)
    )
    x_parts = [x_pair, near, across(near), far, across(far)]
    z_onward = call(
        choose_onward,
        shape(2, BPAD, TWO),
        [],
        info,
        z_before,
        z_after,
        in_specs=[SMEM] + [VMEM] * 2,
    )
    z_far = move(z_onward, lambda z, x, c, y: (z, x, c, y + 1 - 2 * c))
    half_1, wins_1 = halves_of(x_other, amp_again)
    dma = pltpu.SemaphoreType.DMA
    early, x_early = call(
        weigh_early,
        (shape(TWO, 3 * TWO), shape(VPAD, 3 * TWO)),
        [pltpu.VMEM((3, 2, BPAD, TWO), BF16), dma((3, 2)), dma((3,))],
        info,
        half_0,
        half_1,
        *x_parts,
        z_here,
        z_after,
        z_before,
        in_specs=[SMEM] + [VMEM] * 2 + [HBM] * 8,
    )
    left = pltpu.VMEM((8, WIN, TWO), BF16)
    half_shape = shape(TWO, TWO)
    newest, x_newest, back_a, give_a = call(
        last_block,
        (half_shape, shape(VPAD, TWO), half_shape, half_shape),
        [left, dma((2,)), dma((2,))],
        info,
        half_0,
        half_1,
        *x_parts,
        z_far,
        early,
        x_early,
        wins_0,
        wins_1,
        in_specs=[SMEM] + [VMEM] * 2 + [HBM] * 5 + [VMEM] * 3 + [HBM] * 2,
    )
    got_a = across(give_a)
    back_b, give_b = call(
        second_half,
        (half_shape, half_shape),
        [left, dma((2,))],
        early,
        newest,
        x_early,
        x_newest,
        wins_0,
        wins_1,
        in_specs=[VMEM] * 4 + [HBM] * 2,
    )
    got_b = across(give_b)

    to_z = [None] + [(lambda dz: lambda z, x, c, y: (z + dz, x, c, y))(dz) for dz in range(1, 4)]
    to_x = lambda z, x, c, y: (z, x + 2, c, y)
    own_a, send_a = call(
        keep_x,
        (shape(4 * WIN, TWO, dtype=F32), shape(4 * WIN, TWO)),
        [left, dma((2,))],
        back_a,
        wins_0,
        wins_1,
        got_a,
        in_specs=[VMEM, HBM, HBM, VMEM],
    )
    from_x = move(send_a, to_x)
    own_b, *sends_b = call(
        keep_z,
        tuple([shape(2, WIN, TWO, dtype=F32)] + [shape(2, WIN, TWO)] * 3),
        [left, dma((2,))],
        back_b,
        wins_0,
        wins_1,
        got_b,
        in_specs=[VMEM, HBM, HBM, VMEM],
    )
    from_z = [move(send, to_z[dz]) for dz, send in enumerate(sends_b, start=1)]
    total_a, *sends_a = call(
        then_z, tuple([shape(WIN, TWO, dtype=F32)] + [shape(WIN, TWO)] * 3), [], own_a, from_x
    )
    last_z = [move(send, to_z[dz]) for dz, send in enumerate(sends_a, start=1)]
    total_a, from_z = lax.optimization_barrier((total_a, from_z))
    total_b, send_b = call(
        then_x, (shape(WIN, TWO, dtype=F32), shape(WIN, TWO)), [], own_b, *from_z
    )
    for got in last_z:
        total_a = total_a + got.astype(F32)
    total_b = total_b + move(send_b, to_x).astype(F32)
    total = jnp.concatenate([total_a, total_b], axis=1)

    out = total[:, :VIRT] / gaps
    first_cell = grid_pos * share - first_row * VIRT
    return lax.dynamic_slice_in_dim(out.reshape(1, WIN * VIRT), first_cell, share, 1)


def solution(mesh):
    placed = (
        P("pair", None, None),
        P(None, "grid"),
        P("grid", "pair"),
        P("grid", "pair"),
        P("pair"),
        P(),
        P(),
    )
    return jax.shard_map(
        local, mesh=mesh, in_specs=placed, out_specs=P("pair", "grid"), check_vma=False
    )
```

time: 997 us -> 137 us (0.14)
  waiting for transfers between devices: 842 us -> 50.8 us
  local copies, waits for them, and re-layouts: 72.9 us -> 8.96 us
  matrix products: 46.2 us -> 0 us
  Pallas kernels: 0 us -> 45.6 us
  starting transfers between devices: 0.53 us -> 25.3 us
  between operations: 17.5 us -> 2.62 us
  other arithmetic: 16.4 us -> 3.55 us
    psum x2 -> x0, waiting for transfers between devices: 484 us -> none  [the longest x1 296 us: broadcast(): return lax.psum(block, axis)]
    reduce_scatter x1 -> x0, waiting for transfers between devices: 359 us -> none  [local(): lax.psum_scatter(partials, 'pair', scatter_dimension=0, tiled=True)]
    ppermute x0 -> x21, waiting for transfers between devices: none -> 50.8 us  [move(): return lax.ppermute(block, BOTH, pairs)]
    dot_general x3 -> x0, matrix products: 46.2 us -> none  [the longest x1 26.3 us: local(): jnp.einsum('kpq,vq->kpv', weighted, q_factors, preferred_element_type=jnp...]
    pallas_call x0 -> x14, Pallas kernels: none -> 45.6 us  [call(): pl.pallas_call(kernel, out_shape=out_shape, in_specs=in_specs or [VMEM] *...]
    reshape x3 -> x1, local copies, waits for them, and re-layouts: 35.2 us -> 0.97 us  [local(): out.reshape(1, WIN * VIRT)]
    ppermute x0 -> x21, starting transfers between devices: none -> 25.3 us  [move(): return lax.ppermute(block, BOTH, pairs)]
    add x1 -> x0, local copies, waits for them, and re-layouts: 12.2 us -> none  [local(): vir_energy[:, None] + vir_energy[None, :]]
  transfers between devices with their start and end apart: 4 -> 21, of which waited for: 3 -> 12; matrix products, arithmetic and copies ran while one was open for 3% -> 3% of each run, Pallas kernels for 0% -> 24%
where the time goes in v4:
time: 137 us
  waiting for transfers between devices  50.8 us (37%)
  Pallas kernels  45.6 us (33%)
  starting transfers between devices  25.3 us (18%)
  local copies, waits for them, and re-layouts  8.96 us (7%)
  other arithmetic  3.55 us (3%)
  between operations  2.62 us (2%)
    ppermute x21, waiting for transfers between devices, move(): return lax.ppermute(block, BOTH, pairs)  50.8 us
    pallas_call x14, Pallas kernels, call(): pl.pallas_call(kernel, out_shape=out_shape, in_specs=in_specs or [VMEM] *...  45.6 us
    ppermute x21, starting transfers between devices, move(): return lax.ppermute(block, BOTH, pairs)  25.3 us
    unnamed x16, local copies, waits for them, and re-layouts  4.64 us
  transfers between devices with their start and end apart: 21, of which 12 were waited for; matrix products, arithmetic and copies ran while one was open for 3% of the time, Pallas kernels for 24%

profile of v4, /device:TPU:0, one launch (start us, length us, event | category | flops | bytes accessed | tf_op | source)
XLA Modules:
  0.0 136.8 jit_solution(18181962739256459218)
XLA Ops:
  0.0 0.0 collective-permute-start.2
  0.0 2.9 %shard_map.73.own_ref = bf16[384,768]{1,0:T(8,128)(2,1)} custom-call(bf16[375,750]{1,0:T(8,128)(2,1)} %z_hbm.1, f32[3,6]{1,0:T(4,128)} %s_ref.1), custom_call_target="tpu_custom_call" | custom-call | tf_op jit(solution)/shard_map/pallas_call | solution.py:61
  2.9 0.1 collective-permute-done.2.pair_ref
  3.0 2.2 %shard_map.74 = (bf16[2,1536,384]{2,1,0:T(8,128)(2,1)}, bf16[1536,384]{1,0:T(8,128)(2,1)}) custom-call(bf16[1500,375]{1,0:T(8,128)(2,1)S(1)} %copy-done.4, bf16[1500,375]{1,0:T(8,128)(2,1)S(1)} %collective-permute-done.2.pair_ref), custom_call_target="tpu_custom_call" | custom-call | tf_op jit(solution)/shard_map/pallas_call | solution.py:61
  5.2 2.0 %collective-permute-start.5 = (bf16[2,1536,384]{2,1,0:T(8,128)(2,1)}, bf16[2,1536,384]{2,1,0:T(8,128)(2,1)S(1)}, u32[]{:S(2)}, u32[]{:S(2)}) collective-permute-start(bf16[2,1536,384]{2,1,0:T(8,128)(2,1)} %get-tuple-element.58.refs_0_), channel_id=1, source_target_pairs={{0,32},{2,34},{4,36},{6,38},{8,104},{10,106},{12,108},{14,110},{1,... | collective-permute-start | bytes 7077896 | tf_op jit(solution)/shard_map/ppermute | solution.py:33
  7.2 1.5 %collective-permute-start.1 = (bf16[384,768]{1,0:T(8,128)(2,1)}, bf16[384,768]{1,0:T(8,128)(2,1)}, u32[]{:S(2)}, u32[]{:S(2)}) collective-permute-start(bf16[384,768]{1,0:T(8,128)(2,1)} %shard_map.73.own_ref), channel_id=1, source_target_pairs={{1,16},{3,18},{5,20},{7,22},{9,24},{11,26},{13,28},{15,30},{16,1},... | collective-permute-start | bytes 1769480 | tf_op jit(solution)/shard_map/ppermute | solution.py:33
  8.7 3.5 %collective-permute-start = (bf16[384,768]{1,0:T(8,128)(2,1)}, bf16[384,768]{1,0:T(8,128)(2,1)}, u32[]{:S(2)}, u32[]{:S(2)}) collective-permute-start(bf16[384,768]{1,0:T(8,128)(2,1)} %shard_map.73.own_ref), channel_id=1, source_target_pairs={{0,1},{2,3},{4,5},{6,7},{8,9},{10,11},{12,13},{14,15},{1,17},{3,19... | collective-permute-start | bytes 1769480 | tf_op jit(solution)/shard_map/ppermute | solution.py:33
  12.2 0.1 stack.68.info
  12.3 0.0 copy-start
  12.3 2.3 %copy-done = bf16[1,1500,1500]{2,1,0:T(8,128)(2,1)S(1)} copy-done((bf16[1,1500,1500]{2,1,0:T(8,128)(2,1)S(1)}, bf16[1,1500,1500]{2,1,0:T(8,128)(2,1)}, u32[]{:S(2)}) %copy-start) | copy-done | bytes 4500024
  14.6 3.6 %shard_map.75 = (bf16[384,1536]{1,0:T(8,128)(2,1)S(1)}, bf16[2,8,96,384]{3,2,1,0:T(8,128)(2,1)S(1)}) custom-call(s32[16]{0:T(128)S(1)} %stack.68.info, bf16[1536,384]{1,0:T(8,128)(2,1)} %get-tuple-element.60.x_ref, bf16[1,1500,1500]{2,1,0:T(8,128)(2,1)S(1)} %copy-done), custom_call_target="tpu_custom_call" | custom-call | tf_op jit(solution)/shard_map/pallas_call | solution.py:61
  18.2 0.0 collective-permute-done.1.b_ref
  18.2 7.8 %collective-permute-done.a_ref = bf16[384,768]{1,0:T(8,128)(2,1)} collective-permute-done((bf16[384,768]{1,0:T(8,128)(2,1)}, bf16[384,768]{1,0:T(8,128)(2,1)}, u32[]{:S(2)}, u32[]{:S(2)}) %collective-permute-start) | collective-permute-done | bytes 589856 | tf_op jit(solution)/shard_map/ppermute | solution.py:33
  26.0 2.6 %shard_map.76.refs_5_ = bf16[2,384,768]{2,1,0:T(8,128)(2,1)} custom-call(s32[16]{0:T(128)S(1)} %stack.68.info, bf16[384,768]{1,0:T(8,128)(2,1)} %shard_map.73.own_ref, bf16[384,768]{1,0:T(8,128)(2,1)} %collective-permute-done.a_ref, bf16[384,768]{1,0:T(8,128)(2,1)} %collective-permute-done.1.b_ref), custom_call_target="tpu_custom_call" | custom-call | tf_op jit(solution)/shard_map/pallas_call | solution.py:61
  28.6 3.1 %collective-permute-start.4 = (bf16[2,384,768]{2,1,0:T(8,128)(2,1)}, bf16[2,384,768]{2,1,0:T(8,128)(2,1)}, u32[]{:S(2)}, u32[]{:S(2)}) collective-permute-start(bf16[2,384,768]{2,1,0:T(8,128)(2,1)} %shard_map.76.refs_5_), channel_id=1, source_target_pairs={{0,6},{2,0},{4,2},{6,4},{8,14},{10,8},{12,10},{14,12},{1,7},{3,1},... | collective-permute-start | bytes 3538952 | tf_op jit(solution)/shard_map/ppermute | solution.py:33
  31.7 0.0 collective-permute-start.3
  31.7 2.2 %collective-permute-start.7 = (bf16[1536,384]{1,0:T(8,128)(2,1)}, bf16[1536,384]{1,0:T(8,128)(2,1)}, u32[]{:S(2)}, u32[]{:S(2)}) collective-permute-start(bf16[1536,384]{1,0:T(8,128)(2,1)} %get-tuple-element.60.x_ref), channel_id=1, source_target_pairs={{0,17},{2,19},{4,21},{6,23},{8,25},{10,27},{12,29},{14,31},{1,16},... | collective-permute-start | bytes 3538952 | tf_op jit(solution)/shard_map/ppermute | solution.py:33
  33.9 2.4 %collective-permute-done.5.refs_1_ = bf16[2,1536,384]{2,1,0:T(8,128)(2,1)S(1)} collective-permute-done((bf16[2,1536,384]{2,1,0:T(8,128)(2,1)}, bf16[2,1536,384]{2,1,0:T(8,128)(2,1)S(1)}, u32[]{:S(2)}, u32[]{:S(2)}) %collective-permute-start.5) | collective-permute-done | bytes 2359328 | tf_op jit(solution)/shard_map/ppermute | solution.py:33
  36.4 1.1 slice_bitcast_fusion
  38.1 0.6 fusion.1
  40.5 0.1 pad_dynamic-slice_fusion
  40.6 1.2 fusion.4
  41.8 1.6 %add_subtract_fusion = f32[96,1500]{1,0:T(8,128)} fusion(f32[]{:T(128)} %fusion.4, f32[1500]{0:T(1024)S(1)} %copy-done.6, f32[96]{0:T(128)S(1)} %pad_dynamic-slice_fusion), kind=kLoop, calls=%fused_computation.3 | loop fusion | flops 288000 | bytes 582388 | tf_op jit(solution)/shard_map/sub | solution.py:357
  43.3 2.3 %copy-done.1 = bf16[1,1500,1500]{2,1,0:T(8,128)(2,1)S(1)} copy-done((bf16[1,1500,1500]{2,1,0:T(8,128)(2,1)S(1)}, bf16[1,1500,1500]{2,1,0:T(8,128)(2,1)}, u32[]{:S(2)}) %copy-start.1) | copy-done | bytes 4500024
  45.6 0.3 shard_map.77.amp_ref
  45.9 12.4 %collective-permute-done.4.second_ref.refs_6_ = bf16[2,384,768]{2,1,0:T(8,128)(2,1)} collective-permute-done((bf16[2,384,768]{2,1,0:T(8,128)(2,1)}, bf16[2,384,768]{2,1,0:T(8,128)(2,1)}, u32[]{:S(2)}, u32[]{:S(2)}) %collective-permute-start.4) | collective-permute-done | bytes 1179680 | tf_op jit(solution)/shard_map/ppermute | solution.py:33
  58.3 3.5 %collective-permute-done.3.first_ref.refs_7_ = bf16[2,384,768]{2,1,0:T(8,128)(2,1)} collective-permute-done((bf16[2,384,768]{2,1,0:T(8,128)(2,1)}, bf16[2,384,768]{2,1,0:T(8,128)(2,1)}, u32[]{:S(2)}, u32[]{:S(2)}) %collective-permute-start.3) | collective-permute-done | bytes 1179680 | tf_op jit(solution)/shard_map/ppermute | solution.py:33
  61.8 0.0 collective-permute-done.7.x_ref
  61.8 0.0 collective-permute-done.6.refs_3_
  61.9 0.5 collective-permute-start.9
  62.4 1.7 %shard_map.79 = bf16[2,384,768]{2,1,0:T(8,128)(2,1)S(1)} custom-call(s32[16]{0:T(128)S(1)} %stack.68.info, bf16[2,384,768]{2,1,0:T(8,128)(2,1)} %collective-permute-done.3.first_ref.refs_7_, bf16[2,384,768]{2,1,0:T(8,128)(2,1)} %collective-permute-done.4.second_ref.refs_6_), custom_call_target="tpu_custom_call" | custom-call | tf_op jit(solution)/shard_map/pallas_call | solution.py:61
  64.1 0.4 collective-permute-start.10
  64.5 3.6 %shard_map.78 = (bf16[384,1536]{1,0:T(8,128)(2,1)S(1)}, bf16[2,8,96,384]{3,2,1,0:T(8,128)(2,1)S(1)}) custom-call(s32[16]{0:T(128)S(1)} %stack.68.info, bf16[1536,384]{1,0:T(8,128)(2,1)} %collective-permute-done.7.x_ref, bf16[1,1500,1500]{2,1,0:T(8,128)(2,1)S(1)} %shard_map.77.amp_ref), custom_call_target="tpu_custom_call" | custom-call | tf_op jit(solution)/shard_map/pallas_call | solution.py:61
  68.1 0.0 collective-permute-done.8.refs_2_
  68.1 8.7 %shard_map.80 = (bf16[768,2304]{1,0:T(8,128)(2,1)S(1)}, bf16[1536,2304]{1,0:T(8,128)(2,1)S(1)}) custom-call(s32[16]{0:T(128)S(1)} %stack.68.info, bf16[384,1536]{1,0:T(8,128)(2,1)S(1)} %copy-done.3, bf16[384,1536]{1,0:T(8,128)(2,1)S(1)} %get-tuple-element.65.h1_ref, bf16[2,1536,384]{2,1,0:T(8,128)(2,1)} %get-tuple-element.58.refs_0_, ...), custom_call_target="tpu_custom_call" | custom-call | tf_op jit(solution)/shard_map/pallas_call | solution.py:61
  76.8 4.8 %collective-permute-done.10.refs_5_ = bf16[2,384,768]{2,1,0:T(8,128)(2,1)S(1)} collective-permute-done((bf16[2,384,768]{2,1,0:T(8,128)(2,1)S(1)}, bf16[2,384,768]{2,1,0:T(8,128)(2,1)S(1)}, u32[]{:S(2)}, u32[]{:S(2)}) %collective-permute-start.10) | collective-permute-done | bytes 1179680 | tf_op jit(solution)/shard_map/ppermute | solution.py:33
  81.6 10.4 %shard_map.81 = (bf16[768,768]{1,0:T(8,128)(2,1)S(1)}, bf16[1536,768]{1,0:T(8,128)(2,1)S(1)}, bf16[768,768]{1,0:T(8,128)(2,1)S(1)}, bf16[768,768]{1,0:T(8,128)(2,1)S(1)}) custom-call(s32[16]{0:T(128)S(1)} %stack.68.info, bf16[384,1536]{1,0:T(8,128)(2,1)S(1)} %copy-done.3, bf16[384,1536]{1,0:T(8,128)(2,1)S(1)} %get-tuple-element.65.h1_ref, ...), custom_call_target="tpu_custom_call" | custom-call | tf_op jit(solution)/shard_map/pallas_call | solution.py:61
  92.0 0.3 collective-permute-start.11
  92.3 6.9 %shard_map.84 = (bf16[768,768]{1,0:T(8,128)(2,1)S(1)}, bf16[768,768]{1,0:T(8,128)(2,1)S(1)}) custom-call(bf16[768,2304]{1,0:T(8,128)(2,1)S(1)} %get-tuple-element.70.refs_6_.w_ref, bf16[768,768]{1,0:T(8,128)(2,1)S(1)} %get-tuple-element.79.newest_ref, bf16[1536,2304]{1,0:T(8,128)(2,1)S(1)} %get-tuple-element.71.refs_7_.x_ref, ...), custom_call_target="tpu_custom_call" | custom-call | tf_op jit(solution)/shard_map/pallas_call | solution.py:61
  99.2 0.6 collective-permute-start.13
  99.8 1.2 shard_map.82
  101.0 2.3 %collective-permute-start.12 = (bf16[384,768]{1,0:T(8,128)(2,1)S(1)}, bf16[384,768]{1,0:T(8,128)(2,1)S(1)}, u32[]{:S(2)}, u32[]{:S(2)}) collective-permute-start(bf16[384,768]{1,0:T(8,128)(2,1)S(1)} %get-tuple-element.77), channel_id=1, source_target_pairs={{0,16},{2,18},{4,20},{6,22},{8,24},{10,26},{12,28},{14,30},{1,17},... | collective-permute-start | bytes 1769480 | tf_op jit(solution)/shard_map/ppermute | solution.py:33
  103.3 0.0 collective-permute-done.13.got_ref
  103.3 1.2 shard_map.85
  104.6 0.1 collective-permute-start.14
  104.6 1.2 collective-permute-start.15
  105.9 2.0 %collective-permute-start.16 = (bf16[2,96,768]{2,1,0:T(8,128)(2,1)S(1)}, bf16[2,96,768]{2,1,0:T(8,128)(2,1)S(1)}, u32[]{:S(2)}, u32[]{:S(2)}) collective-permute-start(bf16[2,96,768]{2,1,0:T(8,128)(2,1)S(1)} %get-tuple-element.85), channel_id=1, source_target_pairs={{0,96},{2,98},{4,100},{6,102},{8,104},{10,106},{12,108},{14,110},{... | collective-permute-start | bytes 884744 | tf_op jit(solution)/shard_map/ppermute | solution.py:33
  107.9 10.0 %collective-permute-done.12.got_ref = bf16[384,768]{1,0:T(8,128)(2,1)S(1)} collective-permute-done((bf16[384,768]{1,0:T(8,128)(2,1)S(1)}, bf16[384,768]{1,0:T(8,128)(2,1)S(1)}, u32[]{:S(2)}, u32[]{:S(2)}) %collective-permute-start.12) | collective-permute-done | bytes 589856 | tf_op jit(solution)/shard_map/ppermute | solution.py:33
  117.9 0.1 shard_map.83
  118.0 2.8 %collective-permute-done.14.got_1 = bf16[2,96,768]{2,1,0:T(8,128)(2,1)S(1)} collective-permute-done((bf16[2,96,768]{2,1,0:T(8,128)(2,1)S(1)}, bf16[2,96,768]{2,1,0:T(8,128)(2,1)S(1)}, u32[]{:S(2)}, u32[]{:S(2)}) %collective-permute-start.14) | collective-permute-done | bytes 294944 | tf_op jit(solution)/shard_map/ppermute | solution.py:33
  120.8 0.0 collective-permute-done.15.got_2
  120.8 0.6 collective-permute-done.16.got_3
  121.4 0.1 shard_map.86
  121.6 1.9 %collective-permute-start.20 = (bf16[96,768]{1,0:T(8,128)(2,1)S(1)}, bf16[96,768]{1,0:T(8,128)(2,1)S(1)}, u32[]{:S(2)}, u32[]{:S(2)}) collective-permute-start(bf16[96,768]{1,0:T(8,128)(2,1)S(1)} %get-tuple-element.95), channel_id=1, source_target_pairs={{0,16},{2,18},{4,20},{6,22},{8,24},{10,26},{12,28},{14,30},{1,17},... | collective-permute-start | bytes 442376 | tf_op jit(solution)/shard_map/ppermute | solution.py:33
  123.4 0.2 collective-permute-start.17
  123.7 3.6 %collective-permute-start.18 = (bf16[96,768]{1,0:T(8,128)(2,1)S(1)}, bf16[96,768]{1,0:T(8,128)(2,1)S(1)}, u32[]{:S(2)}, u32[]{:S(2)}) collective-permute-start(bf16[96,768]{1,0:T(8,128)(2,1)S(1)} %get-tuple-element.88), channel_id=1, source_target_pairs={{0,64},{2,66},{4,68},{6,70},{8,72},{10,74},{12,76},{14,78},{1,65},... | collective-permute-start | bytes 442376 | tf_op jit(solution)/shard_map/ppermute | solution.py:33
  127.2 0.0 collective-permute-start.19
  127.2 1.1 collective-permute-done.20
  128.3 2.4 %collective-permute-done.17 = bf16[96,768]{1,0:T(8,128)(2,1)S(1)} collective-permute-done((bf16[96,768]{1,0:T(8,128)(2,1)S(1)}, bf16[96,768]{1,0:T(8,128)(2,1)S(1)}, u32[]{:S(2)}, u32[]{:S(2)}) %collective-permute-start.17) | collective-permute-done | bytes 147488 | tf_op jit(solution)/shard_map/ppermute | solution.py:33
  130.8 2.8 %collective-permute-done.18 = bf16[96,768]{1,0:T(8,128)(2,1)S(1)} collective-permute-done((bf16[96,768]{1,0:T(8,128)(2,1)S(1)}, bf16[96,768]{1,0:T(8,128)(2,1)S(1)}, u32[]{:S(2)}, u32[]{:S(2)}) %collective-permute-start.18) | collective-permute-done | bytes 147488 | tf_op jit(solution)/shard_map/ppermute | solution.py:33
  133.6 0.1 convert_add_fusion.1
  133.7 0.1 fusion
  133.7 1.0 reshape.34
  134.7 2.0 %constant_dynamic-slice_fusion = f32[1,140625]{1,0:T(1,128)} fusion(f32[1,144000]{1,0:T(1,128)S(1)} %reshape.34, s32[]{:T(128)S(6)} %select_n.126), kind=kLoop, calls=%fused_computation.19 | loop fusion | bytes 1125004 | tf_op jit(solution)/shard_map/dynamic_slice | solution.py:461
  (19 shorter events, 0.1 us)
Async XLA Ops:
  0.0 3.0 %copy-start.4 = (bf16[1500,375]{1,0:T(8,128)(2,1)S(1)}, bf16[1500,375]{1,0:T(8,128)(2,1)}, u32[]{:S(2)}) copy-start(bf16[1500,375]{1,0:T(8,128)(2,1)} %own_ref.1) | copy-start | bytes 3375004
  0.0 3.0 %collective-permute-start.2 = (bf16[1500,375]{1,0:T(8,128)(2,1)}, bf16[1500,375]{1,0:T(8,128)(2,1)S(1)}, u32[]{:S(2)}, u32[]{:S(2)}) collective-permute-start(bf16[1500,375]{1,0:T(8,128)(2,1)} %own_ref.1), channel_id=1, source_target_pairs={{0,8},{2,10},{4,12},{6,14},{8,0},{10,2},{12,4},{14,6},{1,9},{3,11}... | collective-permute-start | bytes 3375008 | tf_op jit(solution)/shard_map/ppermute | solution.py:33
  5.2 31.2 %collective-permute-start.5 = (bf16[2,1536,384]{2,1,0:T(8,128)(2,1)}, bf16[2,1536,384]{2,1,0:T(8,128)(2,1)S(1)}, u32[]{:S(2)}, u32[]{:S(2)}) collective-permute-start(bf16[2,1536,384]{2,1,0:T(8,128)(2,1)} %get-tuple-element.58.refs_0_), channel_id=1, source_target_pairs={{0,32},{2,34},{4,36},{6,38},{8,104},{10,106},{12,108},{14,110},{1,... | collective-permute-start | bytes 7077896 | tf_op jit(solution)/shard_map/ppermute | solution.py:33
  7.2 11.0 %collective-permute-start.1 = (bf16[384,768]{1,0:T(8,128)(2,1)}, bf16[384,768]{1,0:T(8,128)(2,1)}, u32[]{:S(2)}, u32[]{:S(2)}) collective-permute-start(bf16[384,768]{1,0:T(8,128)(2,1)} %shard_map.73.own_ref), channel_id=1, source_target_pairs={{1,16},{3,18},{5,20},{7,22},{9,24},{11,26},{13,28},{15,30},{16,1},... | collective-permute-start | bytes 1769480 | tf_op jit(solution)/shard_map/ppermute | solution.py:33
  8.7 17.3 %collective-permute-start = (bf16[384,768]{1,0:T(8,128)(2,1)}, bf16[384,768]{1,0:T(8,128)(2,1)}, u32[]{:S(2)}, u32[]{:S(2)}) collective-permute-start(bf16[384,768]{1,0:T(8,128)(2,1)} %shard_map.73.own_ref), channel_id=1, source_target_pairs={{0,1},{2,3},{4,5},{6,7},{8,9},{10,11},{12,13},{14,15},{1,17},{3,19... | collective-permute-start | bytes 1769480 | tf_op jit(solution)/shard_map/ppermute | solution.py:33
  12.3 2.3 %copy-start = (bf16[1,1500,1500]{2,1,0:T(8,128)(2,1)S(1)}, bf16[1,1500,1500]{2,1,0:T(8,128)(2,1)}, u32[]{:S(2)}) copy-start(bf16[1,1500,1500]{2,1,0:T(8,128)(2,1)} %in_ref) | copy-start | bytes 13500004
  18.2 10.4 %copy-start.2 = (bf16[384,1536]{1,0:T(8,128)(2,1)}, bf16[384,1536]{1,0:T(8,128)(2,1)S(1)}, u32[]{:S(2)}) copy-start(bf16[384,1536]{1,0:T(8,128)(2,1)S(1)} %get-tuple-element.54.h0_ref) | copy-start | bytes 3538948
  28.6 11.9 %copy-start.6 = (f32[1500]{0:T(1024)S(1)}, f32[1500]{0:T(1024)}, u32[]{:S(2)}) copy-start(f32[1500]{0:T(1024)} %param.12) | copy-start | bytes 18004
  28.6 12.0 %copy-start.7 = (f32[150]{0:T(256)S(1)}, f32[150]{0:T(256)}, u32[]{:S(2)}) copy-start(f32[150]{0:T(256)} %param.13) | copy-start | bytes 1804
  28.6 29.7 %collective-permute-start.4 = (bf16[2,384,768]{2,1,0:T(8,128)(2,1)}, bf16[2,384,768]{2,1,0:T(8,128)(2,1)}, u32[]{:S(2)}, u32[]{:S(2)}) collective-permute-start(bf16[2,384,768]{2,1,0:T(8,128)(2,1)} %shard_map.76.refs_5_), channel_id=1, source_target_pairs={{0,6},{2,0},{4,2},{6,4},{8,14},{10,8},{12,10},{14,12},{1,7},{3,1},... | collective-permute-start | bytes 3538952 | tf_op jit(solution)/shard_map/ppermute | solution.py:33
  31.7 30.2 %collective-permute-start.3 = (bf16[2,384,768]{2,1,0:T(8,128)(2,1)}, bf16[2,384,768]{2,1,0:T(8,128)(2,1)}, u32[]{:S(2)}, u32[]{:S(2)}) collective-permute-start(bf16[2,384,768]{2,1,0:T(8,128)(2,1)} %shard_map.76.refs_5_), channel_id=1, source_target_pairs={{0,2},{2,4},{4,6},{6,0},{8,10},{10,12},{12,14},{14,8},{1,3},{3,5},... | collective-permute-start | bytes 3538952 | tf_op jit(solution)/shard_map/ppermute | solution.py:33
  31.7 30.2 %collective-permute-start.7 = (bf16[1536,384]{1,0:T(8,128)(2,1)}, bf16[1536,384]{1,0:T(8,128)(2,1)}, u32[]{:S(2)}, u32[]{:S(2)}) collective-permute-start(bf16[1536,384]{1,0:T(8,128)(2,1)} %get-tuple-element.60.x_ref), channel_id=1, source_target_pairs={{0,17},{2,19},{4,21},{6,23},{8,25},{10,27},{12,29},{14,31},{1,16},... | collective-permute-start | bytes 3538952 | tf_op jit(solution)/shard_map/ppermute | solution.py:33
  37.5 24.4 %collective-permute-start.6 = (bf16[1536,384]{1,0:T(8,128)(2,1)}, bf16[1536,384]{1,0:T(8,128)(2,1)}, u32[]{:S(2)}, u32[]{:S(2)}) collective-permute-start(bf16[1536,384]{1,0:T(8,128)(2,1)} %slice_bitcast_fusion), channel_id=1, source_target_pairs={{0,32},{2,34},{4,36},{6,38},{8,104},{10,106},{12,108},{14,110},{1,... | collective-permute-start | bytes 3538952 | tf_op jit(solution)/shard_map/ppermute | solution.py:33
  43.3 2.3 %copy-start.1 = (bf16[1,1500,1500]{2,1,0:T(8,128)(2,1)S(1)}, bf16[1,1500,1500]{2,1,0:T(8,128)(2,1)}, u32[]{:S(2)}) copy-start(bf16[1,1500,1500]{2,1,0:T(8,128)(2,1)} %in_ref) | copy-start | bytes 13500004
  61.8 6.3 %collective-permute-start.8 = (bf16[2,1536,384]{2,1,0:T(8,128)(2,1)S(1)}, bf16[2,1536,384]{2,1,0:T(8,128)(2,1)S(1)}, u32[]{:S(2)}, u32[]{:S(2)}) collective-permute-start(bf16[2,1536,384]{2,1,0:T(8,128)(2,1)S(1)} %collective-permute-done.5.refs_1_), channel_id=1, source_target_pairs={{0,8},{2,10},{4,12},{6,14},{8,0},{10,2},{12,4},{14,6},{1,9},{3,11}... | collective-permute-start | bytes 7077896 | tf_op jit(solution)/shard_map/ppermute | solution.py:33
  61.9 6.2 %collective-permute-start.9 = (bf16[1536,384]{1,0:T(8,128)(2,1)}, bf16[1536,384]{1,0:T(8,128)(2,1)S(1)}, u32[]{:S(2)}, u32[]{:S(2)}) collective-permute-start(bf16[1536,384]{1,0:T(8,128)(2,1)} %collective-permute-done.6.refs_3_), channel_id=1, source_target_pairs={{0,8},{2,10},{4,12},{6,14},{8,0},{10,2},{12,4},{14,6},{1,9},{3,11}... | collective-permute-start | bytes 3538952 | tf_op jit(solution)/shard_map/ppermute | solution.py:33
  64.1 4.0 %copy-start.3 = (bf16[384,1536]{1,0:T(8,128)(2,1)S(1)}, bf16[384,1536]{1,0:T(8,128)(2,1)}, u32[]{:S(2)}) copy-start(bf16[384,1536]{1,0:T(8,128)(2,1)} %copy-done.2) | copy-start | bytes 3538948
  64.1 17.5 %collective-permute-start.10 = (bf16[2,384,768]{2,1,0:T(8,128)(2,1)S(1)}, bf16[2,384,768]{2,1,0:T(8,128)(2,1)S(1)}, u32[]{:S(2)}, u32[]{:S(2)}) collective-permute-start(bf16[2,384,768]{2,1,0:T(8,128)(2,1)S(1)} %shard_map.79), channel_id=1, source_target_pairs={{0,2},{2,4},{4,6},{6,0},{8,14},{10,8},{12,10},{14,12},{1,3},{3,5},... | collective-permute-start | bytes 3538952 | tf_op jit(solution)/shard_map/ppermute | solution.py:33
  92.0 7.8 %collective-permute-start.11 = (bf16[768,768]{1,0:T(8,128)(2,1)S(1)}, bf16[768,768]{1,0:T(8,128)(2,1)S(1)}, u32[]{:S(2)}, u32[]{:S(2)}) collective-permute-start(bf16[768,768]{1,0:T(8,128)(2,1)S(1)} %get-tuple-element.75), channel_id=1, source_target_pairs={{0,8},{2,10},{4,12},{6,14},{8,0},{10,2},{12,4},{14,6},{1,9},{3,11}... | collective-permute-start | bytes 3538952 | tf_op jit(solution)/shard_map/ppermute | solution.py:33
  99.2 4.1 %collective-permute-start.13 = (bf16[768,768]{1,0:T(8,128)(2,1)S(1)}, bf16[768,768]{1,0:T(8,128)(2,1)S(1)}, u32[]{:S(2)}, u32[]{:S(2)}) collective-permute-start(bf16[768,768]{1,0:T(8,128)(2,1)S(1)} %get-tuple-element.82), channel_id=1, source_target_pairs={{0,8},{2,10},{4,12},{6,14},{8,0},{10,2},{12,4},{14,6},{1,9},{3,11}... | collective-permute-start | bytes 3538952 | tf_op jit(solution)/shard_map/ppermute | solution.py:33
  101.0 16.8 %collective-permute-start.12 = (bf16[384,768]{1,0:T(8,128)(2,1)S(1)}, bf16[384,768]{1,0:T(8,128)(2,1)S(1)}, u32[]{:S(2)}, u32[]{:S(2)}) collective-permute-start(bf16[384,768]{1,0:T(8,128)(2,1)S(1)} %get-tuple-element.77), channel_id=1, source_target_pairs={{0,16},{2,18},{4,20},{6,22},{8,24},{10,26},{12,28},{14,30},{1,17},... | collective-permute-start | bytes 1769480 | tf_op jit(solution)/shard_map/ppermute | solution.py:33
  104.6 16.3 %collective-permute-start.14 = (bf16[2,96,768]{2,1,0:T(8,128)(2,1)S(1)}, bf16[2,96,768]{2,1,0:T(8,128)(2,1)S(1)}, u32[]{:S(2)}, u32[]{:S(2)}) collective-permute-start(bf16[2,96,768]{2,1,0:T(8,128)(2,1)S(1)} %get-tuple-element.83), channel_id=1, source_target_pairs={{0,32},{2,34},{4,36},{6,38},{8,40},{10,42},{12,44},{14,46},{1,33},... | collective-permute-start | bytes 884744 | tf_op jit(solution)/shard_map/ppermute | solution.py:33
  104.6 16.2 %collective-permute-start.15 = (bf16[2,96,768]{2,1,0:T(8,128)(2,1)S(1)}, bf16[2,96,768]{2,1,0:T(8,128)(2,1)S(1)}, u32[]{:S(2)}, u32[]{:S(2)}) collective-permute-start(bf16[2,96,768]{2,1,0:T(8,128)(2,1)S(1)} %get-tuple-element.84), channel_id=1, source_target_pairs={{0,64},{2,66},{4,68},{6,70},{8,72},{10,74},{12,76},{14,78},{1,65},... | collective-permute-start | bytes 884744 | tf_op jit(solution)/shard_map/ppermute | solution.py:33
  105.9 15.6 %collective-permute-start.16 = (bf16[2,96,768]{2,1,0:T(8,128)(2,1)S(1)}, bf16[2,96,768]{2,1,0:T(8,128)(2,1)S(1)}, u32[]{:S(2)}, u32[]{:S(2)}) collective-permute-start(bf16[2,96,768]{2,1,0:T(8,128)(2,1)S(1)} %get-tuple-element.85), channel_id=1, source_target_pairs={{0,96},{2,98},{4,100},{6,102},{8,104},{10,106},{12,108},{14,110},{... | collective-permute-start | bytes 884744 | tf_op jit(solution)/shard_map/ppermute | solution.py:33
  121.6 12.1 %copy-start.5 = (f32[96,1500]{1,0:T(8,128)S(1)}, f32[96,1500]{1,0:T(8,128)}, u32[]{:S(2)}) copy-start(f32[96,1500]{1,0:T(8,128)} %add_subtract_fusion) | copy-start | bytes 1728004
  121.6 6.7 %collective-permute-start.20 = (bf16[96,768]{1,0:T(8,128)(2,1)S(1)}, bf16[96,768]{1,0:T(8,128)(2,1)S(1)}, u32[]{:S(2)}, u32[]{:S(2)}) collective-permute-start(bf16[96,768]{1,0:T(8,128)(2,1)S(1)} %get-tuple-element.95), channel_id=1, source_target_pairs={{0,16},{2,18},{4,20},{6,22},{8,24},{10,26},{12,28},{14,30},{1,17},... | collective-permute-start | bytes 442376 | tf_op jit(solution)/shard_map/ppermute | solution.py:33
  123.4 7.3 %collective-permute-start.17 = (bf16[96,768]{1,0:T(8,128)(2,1)S(1)}, bf16[96,768]{1,0:T(8,128)(2,1)S(1)}, u32[]{:S(2)}, u32[]{:S(2)}) collective-permute-start(bf16[96,768]{1,0:T(8,128)(2,1)S(1)} %get-tuple-element.87), channel_id=1, source_target_pairs={{0,32},{2,34},{4,36},{6,38},{8,40},{10,42},{12,44},{14,46},{1,33},... | collective-permute-start | bytes 442376 | tf_op jit(solution)/shard_map/ppermute | solution.py:33
  123.7 9.9 %collective-permute-start.18 = (bf16[96,768]{1,0:T(8,128)(2,1)S(1)}, bf16[96,768]{1,0:T(8,128)(2,1)S(1)}, u32[]{:S(2)}, u32[]{:S(2)}) collective-permute-start(bf16[96,768]{1,0:T(8,128)(2,1)S(1)} %get-tuple-element.88), channel_id=1, source_target_pairs={{0,64},{2,66},{4,68},{6,70},{8,72},{10,74},{12,76},{14,78},{1,65},... | collective-permute-start | bytes 442376 | tf_op jit(solution)/shard_map/ppermute | solution.py:33
  127.2 6.3 %collective-permute-start.19 = (bf16[96,768]{1,0:T(8,128)(2,1)S(1)}, bf16[96,768]{1,0:T(8,128)(2,1)S(1)}, u32[]{:S(2)}, u32[]{:S(2)}) collective-permute-start(bf16[96,768]{1,0:T(8,128)(2,1)S(1)} %get-tuple-element.89), channel_id=1, source_target_pairs={{0,96},{2,98},{4,100},{6,102},{8,104},{10,106},{12,108},{14,110},{... | collective-permute-start | bytes 442376 | tf_op jit(solution)/shard_map/ppermute | solution.py:33

commit v5 on v4

--- a/solution.py
+++ b/solution.py
@@ -37,14 +37,6 @@
     return move(block, lambda z, x, c, y: (z, x, 1 - c, y))
 
 
-def pair_orbitals(packed, occ_count):
-    row_ids = jnp.arange(1, occ_count, dtype=jnp.int32)
-    starts = row_ids * (2 * occ_count - row_ids - 1) // 2
-    first_occ = jnp.sum((starts[None, :] <= packed[:, None]).astype(jnp.int32), axis=1)
-    second = packed - first_occ * (2 * occ_count - first_occ - 1) // 2 + first_occ + 1
-    return (first_occ, second)
-
-
 def dot(a, b, contract_a, contract_b):
     return lax.dot_general(
         a, b, (((contract_a,), (contract_b,)), ((), ())), preferred_element_type=F32
@@ -56,7 +48,7 @@
 HBM = pl.BlockSpec(memory_space=pl.ANY)
 
 
-def call(kernel, out_shape, scratch, *args, in_specs=None, out_specs=None, mib=20):
+def call(kernel, out_shape, scratch, *args, in_specs=None, out_specs=None, mib=20, weight=0):
     many = isinstance(out_shape, (tuple, list))
     return pl.pallas_call(
         kernel,
@@ -64,6 +56,7 @@
         in_specs=in_specs or [VMEM] * len(args),
         out_specs=out_specs or (tuple([VMEM] * len(out_shape)) if many else VMEM),
         scratch_shapes=scratch,
+        cost_estimate=pl.CostEstimate(flops=1 + weight * 10**9, bytes_accessed=1 + weight * 10**6, transcendentals=0),
         compiler_params=pltpu.CompilerParams(vmem_limit_bytes=mib * 2**20),
     )(*args)
 
@@ -275,6 +268,44 @@
     send_ref[...] = total[1].astype(BF16)
 
 
+def add_parts(own_ref, *refs):
+    o_ref = refs[-1]
+    total = own_ref[...]
+    for ref in refs[:-1]:
+        total = total + ref[...].astype(F32)
+    o_ref[...] = total
+
+
+def finish(numbers, occ_ref, vir_ref, a_ref, b_ref, b1_ref, o_ref, out):
+    packed, first_row, first_cell = numbers[0], numbers[1], numbers[2]
+    count = occ_ref.shape[1]
+    orbital = lax.broadcasted_iota(jnp.int32, (1, count), 1)
+    starts = orbital * (2 * count - orbital - 1) // 2
+    first_occ = jnp.sum(((starts <= packed) & (orbital > 0)).astype(jnp.int32))
+    second_occ = packed - first_occ * (2 * count - first_occ - 1) // 2 + first_occ + 1
+    occ = jnp.where(orbital == first_occ, occ_ref[...], 0.0)
+    occ = occ + jnp.where(orbital == second_occ, occ_ref[...], 0.0)
+    row = lax.broadcasted_iota(jnp.int32, (WIN, VIRT), 0) + first_row
+    column = lax.broadcasted_iota(jnp.int32, (WIN, VIRT), 1)
+    vir = vir_ref[...]
+    vir_rows = jnp.sum(jnp.where(row == column, vir, 0.0), axis=1, keepdims=True)
+    vir_rows = jnp.where(row[:, :1] < VIRT, vir_rows, 1.0)
+    gaps = vir_rows + vir - jnp.sum(occ, axis=1, keepdims=True)
+    out[:, :TWO] = a_ref[...] / gaps[:, :TWO]
+    total_b = b_ref[...] + b1_ref[...].astype(F32)
+    out[:, TWO:] = total_b[:, : VIRT - TWO] / gaps[:, TWO:]
+    rows = o_ref.shape[0]
+    for shift in range(0, VIRT, BLK):
+
+        @pl.when(first_cell == shift)
+        def _():
+            if shift == 0:
+                o_ref[...] = out[:rows, :]
+            else:
+                o_ref[:, : VIRT - shift] = out[:rows, shift:]
+                o_ref[:, VIRT - shift :] = out[1 : rows + 1, :shift]
+
+
 def shape(*dims, dtype=BF16):
     return jax.ShapeDtypeStruct(dims, dtype)
 
@@ -315,7 +346,7 @@
         pad_factors, (shape(2, VPAD, BPAD), shape(VPAD, BPAD)), [], factors, theirs
     )
 
-    def halves_of(block, amp):
+    def halves_of(block, amp, weight=0):
         return call(
             half,
             (shape(BPAD, VPAD), shape(2, 8, WIN, BPAD)),
@@ -324,14 +355,13 @@
             block,
             amp,
             in_specs=[SMEM, VMEM, VMEM],
+            weight=weight,
         )
 
     half_0, wins_0 = halves_of(x_own, amplitudes)
     onward = lambda z, x, c, y: (z + 1 - 2 * c, x, c, y)
     near = move(x_pair, onward)
-    recv_a, recv_b, half_0, x_again, pair_index = lax.optimization_barrier(
-        (recv_a, recv_b, half_0, x_own, pair_index)
-    )
+    recv_a, recv_b, half_0, x_again = lax.optimization_barrier((recv_a, recv_b, half_0, x_own))
     x_other = move(x_again, lambda z, x, c, y: (z, 3 - x, c, y))
     z_here = call(
         choose_rows,
@@ -342,26 +372,16 @@
         recv_a,
         recv_b,
         in_specs=[SMEM] + [VMEM] * 3,
+        weight=20,
     )
     z_before = move(z_here, lambda z, x, c, y: (z, x, c, y + 1))
     z_after = move(z_here, lambda z, x, c, y: (z, x, c, y - 1))
-    occ_count = occ_energy.shape[0]
-    first_occ, second_occ = pair_orbitals(pair_index, occ_count)
-    orbital_ids = jnp.arange(occ_count, dtype=jnp.int32)
-    one_first = (orbital_ids[None, :] == first_occ[:, None]).astype(F32)
-    one_second = (orbital_ids[None, :] == second_occ[:, None]).astype(F32)
-    occ_sum = jnp.sum((one_first + one_second) * occ_energy[None, :], axis=1)
-    share = VIRT * VIRT // 16
-    first_row = grid_pos * BLK // 4
-    vir_rows = lax.dynamic_slice_in_dim(jnp.pad(vir_energy, (0, VPAD - VIRT)), first_row, WIN, 0)
-    gaps = vir_rows[:, None] + vir_energy[None, :] - occ_sum
     far = move(near[0], onward)
-    amp_later, near = lax.optimization_barrier((amplitudes, near))
+    amp_later, far_source = lax.optimization_barrier((amplitudes, near))
     amp_again = call(copy_whole, shape(1, VIRT, VIRT), [], amp_later)
-    z_before, z_after, near, far, x_other, gaps, amp_again = lax.optimization_barrier(
-        (z_before, z_after, near, far, x_other, gaps, amp_again)
-    )
-    x_parts = [x_pair, near, across(near), far, across(far)]
+    x_other, amp_again = lax.optimization_barrier((x_other, amp_again))
+    half_1, wins_1 = halves_of(x_other, amp_again, 10)
+    z_before, z_after, half_1 = lax.optimization_barrier((z_before, z_after, half_1))
     z_onward = call(
         choose_onward,
         shape(2, BPAD, TWO),
@@ -372,7 +392,8 @@
         in_specs=[SMEM] + [VMEM] * 2,
     )
     z_far = move(z_onward, lambda z, x, c, y: (z, x, c, y + 1 - 2 * c))
-    half_1, wins_1 = halves_of(x_other, amp_again)
+    far, _ = lax.optimization_barrier((far, z_onward))
+    x_parts = [x_pair, near, across(near), far, across(far)]
     dma = pltpu.SemaphoreType.DMA
     early, x_early = call(
         weigh_early,
@@ -451,14 +472,24 @@
     total_b, send_b = call(
         then_x, (shape(WIN, TWO, dtype=F32), shape(WIN, TWO)), [], own_b, *from_z
     )
-    for got in last_z:
-        total_a = total_a + got.astype(F32)
-    total_b = total_b + move(send_b, to_x).astype(F32)
-    total = jnp.concatenate([total_a, total_b], axis=1)
-
-    out = total[:, :VIRT] / gaps
+    total_a = call(add_parts, shape(WIN, TWO, dtype=F32), [], total_a, *last_z, weight=10)
+    share = VIRT * VIRT // 16
+    first_row = grid_pos * BLK // 4
     first_cell = grid_pos * share - first_row * VIRT
-    return lax.dynamic_slice_in_dim(out.reshape(1, WIN * VIRT), first_cell, share, 1)
+    numbers = jnp.stack([pair_index[0], first_row, first_cell]).astype(jnp.int32)
+    out = call(
+        finish,
+        shape(94, VIRT, dtype=F32),
+        [pltpu.VMEM((WIN, VIRT), F32)],
+        numbers,
+        occ_energy.reshape(1, -1),
+        vir_energy.reshape(1, -1),
+        total_a,
+        total_b,
+        move(send_b, to_x),
+        in_specs=[SMEM] + [VMEM] * 5,
+    )
+    return out.reshape(1, 94 * VIRT)[:, :share]
 
 
 def solution(mesh):

time: 137 us -> 129 us (0.942)
  starting transfers between devices: 25.3 us -> 30.7 us
  other arithmetic: 3.55 us -> 0.08 us
  waiting for transfers between devices: 50.8 us -> 47.7 us
  local copies, waits for them, and re-layouts: 8.96 us -> 5.87 us
  Pallas kernels: 45.6 us -> 43.5 us
  between operations: 2.62 us -> 0.87 us
    ppermute x21, starting transfers between devices: 25.3 us -> 30.7 us  [move(): return lax.ppermute(block, BOTH, pairs)]
    ppermute x21, waiting for transfers between devices: 50.8 us -> 47.7 us  [move(): return lax.ppermute(block, BOTH, pairs)]
    dynamic_slice x2 -> x0, local copies, waits for them, and re-layouts: 2.13 us -> none  [the longest x1 2.04 us: local(): lax.dynamic_slice_in_dim(out.reshape(1, WIN * VIRT), first_cell, share, 1)]
    pallas_call x14 -> x16, Pallas kernels: 45.6 us -> 43.5 us  [call(): pl.pallas_call(kernel, out_shape=out_shape, in_specs=in_specs or [VMEM] *...]
    reduce_sum x2 -> x0, other arithmetic: 1.8 us -> none  [the longest x1 1.17 us: local(): occ_sum = jnp.sum((one_first + one_second) * occ_energy[None, :], axis=1)]
    sub x1 -> x0, other arithmetic: 1.56 us -> none  [local(): gaps = vir_rows[:, None] + vir_energy[None, :] - occ_sum]
    unnamed x16 -> x22, local copies, waits for them, and re-layouts: 4.64 us -> 3.86 us
  transfers between devices with their start and end apart: 21 -> 21, of which waited for: 12 -> 13; matrix products, arithmetic and copies ran while one was open for 3% -> 0% of each run, Pallas kernels for 24% -> 26%
where the time goes in v5:
time: 129 us
  waiting for transfers between devices  47.7 us (37%)
  Pallas kernels  43.5 us (34%)
  starting transfers between devices  30.7 us (24%)
  local copies, waits for them, and re-layouts  5.87 us (5%)
    ppermute x21, waiting for transfers between devices, move(): return lax.ppermute(block, BOTH, pairs)  47.7 us
    pallas_call x16, Pallas kernels, call(): pl.pallas_call(kernel, out_shape=out_shape, in_specs=in_specs or [VMEM] *...  43.5 us
    ppermute x21, starting transfers between devices, move(): return lax.ppermute(block, BOTH, pairs)  30.7 us
    unnamed x22, local copies, waits for them, and re-layouts  3.86 us
  transfers between devices with their start and end apart: 21, of which 13 were waited for; matrix products, arithmetic and copies ran while one was open for 0% of the time, Pallas kernels for 26%

profile of v5, /device:TPU:0, one launch (start us, length us, event | category | flops | bytes accessed | tf_op | source)
XLA Modules:
  0.0 128.7 jit_solution(17631683012347212035)
XLA Ops:
  0.0 0.0 collective-permute-start.2
  0.0 2.9 %shard_map.73.own_ref = bf16[384,768]{1,0:T(8,128)(2,1)} custom-call(bf16[375,750]{1,0:T(8,128)(2,1)} %z_hbm.1, f32[3,6]{1,0:T(4,128)} %s_ref.1), custom_call_target="tpu_custom_call" | custom-call | flops 1 | bytes 1 | tf_op jit(solution)/shard_map/pallas_call | solution.py:53
  2.9 1.7 %collective-permute-start = (bf16[384,768]{1,0:T(8,128)(2,1)}, bf16[384,768]{1,0:T(8,128)(2,1)}, u32[]{:S(2)}, u32[]{:S(2)}) collective-permute-start(bf16[384,768]{1,0:T(8,128)(2,1)} %shard_map.73.own_ref), channel_id=1, source_target_pairs={{0,1},{2,3},{4,5},{6,7},{8,9},{10,11},{12,13},{14,15},{1,17},{3,19... | collective-permute-start | bytes 1769480 | tf_op jit(solution)/shard_map/ppermute | solution.py:33
  4.6 1.5 %collective-permute-start.1 = (bf16[384,768]{1,0:T(8,128)(2,1)}, bf16[384,768]{1,0:T(8,128)(2,1)}, u32[]{:S(2)}, u32[]{:S(2)}) collective-permute-start(bf16[384,768]{1,0:T(8,128)(2,1)} %shard_map.73.own_ref), channel_id=1, source_target_pairs={{1,16},{3,18},{5,20},{7,22},{9,24},{11,26},{13,28},{15,30},{16,1},... | collective-permute-start | bytes 1769480 | tf_op jit(solution)/shard_map/ppermute | solution.py:33
  6.1 0.0 collective-permute-done.2.pair_ref
  6.1 1.9 %shard_map.74 = (bf16[2,1536,384]{2,1,0:T(8,128)(2,1)}, bf16[1536,384]{1,0:T(8,128)(2,1)S(1)}) custom-call(bf16[1500,375]{1,0:T(8,128)(2,1)S(1)} %copy-done.1, bf16[1500,375]{1,0:T(8,128)(2,1)S(1)} %collective-permute-done.2.pair_ref), custom_call_target="tpu_custom_call" | custom-call | flops 1 | bytes 1 | tf_op jit(solution)/shard_map/pallas_call | solution.py:53
  8.0 1.9 %collective-permute-start.6 = (bf16[2,1536,384]{2,1,0:T(8,128)(2,1)}, bf16[2,1536,384]{2,1,0:T(8,128)(2,1)S(1)}, u32[]{:S(2)}, u32[]{:S(2)}) collective-permute-start(bf16[2,1536,384]{2,1,0:T(8,128)(2,1)} %get-tuple-element.56.refs_0_), channel_id=1, source_target_pairs={{0,32},{2,34},{4,36},{6,38},{8,104},{10,106},{12,108},{14,110},{1,... | collective-permute-start | bytes 7077896 | tf_op jit(solution)/shard_map/ppermute | solution.py:33
  9.9 0.1 stack.80.info
  10.0 0.0 copy-start
  10.0 2.3 %copy-done = bf16[1,1500,1500]{2,1,0:T(8,128)(2,1)S(1)} copy-done((bf16[1,1500,1500]{2,1,0:T(8,128)(2,1)S(1)}, bf16[1,1500,1500]{2,1,0:T(8,128)(2,1)}, u32[]{:S(2)}) %copy-start) | copy-done | bytes 4500024
  12.3 2.8 %shard_map.75 = (bf16[384,1536]{1,0:T(8,128)(2,1)S(1)}, bf16[2,8,96,384]{3,2,1,0:T(8,128)(2,1)S(1)}) custom-call(s32[16]{0:T(128)S(1)} %stack.80.info, bf16[1536,384]{1,0:T(8,128)(2,1)S(1)} %get-tuple-element.55.x_ref, bf16[1,1500,1500]{2,1,0:T(8,128)(2,1)S(1)} %copy-done), custom_call_target="tpu_custom_call" | custom-call | flops 1 | bytes 1 | tf_op jit(solution)/shard_map/pallas_call | solution.py:53
  15.1 5.3 %collective-permute-done.a_ref = bf16[384,768]{1,0:T(8,128)(2,1)} collective-permute-done((bf16[384,768]{1,0:T(8,128)(2,1)}, bf16[384,768]{1,0:T(8,128)(2,1)}, u32[]{:S(2)}, u32[]{:S(2)}) %collective-permute-start) | collective-permute-done | bytes 589856 | tf_op jit(solution)/shard_map/ppermute | solution.py:33
  20.4 0.0 collective-permute-done.1.b_ref
  20.4 2.9 %collective-permute-start.5 = (bf16[1536,384]{1,0:T(8,128)(2,1)S(1)}, bf16[1536,384]{1,0:T(8,128)(2,1)S(1)}, u32[]{:S(2)}, u32[]{:S(2)}) collective-permute-start(bf16[1536,384]{1,0:T(8,128)(2,1)S(1)} %get-tuple-element.55.x_ref), channel_id=1, source_target_pairs={{0,17},{2,19},{4,21},{6,23},{8,25},{10,27},{12,29},{14,31},{1,16},... | collective-permute-start | bytes 3538952 | tf_op jit(solution)/shard_map/ppermute | solution.py:33
  23.4 1.3 %shard_map.76.refs_5_ = bf16[2,384,768]{2,1,0:T(8,128)(2,1)S(1)} custom-call(s32[16]{0:T(128)S(1)} %stack.80.info, bf16[384,768]{1,0:T(8,128)(2,1)S(1)} %copy-done.2, bf16[384,768]{1,0:T(8,128)(2,1)} %collective-permute-done.a_ref, bf16[384,768]{1,0:T(8,128)(2,1)} %collective-permute-done.1.b_ref), custom_call_target="tpu_custom_call" | custom-call | flops 20000000000 | bytes 20000000 | tf_op jit(solution)/shard_map/pallas_call | solution.py:53
  24.7 1.6 %collective-permute-start.3 = (bf16[2,384,768]{2,1,0:T(8,128)(2,1)S(1)}, bf16[2,384,768]{2,1,0:T(8,128)(2,1)S(1)}, u32[]{:S(2)}, u32[]{:S(2)}) collective-permute-start(bf16[2,384,768]{2,1,0:T(8,128)(2,1)S(1)} %shard_map.76.refs_5_), channel_id=1, source_target_pairs={{0,2},{2,4},{4,6},{6,0},{8,10},{10,12},{12,14},{14,8},{1,3},{3,5},... | collective-permute-start | bytes 3538952 | tf_op jit(solution)/shard_map/ppermute | solution.py:33
  26.4 1.7 %collective-permute-start.4 = (bf16[2,384,768]{2,1,0:T(8,128)(2,1)S(1)}, bf16[2,384,768]{2,1,0:T(8,128)(2,1)S(1)}, u32[]{:S(2)}, u32[]{:S(2)}) collective-permute-start(bf16[2,384,768]{2,1,0:T(8,128)(2,1)S(1)} %shard_map.76.refs_5_), channel_id=1, source_target_pairs={{0,6},{2,0},{4,2},{6,4},{8,14},{10,8},{12,10},{14,12},{1,7},{3,1},... | collective-permute-start | bytes 3538952 | tf_op jit(solution)/shard_map/ppermute | solution.py:33
  28.0 11.0 %collective-permute-done.6.refs_1_ = bf16[2,1536,384]{2,1,0:T(8,128)(2,1)S(1)} collective-permute-done((bf16[2,1536,384]{2,1,0:T(8,128)(2,1)}, bf16[2,1536,384]{2,1,0:T(8,128)(2,1)S(1)}, u32[]{:S(2)}, u32[]{:S(2)}) %collective-permute-start.6) | collective-permute-done | bytes 2359328 | tf_op jit(solution)/shard_map/ppermute | solution.py:33
  39.0 0.1 slice_bitcast_fusion
  39.2 0.1 collective-permute-start.8
  39.2 2.2 %collective-permute-start.7 = (bf16[2,1536,384]{2,1,0:T(8,128)(2,1)S(1)}, bf16[2,1536,384]{2,1,0:T(8,128)(2,1)S(1)}, u32[]{:S(2)}, u32[]{:S(2)}) collective-permute-start(bf16[2,1536,384]{2,1,0:T(8,128)(2,1)S(1)} %collective-permute-done.6.refs_1_), channel_id=1, source_target_pairs={{0,8},{2,10},{4,12},{6,14},{8,0},{10,2},{12,4},{14,6},{1,9},{3,11}... | collective-permute-start | bytes 7077896 | tf_op jit(solution)/shard_map/ppermute | solution.py:33
  41.4 0.3 shard_map.77.amp_ref
  41.7 7.4 %collective-permute-done.5.x_ref = bf16[1536,384]{1,0:T(8,128)(2,1)S(1)} collective-permute-done((bf16[1536,384]{1,0:T(8,128)(2,1)S(1)}, bf16[1536,384]{1,0:T(8,128)(2,1)S(1)}, u32[]{:S(2)}, u32[]{:S(2)}) %collective-permute-start.5) | collective-permute-done | bytes 1179680 | tf_op jit(solution)/shard_map/ppermute | solution.py:33
  49.2 2.8 %shard_map.78 = (bf16[384,1536]{1,0:T(8,128)(2,1)S(1)}, bf16[2,8,96,384]{3,2,1,0:T(8,128)(2,1)S(1)}) custom-call(s32[16]{0:T(128)S(1)} %stack.80.info, bf16[1536,384]{1,0:T(8,128)(2,1)S(1)} %collective-permute-done.5.x_ref, bf16[1,1500,1500]{2,1,0:T(8,128)(2,1)S(1)} %shard_map.77.amp_ref), custom_call_target="tpu_custom_call" | custom-call | flops 10000000000 | bytes 10000001 | tf_op jit(solution)/shard_map/pallas_call | solution.py:53
  52.0 1.2 collective-permute-done.3.first_ref.refs_7_
  53.2 0.0 collective-permute-done.4.second_ref.refs_6_
  53.2 0.6 shard_map.79
  53.9 2.8 %collective-permute-done.8.refs_3_ = bf16[1536,384]{1,0:T(8,128)(2,1)S(1)} collective-permute-done((bf16[1536,384]{1,0:T(8,128)(2,1)S(1)}, bf16[1536,384]{1,0:T(8,128)(2,1)S(1)}, u32[]{:S(2)}, u32[]{:S(2)}) %collective-permute-start.8) | collective-permute-done | bytes 1179680 | tf_op jit(solution)/shard_map/ppermute | solution.py:33
  56.6 0.0 collective-permute-start.9
  56.6 1.6 %collective-permute-start.10 = (bf16[2,384,768]{2,1,0:T(8,128)(2,1)S(1)}, bf16[2,384,768]{2,1,0:T(8,128)(2,1)S(1)}, u32[]{:S(2)}, u32[]{:S(2)}) collective-permute-start(bf16[2,384,768]{2,1,0:T(8,128)(2,1)S(1)} %shard_map.79), channel_id=1, source_target_pairs={{0,2},{2,4},{4,6},{6,0},{8,14},{10,8},{12,10},{14,12},{1,3},{3,5},... | collective-permute-start | bytes 3538952 | tf_op jit(solution)/shard_map/ppermute | solution.py:33
  58.2 1.3 collective-permute-done.9.refs_4_
  59.5 8.2 %shard_map.80 = (bf16[768,2304]{1,0:T(8,128)(2,1)S(1)}, bf16[1536,2304]{1,0:T(8,128)(2,1)S(1)}) custom-call(s32[16]{0:T(128)S(1)} %stack.80.info, bf16[384,1536]{1,0:T(8,128)(2,1)S(1)} %get-tuple-element.51.h0_ref, bf16[384,1536]{1,0:T(8,128)(2,1)S(1)} %get-tuple-element.61.h1_ref, bf16[2,1536,384]{2,1,0:T(8,128)(2,1)} %get-tuple-element.56.refs_0_, ...), custom_call_target="tpu_custom_call" | custom-call | flops 1 | bytes 1 | tf_op jit(solution)/shard_map/pallas_call | solution.py:53
  67.7 6.3 %collective-permute-done.10.refs_5_ = bf16[2,384,768]{2,1,0:T(8,128)(2,1)S(1)} collective-permute-done((bf16[2,384,768]{2,1,0:T(8,128)(2,1)S(1)}, bf16[2,384,768]{2,1,0:T(8,128)(2,1)S(1)}, u32[]{:S(2)}, u32[]{:S(2)}) %collective-permute-start.10) | collective-permute-done | bytes 1179680 | tf_op jit(solution)/shard_map/ppermute | solution.py:33
  74.1 9.5 %shard_map.81 = (bf16[768,768]{1,0:T(8,128)(2,1)S(1)}, bf16[1536,768]{1,0:T(8,128)(2,1)S(1)}, bf16[768,768]{1,0:T(8,128)(2,1)S(1)}, bf16[768,768]{1,0:T(8,128)(2,1)S(1)}) custom-call(s32[16]{0:T(128)S(1)} %stack.80.info, bf16[384,1536]{1,0:T(8,128)(2,1)S(1)} %get-tuple-element.51.h0_ref, bf16[384,1536]{1,0:T(8,128)(2,1)S(1)} %get-tuple-element.61.h1_ref, ...), custom_call_target="tpu_custom_call" | custom-call | flops 1 | bytes 1 | tf_op jit(solution)/shard_map/pallas_call | solution.py:53
  83.6 0.3 collective-permute-start.11
  83.9 6.9 %shard_map.84 = (bf16[768,768]{1,0:T(8,128)(2,1)S(1)}, bf16[768,768]{1,0:T(8,128)(2,1)S(1)}) custom-call(bf16[768,2304]{1,0:T(8,128)(2,1)S(1)} %get-tuple-element.65.refs_6_.w_ref, bf16[768,768]{1,0:T(8,128)(2,1)S(1)} %get-tuple-element.74.newest_ref, bf16[1536,2304]{1,0:T(8,128)(2,1)S(1)} %get-tuple-element.66.refs_7_.x_ref, ...), custom_call_target="tpu_custom_call" | custom-call | flops 1 | bytes 1 | tf_op jit(solution)/shard_map/pallas_call | solution.py:53
  90.8 0.6 collective-permute-start.13
  91.4 0.0 collective-permute-done.11.got_ref
  91.4 1.2 shard_map.82
  92.6 4.7 %collective-permute-start.12 = (bf16[384,768]{1,0:T(8,128)(2,1)S(1)}, bf16[384,768]{1,0:T(8,128)(2,1)S(1)}, u32[]{:S(2)}, u32[]{:S(2)}) collective-permute-start(bf16[384,768]{1,0:T(8,128)(2,1)S(1)} %get-tuple-element.72), channel_id=1, source_target_pairs={{0,16},{2,18},{4,20},{6,22},{8,24},{10,26},{12,28},{14,30},{1,17},... | collective-permute-start | bytes 1769480 | tf_op jit(solution)/shard_map/ppermute | solution.py:33
  97.3 2.0 %shard_map.85 = (f32[2,96,768]{2,1,0:T(8,128)S(1)}, bf16[2,96,768]{2,1,0:T(8,128)(2,1)S(1)}, bf16[2,96,768]{2,1,0:T(8,128)(2,1)}, bf16[2,96,768]{2,1,0:T(8,128)(2,1)}) custom-call(bf16[768,768]{1,0:T(8,128)(2,1)S(1)} %get-tuple-element.76.back_ref, bf16[2,8,96,384]{3,2,1,0:T(8,128)(2,1)S(1)} %get-tuple-element.67.refs_8_.w0_ref, ...), custom_call_target="tpu_custom_call" | custom-call | flops 1 | bytes 1 | tf_op jit(solution)/shard_map/pallas_call | solution.py:53
  99.4 0.8 copy-done.3
  100.2 0.0 collective-permute-start.14
  100.2 2.5 %collective-permute-start.15 = (bf16[2,96,768]{2,1,0:T(8,128)(2,1)}, bf16[2,96,768]{2,1,0:T(8,128)(2,1)}, u32[]{:S(2)}, u32[]{:S(2)}) collective-permute-start(bf16[2,96,768]{2,1,0:T(8,128)(2,1)} %get-tuple-element.79), channel_id=1, source_target_pairs={{0,64},{2,66},{4,68},{6,70},{8,72},{10,74},{12,76},{14,78},{1,65},... | collective-permute-start | bytes 884744 | tf_op jit(solution)/shard_map/ppermute | solution.py:33
  102.7 2.0 %collective-permute-start.16 = (bf16[2,96,768]{2,1,0:T(8,128)(2,1)}, bf16[2,96,768]{2,1,0:T(8,128)(2,1)}, u32[]{:S(2)}, u32[]{:S(2)}) collective-permute-start(bf16[2,96,768]{2,1,0:T(8,128)(2,1)} %get-tuple-element.80), channel_id=1, source_target_pairs={{0,96},{2,98},{4,100},{6,102},{8,104},{10,106},{12,108},{14,110},{... | collective-permute-start | bytes 884744 | tf_op jit(solution)/shard_map/ppermute | solution.py:33
  104.7 6.1 %collective-permute-done.12.got_ref = bf16[384,768]{1,0:T(8,128)(2,1)S(1)} collective-permute-done((bf16[384,768]{1,0:T(8,128)(2,1)S(1)}, bf16[384,768]{1,0:T(8,128)(2,1)S(1)}, u32[]{:S(2)}, u32[]{:S(2)}) %collective-permute-start.12) | collective-permute-done | bytes 589856 | tf_op jit(solution)/shard_map/ppermute | solution.py:33
  110.8 0.8 shard_map.83
  111.6 0.7 copy-done.6
  112.3 0.0 collective-permute-start.17
  112.3 2.5 %collective-permute-start.18 = (bf16[96,768]{1,0:T(8,128)(2,1)}, bf16[96,768]{1,0:T(8,128)(2,1)S(1)}, u32[]{:S(2)}, u32[]{:S(2)}) collective-permute-start(bf16[96,768]{1,0:T(8,128)(2,1)} %get-tuple-element.83), channel_id=1, source_target_pairs={{0,64},{2,66},{4,68},{6,70},{8,72},{10,74},{12,76},{14,78},{1,65},... | collective-permute-start | bytes 442376 | tf_op jit(solution)/shard_map/ppermute | solution.py:33
  114.8 1.9 %collective-permute-done.14.got_1 = bf16[2,96,768]{2,1,0:T(8,128)(2,1)S(1)} collective-permute-done((bf16[2,96,768]{2,1,0:T(8,128)(2,1)S(1)}, bf16[2,96,768]{2,1,0:T(8,128)(2,1)S(1)}, u32[]{:S(2)}, u32[]{:S(2)}) %collective-permute-start.14) | collective-permute-done | bytes 294944 | tf_op jit(solution)/shard_map/ppermute | solution.py:33
  116.7 0.1 collective-permute-start.19
  117.5 0.1 pad_add_fusion.numbers
  117.6 0.4 collective-permute-done.16.got_3
  118.1 1.2 shard_map.87
  119.2 0.0 copy-start.5
  119.2 2.9 %collective-permute-start.20 = (bf16[96,768]{1,0:T(8,128)(2,1)S(1)}, bf16[96,768]{1,0:T(8,128)(2,1)S(1)}, u32[]{:S(2)}, u32[]{:S(2)}) collective-permute-start(bf16[96,768]{1,0:T(8,128)(2,1)S(1)} %get-tuple-element.90), channel_id=1, source_target_pairs={{0,16},{2,18},{4,20},{6,22},{8,24},{10,26},{12,28},{14,30},{1,17},... | collective-permute-start | bytes 442376 | tf_op jit(solution)/shard_map/ppermute | solution.py:33
  122.1 0.6 collective-permute-done.17.refs_0_
  122.7 0.9 collective-permute-done.19.refs_2_
  123.6 0.1 shard_map.86.a_ref
  123.7 2.3 %collective-permute-done.20.b1_ref = bf16[96,768]{1,0:T(8,128)(2,1)S(1)} collective-permute-done((bf16[96,768]{1,0:T(8,128)(2,1)S(1)}, bf16[96,768]{1,0:T(8,128)(2,1)S(1)}, u32[]{:S(2)}, u32[]{:S(2)}) %collective-permute-start.20) | collective-permute-done | bytes 147488 | tf_op jit(solution)/shard_map/ppermute | solution.py:33
  126.0 0.9 shard_map.88
  126.9 0.9 reshape.11
  127.8 0.8 slice.9
  (23 shorter events, 0.0 us)
Async XLA Ops:
  0.0 6.1 %copy-start.1 = (bf16[1500,375]{1,0:T(8,128)(2,1)S(1)}, bf16[1500,375]{1,0:T(8,128)(2,1)}, u32[]{:S(2)}) copy-start(bf16[1500,375]{1,0:T(8,128)(2,1)} %own_ref.1) | copy-start | bytes 3375004
  0.0 6.1 %collective-permute-start.2 = (bf16[1500,375]{1,0:T(8,128)(2,1)}, bf16[1500,375]{1,0:T(8,128)(2,1)S(1)}, u32[]{:S(2)}, u32[]{:S(2)}) collective-permute-start(bf16[1500,375]{1,0:T(8,128)(2,1)} %own_ref.1), channel_id=1, source_target_pairs={{0,8},{2,10},{4,12},{6,14},{8,0},{10,2},{12,4},{14,6},{1,9},{3,11}... | collective-permute-start | bytes 3375008 | tf_op jit(solution)/shard_map/ppermute | solution.py:33
  2.9 17.5 %collective-permute-start = (bf16[384,768]{1,0:T(8,128)(2,1)}, bf16[384,768]{1,0:T(8,128)(2,1)}, u32[]{:S(2)}, u32[]{:S(2)}) collective-permute-start(bf16[384,768]{1,0:T(8,128)(2,1)} %shard_map.73.own_ref), channel_id=1, source_target_pairs={{0,1},{2,3},{4,5},{6,7},{8,9},{10,11},{12,13},{14,15},{1,17},{3,19... | collective-permute-start | bytes 1769480 | tf_op jit(solution)/shard_map/ppermute | solution.py:33
  4.6 15.8 %collective-permute-start.1 = (bf16[384,768]{1,0:T(8,128)(2,1)}, bf16[384,768]{1,0:T(8,128)(2,1)}, u32[]{:S(2)}, u32[]{:S(2)}) collective-permute-start(bf16[384,768]{1,0:T(8,128)(2,1)} %shard_map.73.own_ref), channel_id=1, source_target_pairs={{1,16},{3,18},{5,20},{7,22},{9,24},{11,26},{13,28},{15,30},{16,1},... | collective-permute-start | bytes 1769480 | tf_op jit(solution)/shard_map/ppermute | solution.py:33
  8.0 31.1 %collective-permute-start.6 = (bf16[2,1536,384]{2,1,0:T(8,128)(2,1)}, bf16[2,1536,384]{2,1,0:T(8,128)(2,1)S(1)}, u32[]{:S(2)}, u32[]{:S(2)}) collective-permute-start(bf16[2,1536,384]{2,1,0:T(8,128)(2,1)} %get-tuple-element.56.refs_0_), channel_id=1, source_target_pairs={{0,32},{2,34},{4,36},{6,38},{8,104},{10,106},{12,108},{14,110},{1,... | collective-permute-start | bytes 7077896 | tf_op jit(solution)/shard_map/ppermute | solution.py:33
  10.0 2.3 %copy-start = (bf16[1,1500,1500]{2,1,0:T(8,128)(2,1)S(1)}, bf16[1,1500,1500]{2,1,0:T(8,128)(2,1)}, u32[]{:S(2)}) copy-start(bf16[1,1500,1500]{2,1,0:T(8,128)(2,1)} %in_ref) | copy-start | bytes 13500004
  12.3 11.1 %copy-start.2 = (bf16[384,768]{1,0:T(8,128)(2,1)S(1)}, bf16[384,768]{1,0:T(8,128)(2,1)}, u32[]{:S(2)}) copy-start(bf16[384,768]{1,0:T(8,128)(2,1)} %shard_map.73.own_ref) | copy-start | bytes 1769476
  20.4 21.0 %slice-start = ((s8[4620288]{0:T(1024)(128)(4,1)}), s8[4194304]{0:T(1024)(128)(4,1)S(1)}, s32[]{:S(2)}) async-start(s8[4620288]{0:T(1024)(128)(4,1)} %bitcast.20), calls=%async_computation | async-start | bytes 8388608
  20.4 21.0 %slice-start.1 = ((s8[4620288]{0:T(1024)(128)(4,1)}), s8[425984]{0:T(1024)(128)(4,1)S(1)}, s32[]{:S(2)}) async-start(s8[4620288]{0:T(1024)(128)(4,1)} %bitcast.20), calls=%async_computation.1 | async-start | bytes 851968
  20.4 28.7 %collective-permute-start.5 = (bf16[1536,384]{1,0:T(8,128)(2,1)S(1)}, bf16[1536,384]{1,0:T(8,128)(2,1)S(1)}, u32[]{:S(2)}, u32[]{:S(2)}) collective-permute-start(bf16[1536,384]{1,0:T(8,128)(2,1)S(1)} %get-tuple-element.55.x_ref), channel_id=1, source_target_pairs={{0,17},{2,19},{4,21},{6,23},{8,25},{10,27},{12,29},{14,31},{1,16},... | collective-permute-start | bytes 3538952 | tf_op jit(solution)/shard_map/ppermute | solution.py:33
  24.7 28.5 %collective-permute-start.3 = (bf16[2,384,768]{2,1,0:T(8,128)(2,1)S(1)}, bf16[2,384,768]{2,1,0:T(8,128)(2,1)S(1)}, u32[]{:S(2)}, u32[]{:S(2)}) collective-permute-start(bf16[2,384,768]{2,1,0:T(8,128)(2,1)S(1)} %shard_map.76.refs_5_), channel_id=1, source_target_pairs={{0,2},{2,4},{4,6},{6,0},{8,10},{10,12},{12,14},{14,8},{1,3},{3,5},... | collective-permute-start | bytes 3538952 | tf_op jit(solution)/shard_map/ppermute | solution.py:33
  26.4 26.9 %collective-permute-start.4 = (bf16[2,384,768]{2,1,0:T(8,128)(2,1)S(1)}, bf16[2,384,768]{2,1,0:T(8,128)(2,1)S(1)}, u32[]{:S(2)}, u32[]{:S(2)}) collective-permute-start(bf16[2,384,768]{2,1,0:T(8,128)(2,1)S(1)} %shard_map.76.refs_5_), channel_id=1, source_target_pairs={{0,6},{2,0},{4,2},{6,4},{8,14},{10,8},{12,10},{14,12},{1,7},{3,1},... | collective-permute-start | bytes 3538952 | tf_op jit(solution)/shard_map/ppermute | solution.py:33
  39.2 17.5 %collective-permute-start.8 = (bf16[1536,384]{1,0:T(8,128)(2,1)S(1)}, bf16[1536,384]{1,0:T(8,128)(2,1)S(1)}, u32[]{:S(2)}, u32[]{:S(2)}) collective-permute-start(bf16[1536,384]{1,0:T(8,128)(2,1)S(1)} %slice_bitcast_fusion), channel_id=1, source_target_pairs={{0,32},{2,34},{4,36},{6,38},{8,104},{10,106},{12,108},{14,110},{1,... | collective-permute-start | bytes 3538952 | tf_op jit(solution)/shard_map/ppermute | solution.py:33
  39.2 20.3 %collective-permute-start.7 = (bf16[2,1536,384]{2,1,0:T(8,128)(2,1)S(1)}, bf16[2,1536,384]{2,1,0:T(8,128)(2,1)S(1)}, u32[]{:S(2)}, u32[]{:S(2)}) collective-permute-start(bf16[2,1536,384]{2,1,0:T(8,128)(2,1)S(1)} %collective-permute-done.6.refs_1_), channel_id=1, source_target_pairs={{0,8},{2,10},{4,12},{6,14},{8,0},{10,2},{12,4},{14,6},{1,9},{3,11}... | collective-permute-start | bytes 7077896 | tf_op jit(solution)/shard_map/ppermute | solution.py:33
  56.6 2.8 %collective-permute-start.9 = (bf16[1536,384]{1,0:T(8,128)(2,1)S(1)}, bf16[1536,384]{1,0:T(8,128)(2,1)S(1)}, u32[]{:S(2)}, u32[]{:S(2)}) collective-permute-start(bf16[1536,384]{1,0:T(8,128)(2,1)S(1)} %collective-permute-done.8.refs_3_), channel_id=1, source_target_pairs={{0,8},{2,10},{4,12},{6,14},{8,0},{10,2},{12,4},{14,6},{1,9},{3,11}... | collective-permute-start | bytes 3538952 | tf_op jit(solution)/shard_map/ppermute | solution.py:33
  56.6 17.4 %collective-permute-start.10 = (bf16[2,384,768]{2,1,0:T(8,128)(2,1)S(1)}, bf16[2,384,768]{2,1,0:T(8,128)(2,1)S(1)}, u32[]{:S(2)}, u32[]{:S(2)}) collective-permute-start(bf16[2,384,768]{2,1,0:T(8,128)(2,1)S(1)} %shard_map.79), channel_id=1, source_target_pairs={{0,2},{2,4},{4,6},{6,0},{8,14},{10,8},{12,10},{14,12},{1,3},{3,5},... | collective-permute-start | bytes 3538952 | tf_op jit(solution)/shard_map/ppermute | solution.py:33
  83.6 7.8 %collective-permute-start.11 = (bf16[768,768]{1,0:T(8,128)(2,1)S(1)}, bf16[768,768]{1,0:T(8,128)(2,1)S(1)}, u32[]{:S(2)}, u32[]{:S(2)}) collective-permute-start(bf16[768,768]{1,0:T(8,128)(2,1)S(1)} %get-tuple-element.70), channel_id=1, source_target_pairs={{0,8},{2,10},{4,12},{6,14},{8,0},{10,2},{12,4},{14,6},{1,9},{3,11}... | collective-permute-start | bytes 3538952 | tf_op jit(solution)/shard_map/ppermute | solution.py:33
  90.8 6.5 %collective-permute-start.13 = (bf16[768,768]{1,0:T(8,128)(2,1)S(1)}, bf16[768,768]{1,0:T(8,128)(2,1)S(1)}, u32[]{:S(2)}, u32[]{:S(2)}) collective-permute-start(bf16[768,768]{1,0:T(8,128)(2,1)S(1)} %get-tuple-element.77), channel_id=1, source_target_pairs={{0,8},{2,10},{4,12},{6,14},{8,0},{10,2},{12,4},{14,6},{1,9},{3,11}... | collective-permute-start | bytes 3538952 | tf_op jit(solution)/shard_map/ppermute | solution.py:33
  92.6 18.2 %collective-permute-start.12 = (bf16[384,768]{1,0:T(8,128)(2,1)S(1)}, bf16[384,768]{1,0:T(8,128)(2,1)S(1)}, u32[]{:S(2)}, u32[]{:S(2)}) collective-permute-start(bf16[384,768]{1,0:T(8,128)(2,1)S(1)} %get-tuple-element.72), channel_id=1, source_target_pairs={{0,16},{2,18},{4,20},{6,22},{8,24},{10,26},{12,28},{14,30},{1,17},... | collective-permute-start | bytes 1769480 | tf_op jit(solution)/shard_map/ppermute | solution.py:33
  99.4 0.8 copy-start.3
  100.2 17.3 %copy-start.8 = (f32[1500]{0:T(1024)S(1)}, f32[1500]{0:T(1024)}, u32[]{:S(2)}) copy-start(f32[1500]{0:T(1024)} %param.12) | copy-start | bytes 18004
  100.2 17.9 %copy-start.4 = (f32[2,96,768]{2,1,0:T(8,128)S(1)}, f32[2,96,768]{2,1,0:T(8,128)}, u32[]{:S(2)}) copy-start(f32[2,96,768]{2,1,0:T(8,128)} %copy-done.3) | copy-start | bytes 1769476
  100.2 16.5 %collective-permute-start.14 = (bf16[2,96,768]{2,1,0:T(8,128)(2,1)S(1)}, bf16[2,96,768]{2,1,0:T(8,128)(2,1)S(1)}, u32[]{:S(2)}, u32[]{:S(2)}) collective-permute-start(bf16[2,96,768]{2,1,0:T(8,128)(2,1)S(1)} %get-tuple-element.78), channel_id=1, source_target_pairs={{0,32},{2,34},{4,36},{6,38},{8,40},{10,42},{12,44},{14,46},{1,33},... | collective-permute-start | bytes 884744 | tf_op jit(solution)/shard_map/ppermute | solution.py:33
  100.2 17.4 %collective-permute-start.15 = (bf16[2,96,768]{2,1,0:T(8,128)(2,1)}, bf16[2,96,768]{2,1,0:T(8,128)(2,1)}, u32[]{:S(2)}, u32[]{:S(2)}) collective-permute-start(bf16[2,96,768]{2,1,0:T(8,128)(2,1)} %get-tuple-element.79), channel_id=1, source_target_pairs={{0,64},{2,66},{4,68},{6,70},{8,72},{10,74},{12,76},{14,78},{1,65},... | collective-permute-start | bytes 884744 | tf_op jit(solution)/shard_map/ppermute | solution.py:33
  102.7 15.4 %collective-permute-start.16 = (bf16[2,96,768]{2,1,0:T(8,128)(2,1)}, bf16[2,96,768]{2,1,0:T(8,128)(2,1)}, u32[]{:S(2)}, u32[]{:S(2)}) collective-permute-start(bf16[2,96,768]{2,1,0:T(8,128)(2,1)} %get-tuple-element.80), channel_id=1, source_target_pairs={{0,96},{2,98},{4,100},{6,102},{8,104},{10,106},{12,108},{14,110},{... | collective-permute-start | bytes 884744 | tf_op jit(solution)/shard_map/ppermute | solution.py:33
  111.6 0.7 copy-start.6
  112.3 11.2 %copy-start.7 = (f32[96,768]{1,0:T(8,128)S(1)}, f32[96,768]{1,0:T(8,128)}, u32[]{:S(2)}) copy-start(f32[96,768]{1,0:T(8,128)} %copy-done.6) | copy-start | bytes 884740
  112.3 10.4 %collective-permute-start.17 = (bf16[96,768]{1,0:T(8,128)(2,1)}, bf16[96,768]{1,0:T(8,128)(2,1)S(1)}, u32[]{:S(2)}, u32[]{:S(2)}) collective-permute-start(bf16[96,768]{1,0:T(8,128)(2,1)} %get-tuple-element.82), channel_id=1, source_target_pairs={{0,32},{2,34},{4,36},{6,38},{8,40},{10,42},{12,44},{14,46},{1,33},... | collective-permute-start | bytes 442376 | tf_op jit(solution)/shard_map/ppermute | solution.py:33
  112.3 10.4 %collective-permute-start.18 = (bf16[96,768]{1,0:T(8,128)(2,1)}, bf16[96,768]{1,0:T(8,128)(2,1)S(1)}, u32[]{:S(2)}, u32[]{:S(2)}) collective-permute-start(bf16[96,768]{1,0:T(8,128)(2,1)} %get-tuple-element.83), channel_id=1, source_target_pairs={{0,64},{2,66},{4,68},{6,70},{8,72},{10,74},{12,76},{14,78},{1,65},... | collective-permute-start | bytes 442376 | tf_op jit(solution)/shard_map/ppermute | solution.py:33
  116.7 6.8 %collective-permute-start.19 = (bf16[96,768]{1,0:T(8,128)(2,1)S(1)}, bf16[96,768]{1,0:T(8,128)(2,1)S(1)}, u32[]{:S(2)}, u32[]{:S(2)}) collective-permute-start(bf16[96,768]{1,0:T(8,128)(2,1)S(1)} %get-tuple-element.84), channel_id=1, source_target_pairs={{0,96},{2,98},{4,100},{6,102},{8,104},{10,106},{12,108},{14,110},{... | collective-permute-start | bytes 442376 | tf_op jit(solution)/shard_map/ppermute | solution.py:33
  119.2 6.7 %copy-start.5 = (f32[150]{0:T(256)S(1)}, f32[150]{0:T(256)}, u32[]{:S(2)}) copy-start(f32[150]{0:T(256)} %param.13) | copy-start | bytes 1804
  119.2 6.7 %collective-permute-start.20 = (bf16[96,768]{1,0:T(8,128)(2,1)S(1)}, bf16[96,768]{1,0:T(8,128)(2,1)S(1)}, u32[]{:S(2)}, u32[]{:S(2)}) collective-permute-start(bf16[96,768]{1,0:T(8,128)(2,1)S(1)} %get-tuple-element.90), channel_id=1, source_target_pairs={{0,16},{2,18},{4,20},{6,22},{8,24},{10,26},{12,28},{14,30},{1,17},... | collective-permute-start | bytes 442376 | tf_op jit(solution)/shard_map/ppermute | solution.py:33
